TPU v7x, 32 devices: a whole 2x2x4 slice. The times are simulated.
32 devices in a mesh: section: 2 (over core), dp: 16 (over z, y, x).
Axes of the slice: x: 2, y: 2, z: 4, core: 2. Of those that a mesh axis runs over, the one named last changes fastest.
Arguments:
- inputs: bfloat16 [6, 8192, 384], P(None, 'dp'), may hold values from -120 to 120
- series_id: int32 [6, 8192], P(None, 'dp'), may hold values from 0 to 63, as said below
- item_offset: int32 [6, 8192], P(None, 'dp'), may hold values from 0 to 383, as said below
- variate_offset: int32 [6, 8192], P(None, 'dp'), may hold values from 0 to 511, as said below
- cotangent: bfloat16 [6, 8192, 384], P(None, 'dp'), may hold values from -30 to 30
- attention_gain: bfloat16 [2, 384], P('section'), may hold values from 0.099609375 to 1.8984375
- query_weight: bfloat16 [2, 384, 384], P('section'), may hold values from -0.3125 to 0.3125
- key_weight: bfloat16 [2, 384, 384], P('section'), may hold values from -0.3125 to 0.3125
- value_weight: bfloat16 [2, 384, 384], P('section'), may hold values from -0.3125 to 0.3125
- out_weight: bfloat16 [2, 384, 384], P('section'), may hold values from -1.25 to 1.25
- variate_bias: bfloat16 [2, 6, 2], P('section'), may hold values from -3 to 3
- feed_gain: bfloat16 [2, 384], P('section'), may hold values from 0.099609375 to 1.8984375
- gate_weight: bfloat16 [2, 384, 1024], P('section'), may hold values from -0.3125 to 0.3125
- up_weight: bfloat16 [2, 384, 1024], P('section'), may hold values from -0.3125 to 0.3125
- down_weight: bfloat16 [2, 1024, 384], P('section'), may hold values from -0.1875 to 0.1875
Outputs:
- section_output: bfloat16 [2, 6, 8192, 384], P('section', None, 'dp')
- input_grads: float32 [2, 6, 8192, 384], P('section', None, 'dp')
- grad_attention_gain: float32 [2, 384], P('section')
- grad_query: float32 [2, 384, 384], P('section')
- grad_key: float32 [2, 384, 384], P('section')
- grad_value: float32 [2, 384, 384], P('section')
- grad_out: float32 [2, 384, 384], P('section')
- grad_bias: float32 [2, 6, 2], P('section')
- grad_feed_gain: float32 [2, 384], P('section')
- grad_gate: float32 [2, 384, 1024], P('section')
- grad_up: float32 [2, 384, 1024], P('section')
- grad_down: float32 [2, 1024, 384], P('section')
Inputs may be any that keep to these rules, and one draw needn't show every extreme that they name: `series_id`: tokens of one variate share a series; in each micro-batch one series, drawn from the seed, holds the first variate of every block of 512 tokens. Each aligned block of 512 tokens holds two items, runs of tokens; the first begins at 0, so a token's item_offset is at most its position in the block. Variates are runs within an item; a token's variate_offset lies between its item_offset and its position in the block.
All inputs are finite; a program needn't handle non-finite values.
Results may differ from a plain program's by a relative error of at most 0.015.
Values may be sent and summed in bfloat16 or wider, within the bound.
No kernel may reach another device: no remote copies, remote signals or barrier semaphores. Data moves between devices by JAX's collectives and lax.ppermute only.
A program may use at most 320 MiB of HBM per device.

v0:
```python
import jax
import jax.numpy as jnp
import numpy as np
from jax import lax
from jax.experimental import pallas as pl
from jax.experimental.pallas import tpu as pltpu
from jax.sharding import PartitionSpec as P

HD = 64
BLOCK = 512
SER_DEV = 4
LANES = 128
CHUNK = 256
TILE = 256

norm_epsilon = 1e-05
scale_epsilon = 1e-05
masked_score = -1e30

f32 = jnp.float32
bf16 = jnp.bfloat16

AS_IS = (((1,), (0,)), ((), ()))
RIGHT_T = (((1,), (1,)), ((), ()))
LEFT_T = (((0,), (0,)), ((), ()))


def dot(left, right, dims=AS_IS):
    return lax.dot_general(left, right, dims, preferred_element_type=f32)


def column(row):
    return jnp.broadcast_to(row.astype(f32), (LANES, row.shape[1])).T


def lane_index(rows):
    return lax.broadcasted_iota(jnp.int32, (rows, LANES), 1)


def regroup(x):
    group = lane_index(x.shape[0]) // (HD // 2)
    return jnp.where(
        group == 1,
        pltpu.roll(x, LANES - HD // 2, 1),
        jnp.where(group == 2, pltpu.roll(x, HD // 2, 1), x),
    )


def turn(x, cosine, sine):
    return x * cosine + pltpu.roll(x, LANES // 2, 1) * sine


def turn_back(x, cosine, sine):
    return x * cosine - pltpu.roll(x, LANES // 2, 1) * sine


def inverse_rms(x):
    return lax.rsqrt(jnp.mean(x * x, axis=1, keepdims=True) + norm_epsilon)


def series_hits(sid_col, piece):
    return sid_col == (lane_index(sid_col.shape[0]) + piece * LANES).astype(f32)


def rows_of(hits, per_series):
    return jnp.sum(jnp.where(hits, per_series, 0.0), axis=1, keepdims=True)


def series_of(hits, per_row):
    return jnp.sum(jnp.where(hits, per_row, 0.0), axis=0, keepdims=True)


def stats_body(sec_ref, x_ref, sid_ref, out_ref):
    m = pl.num_programs(0) * sec_ref[0] + pl.program_id(0)
    x = x_ref[0].astype(f32)
    width = x.shape[1]
    sid_col = column(sid_ref[pl.ds(m, 1), :])
    pieces = out_ref.shape[-1] // LANES
    totals = jnp.sum(x, axis=1, keepdims=True)
    centre = jnp.zeros_like(totals)
    out_ref[0] = jnp.zeros(out_ref.shape[1:], f32)
    for piece in range(pieces):
        hits = series_hits(sid_col, piece)
        count = series_of(hits, 1.0)
        total = series_of(hits, totals)
        centre = centre + rows_of(hits, total / (jnp.maximum(count, 1.0) * width))
        out_ref[0, 0:1, piece * LANES : (piece + 1) * LANES] = count
        out_ref[0, 1:2, piece * LANES : (piece + 1) * LANES] = total
    centred = x - centre
    squares = jnp.sum(centred * centred, axis=1, keepdims=True)
    for piece in range(pieces):
        hits = series_hits(sid_col, piece)
        out_ref[0, 2:3, piece * LANES : (piece + 1) * LANES] = series_of(hits, squares)


def merge_stats(here, there, width):
    count_a, total_a, spread_a = here[:, 0], here[:, 1], here[:, 2]
    count_b, total_b, spread_b = there[:, 0], there[:, 1], there[:, 2]
    count = count_a + count_b
    gap = total_a / (jnp.maximum(count_a, 1.0) * width) - total_b / (
        jnp.maximum(count_b, 1.0) * width
    )
    weight = count_a * count_b * width / jnp.maximum(count, 1.0)
    spread = spread_a + spread_b + gap * gap * weight
    rest = jnp.zeros_like(here[:, 3:])
    return jnp.concatenate(
        [jnp.stack([count, total_a + total_b, spread], axis=1), rest], axis=1
    )


def centre_and_scale(stats, width):
    entries = jnp.maximum(stats[0:1], 1.0) * width
    centre = stats[1:2] / entries
    scaling = jnp.sqrt(stats[2:3] / entries + scale_epsilon)
    return entries, centre, scaling


class Weights:
    def __init__(self, section, own_refs, other_refs, big_ref, down_ref, sems):
        self.first_step = pl.program_id(0) == 0
        self.big_ref, self.down_ref = big_ref, down_ref
        self.own_refs, self.sems = own_refs, sems

        @pl.when(self.first_step)
        def _():
            for layer_of, refs in ((section, own_refs), (1 - section, other_refs)):
                for k, ref in enumerate(refs):
                    pltpu.make_async_copy(ref, self.target(layer_of, k), sems.at[layer_of, k]).start()

    def target(self, layer, k):
        if k == 6:
            return self.down_ref.at[layer]
        at = sum(ref.shape[1] for ref in self.own_refs[:k])
        return self.big_ref.at[layer, :, pl.ds(at, self.own_refs[k].shape[1])]

    def wait_here(self, layer, numbers):
        for k in numbers:
            pltpu.make_async_copy(
                self.own_refs[k], self.target(layer, k), self.sems.at[layer, k]
            ).wait()

    def wait_attention(self, layer):
        width = self.big_ref.shape[1]

        @pl.when(self.first_step)
        def _():
            self.wait_here(layer, (0, 1, 2, 3))
            for at in range(0, 2 * width, LANES):
                tile = self.big_ref[layer, :, at : at + LANES].astype(f32)
                self.big_ref[layer, :, at : at + LANES] = regroup(tile).astype(bf16)

    def wait_feed(self, layer):
        @pl.when(self.first_step)
        def _():
            self.wait_here(layer, (4, 5, 6))


def sigmoid(x):
    return 0.5 * jnp.tanh(0.5 * x) + 0.5


def in_head(half, lanes, grouped):
    if grouped:
        return (lanes % HD) // (HD // 2) == half
    return lanes // HD == half


def row_index(rows):
    return lax.broadcasted_iota(jnp.int32, (LANES, rows), 0)


class Block:
    def __init__(self, cosine, sine, item_col, var_col, var_row, same_ref):
        rows = cosine.shape[0]
        self.cosine, self.sine, self.same_ref = cosine, sine, same_ref
        row = var_row.astype(f32)
        for at in range(0, rows, LANES):
            same_ref[:, at : at + LANES] = jnp.where(var_col == row[:, at : at + LANES], 1.0, 0.0)
        lane = lane_index(rows)
        second = jnp.where(item_col > 0.0, 1.0, 0.0)
        self.item_q = jnp.where(
            lane == 0, second, jnp.where(lane == 1, 1.0 - second, 0.0)
        ).astype(bf16)
        self.item_k = jnp.where(
            lane == 0,
            (1.0 - second) * masked_score,
            jnp.where(lane == 1, second * masked_score, 0.0),
        ).astype(bf16)


def attention_forward(layer, hidden, gains, block, bias_ref, weights, saved):
    qkv_ref, prob_ref, inv_ref, mixed_ref = (ref.at[layer] for ref in saved)
    bias_at = layer * (bias_ref.shape[0] // 2)
    rows, width = hidden.shape
    pairs = width // LANES
    tiles = rows // TILE
    big_ref = weights.big_ref.at[layer]
    normed = (hidden * inverse_rms(hidden) * gains).astype(bf16)
    weights.wait_attention(layer)
    lane = lane_index(rows)
    first_rows = row_index(rows) < HD
    extra = lax.broadcasted_iota(jnp.int32, (16, rows), 0)

    projected = dot(normed, big_ref[:, : 3 * width])

    def project(p):
        at = p * LANES
        q = turn(projected[:, at : at + LANES], block.cosine, block.sine)
        k = turn(projected[:, width + at : width + at + LANES], block.cosine, block.sine)
        v = projected[:, 2 * width + at : 2 * width + at + LANES]
        qkv_ref[:, at : at + LANES] = (q * HD**-0.5).astype(bf16)
        qkv_ref[:, width + at : width + at + LANES] = k.astype(bf16)
        qkv_ref[:, 2 * width + at : 2 * width + at + LANES] = v.astype(bf16)

    def operands(p):
        at = p * LANES
        q_pair = qkv_ref[:, at : at + LANES]
        k_aug = jnp.concatenate([qkv_ref[:, width + at : width + at + LANES], block.item_k], axis=1)
        v_turned = qkv_ref[:, 2 * width + at : 2 * width + at + LANES].T
        heads = []
        for half in range(2):
            q_aug = jnp.concatenate(
                [jnp.where(in_head(half, lane, True), q_pair, 0.0).astype(bf16), block.item_q],
                axis=1,
            )
            own_rows = first_rows if half == 0 else jnp.logical_not(first_rows)
            v_aug = jnp.concatenate(
                [
                    jnp.where(own_rows, v_turned, 0.0).astype(bf16),
                    jnp.where(extra == half, 1.0, 0.0).astype(bf16),
                ],
                axis=0,
            )
            heads.append((q_aug, v_aug))
        return k_aug, heads

    prepared = {}

    def scores_of(p, half, t):
        if p not in prepared:
            project(p)
            prepared[p] = operands(p)
        k_aug, heads = prepared[p]
        return dot(k_aug, heads[half][0][t * TILE : (t + 1) * TILE, :], RIGHT_T)

    order = [(p, half, t) for p in range(pairs) for half in range(2) for t in range(tiles)]
    attended = {}
    scores = scores_of(*order[0])
    for n, (p, half, t) in enumerate(order):
        following = scores_of(*order[n + 1]) if n + 1 < len(order) else None
        head = 2 * p + half
        cols = slice(t * TILE, (t + 1) * TILE)
        gap = bias_ref[bias_at + 2 * head] - bias_ref[bias_at + 2 * head + 1]
        biased = scores + block.same_ref[:, cols] * gap
        peak = jnp.max(biased, axis=0, keepdims=True)
        prob = jnp.exp(biased - peak).astype(bf16)
        prob_ref[head, :, cols] = prob
        part = dot(prepared[p][1][half][1], prob)
        attended[p, t] = part if half == 0 else attended[p, t] + part
        if half == 1:
            sums = attended.pop((p, t))
            own_rows = row_index(TILE) < HD
            inv = jnp.where(
                own_rows, 1.0 / sums[LANES : LANES + 1], 1.0 / sums[LANES + 1 : LANES + 2]
            )
            inv_ref[cols, p * LANES : (p + 1) * LANES] = inv.T
            mixed_ref[cols, p * LANES : (p + 1) * LANES] = (sums[:LANES] * inv).T
        scores = following
    return hidden + dot(mixed_ref[...].astype(bf16), big_ref[:, 3 * width : 4 * width])


def feed_forward(layer, middle, gains, weights):
    big_ref, down_ref = weights.big_ref.at[layer], weights.down_ref.at[layer]
    weights.wait_feed(layer)
    width = middle.shape[1]
    hidden = down_ref.shape[0]
    feed = (middle * inverse_rms(middle) * gains).astype(bf16)
    total = middle
    for at in range(0, hidden, CHUNK):
        gate = dot(feed, big_ref[:, 4 * width + at : 4 * width + at + CHUNK])
        up = dot(feed, big_ref[:, 4 * width + hidden + at : 4 * width + hidden + at + CHUNK])
        active = (gate * sigmoid(gate) * up).astype(bf16)
        total = total + dot(active, down_ref[at : at + CHUNK, :])
    return total.astype(bf16)


def feed_backward(layer, middle, gains, grad_low, weights, accs):
    gate_acc, up_acc, down_acc, gain_acc = (acc.at[layer] for acc in accs)
    big_ref, down_ref = weights.big_ref.at[layer], weights.down_ref.at[layer]
    width = middle.shape[1]
    hidden = down_ref.shape[0]
    inverse = inverse_rms(middle)
    feed = (middle * inverse * gains).astype(bf16)
    feed_t = feed.T
    feed_grad = jnp.zeros(middle.shape, f32)
    for at in range(0, hidden, CHUNK):
        gate_w = big_ref[:, 4 * width + at : 4 * width + at + CHUNK]
        up_w = big_ref[:, 4 * width + hidden + at : 4 * width + hidden + at + CHUNK]
        down_w = down_ref[at : at + CHUNK, :]
        gate = dot(feed, gate_w)
        up = dot(feed, up_w)
        act_grad = dot(grad_low, down_w, RIGHT_T)
        gated = sigmoid(gate)
        swish = gate * gated
        active = (swish * up).astype(bf16)
        gate_grad = (act_grad * up * (gated + swish * (1.0 - gated))).astype(bf16)
        up_grad = (act_grad * swish).astype(bf16)
        feed_grad = feed_grad + dot(gate_grad, gate_w, RIGHT_T) + dot(up_grad, up_w, RIGHT_T)
        gate_acc[:, at : at + CHUNK] += dot(feed_t, gate_grad)
        up_acc[:, at : at + CHUNK] += dot(feed_t, up_grad)
        down_acc[at : at + CHUNK, :] += dot(active, grad_low, LEFT_T)
    scaled = feed_grad * gains
    gain_acc[...] += jnp.sum(feed_grad * middle * inverse, axis=0, keepdims=True)
    return (
        grad_low.astype(f32)
        + inverse * scaled
        - middle * (inverse * inverse * inverse) * jnp.mean(scaled * middle, axis=1, keepdims=True)
    )


def attention_backward(layer, middle_grad, hidden, gains, block, weights, saved, grads_ref, accs):
    qkv_ref, prob_ref, inv_ref, mixed_ref = (ref.at[layer] for ref in saved)
    qkv_acc, out_acc, gain_acc, bias_acc = (acc.at[layer] for acc in accs)
    rows, width = hidden.shape
    pairs = width // LANES
    tiles = rows // TILE
    big_ref = weights.big_ref.at[layer]
    mix_grad = middle_grad.astype(bf16)
    att_grad = dot(mix_grad, big_ref[:, 3 * width : 4 * width], RIGHT_T).astype(bf16)
    lane = lane_index(rows)
    ones_four = jnp.where(lane < 4, 1.0, 0.0).astype(bf16)
    source = lax.broadcasted_iota(jnp.int32, (2 * LANES, LANES), 0) % LANES // HD
    target = lax.broadcasted_iota(jnp.int32, (2 * LANES, LANES), 1)
    gather = jnp.where((target // 2 == source) & (target < 4), 1.0, 0.0).astype(bf16)

    def operands(p):
        at = p * LANES
        q_pair = qkv_ref[:, at : at + LANES]
        k_turned = qkv_ref[:, width + at : width + at + LANES].T
        v_aug = jnp.concatenate(
            [qkv_ref[:, 2 * width + at : 2 * width + at + LANES], ones_four], axis=1
        )
        grad_pair = (att_grad[:, at : at + LANES].astype(f32) * inv_ref[:, at : at + LANES]).astype(
            bf16
        )
        product = grad_pair.astype(f32) * mixed_ref[:, at : at + LANES]
        high = product.astype(bf16)
        low = (product - high.astype(f32)).astype(bf16)
        inner = dot(jnp.concatenate([high, low], axis=1), gather)
        inner_high = inner.astype(bf16).astype(f32)
        tail = jnp.where(lane % 2 == 0, -inner_high, inner_high - inner)
        heads = []
        for half in range(2):
            grad_low = jnp.where(in_head(half, lane, False), grad_pair, 0.0).astype(bf16)
            tail_low = jnp.where(lane // 2 == half, tail, 0.0).astype(bf16)
            q_mine = jnp.where(in_head(half, lane, True), q_pair, 0.0).astype(bf16)
            k_mine = jnp.where(in_head(half, row_index(rows), True), k_turned, 0.0).astype(bf16)
            heads.append(
                (jnp.concatenate([grad_low, tail_low], axis=1), grad_low, q_mine, k_mine)
            )
        return v_aug, heads

    prepared = {}

    def prob_grad_of(p, half, t):
        if p not in prepared:
            prepared[p] = operands(p)
        v_aug, heads = prepared[p]
        return dot(v_aug, heads[half][0][t * TILE : (t + 1) * TILE, :], RIGHT_T)

    order = [(p, half, t) for p in range(pairs) for half in range(2) for t in range(tiles)]
    value_grad = key_grad = None
    query_grad = {}
    prob_grad = prob_grad_of(*order[0])
    for n, (p, half, t) in enumerate(order):
        following = prob_grad_of(*order[n + 1]) if n + 1 < len(order) else None
        head = 2 * p + half
        cols = slice(t * TILE, (t + 1) * TILE)
        at = p * LANES
        _, grad_low, q_mine, k_mine = prepared[p][1][half]
        prob = prob_ref[head, :, cols]
        score_grad = prob.astype(f32) * prob_grad
        bias_acc[head : head + 1, cols] += jnp.sum(
            score_grad * block.same_ref[:, cols], axis=0, keepdims=True
        )
        score_low = score_grad.astype(bf16)
        part_v = dot(prob, grad_low[cols, :])
        part_k = dot(score_low, q_mine[cols, :])
        part_q = dot(k_mine, score_low)
        value_grad = part_v if value_grad is None else value_grad + part_v
        key_grad = part_k if key_grad is None else key_grad + part_k
        query_grad[t] = part_q if half == 0 else query_grad[t] + part_q
        if half == 1:
            back = query_grad[t].T * HD**-0.5
            grads_ref[cols, at : at + LANES] = turn_back(
                back, block.cosine[cols, :], block.sine[cols, :]
            ).astype(bf16)
        if half == 1 and t == tiles - 1:
            grads_ref[:, width + at : width + at + LANES] = turn_back(
                key_grad, block.cosine, block.sine
            ).astype(bf16)
            grads_ref[:, 2 * width + at : 2 * width + at + LANES] = value_grad.astype(bf16)
            value_grad = key_grad = None
        prob_grad = following
    out_acc[...] += dot(mixed_ref[...].astype(bf16), mix_grad, LEFT_T)
    inverse = inverse_rms(hidden)
    normed = (hidden * inverse * gains).astype(bf16)
    normed_grad = dot(grads_ref[...], big_ref[:, : 3 * width], RIGHT_T)
    qkv_acc[...] += dot(normed, grads_ref[...], LEFT_T)
    scaled = normed_grad * gains
    gain_acc[...] += jnp.sum(normed_grad * hidden * inverse, axis=0, keepdims=True)
    return (
        middle_grad
        + inverse * scaled
        - hidden * (inverse * inverse * inverse) * jnp.mean(scaled * hidden, axis=1, keepdims=True)
    )


def column_tiles(acc_ref):
    return [acc_ref[:, at : at + LANES] for at in range(0, acc_ref.shape[1], LANES)]


class Packer:
    def __init__(self, stage_ref, sems, kept_refs, sent_refs):
        self.stage_ref, self.sems = stage_ref, sems
        self.kept_refs, self.sent_refs = kept_refs, sent_refs
        self.sent = []

    def copy(self, out_ref, slot, count):
        source = self.stage_ref.at[slot, pl.ds(0, count)]
        return pltpu.make_async_copy(source, out_ref, self.sems.at[slot])

    def send(self, keep, part, start, tiles):
        slot = len(self.sent) % 2
        if len(self.sent) >= 2:
            self.wait(2)
        at = 0
        for tile in tiles:
            self.stage_ref[slot, at : at + tile.shape[0], :] = tile.astype(bf16)
            at += tile.shape[0]
        where = pl.ds(start, at)

        @pl.when(keep)
        def _():
            self.copy(self.kept_refs[part].at[where], slot, at).start()

        @pl.when(jnp.logical_not(keep))
        def _():
            self.copy(self.sent_refs[part].at[where], slot, at).start()

        self.sent.append((self.kept_refs[part].at[where], slot, at))

    def wait(self, back):
        self.copy(*self.sent[-back]).wait()

    def finish(self):
        self.wait(2)
        self.wait(1)


def layers_body(
    sec_ref, bias_ref, x_ref, cotangent_ref, sid_ref, item_ref, var_ref, stats_ref, table_ref,
    gain_ref, *refs
):
    own_refs, other_refs, refs = refs[:7], refs[7:14], refs[14:]
    results_ref, grad_one_ref, grad_zero_ref, series_ref, small_ref = refs[:5]
    kept_refs, sent_refs, refs = refs[5:7], refs[7:9], refs[9:]
    big_ref, down_ref, refs = refs[0], refs[1], refs[2:]
    feed_accs, attention_accs, saved, refs = refs[:4], refs[4:8], refs[8:12], refs[12:]
    same_ref, grads_ref, hidden_ref, middle_ref, grad_ref, stage_ref, sems, stage_sems = refs

    i = pl.program_id(0)
    last = i == pl.num_programs(0) - 1
    m = pl.num_programs(0) * sec_ref[0] + i
    weights = Weights(sec_ref[0], own_refs, other_refs, big_ref, down_ref, sems)

    @pl.when(i == 0)
    def _():
        for acc in feed_accs + attention_accs:
            acc[...] = jnp.zeros_like(acc)

    x = x_ref[0].astype(f32)
    rows, width = x.shape
    var_row = var_ref[pl.ds(m, 1), :]
    var_col = column(var_row)
    sid_col = column(sid_ref[pl.ds(m, 1), :])
    pieces = stats_ref.shape[-1] // LANES

    time = lax.broadcasted_iota(jnp.int32, (rows, LANES), 0).astype(f32) - var_col
    cosine = sine = jnp.zeros((rows, LANES), f32)
    for at in range(0, rows, LANES):
        hot = jnp.where(time == (lane_index(rows) + at).astype(f32), 1.0, 0.0).astype(bf16)
        found = dot(hot, table_ref[at : at + LANES, :])
        cosine = cosine + found[:, :LANES] + found[:, LANES : 2 * LANES]
        sine = sine + found[:, 2 * LANES : 3 * LANES] + found[:, 3 * LANES :]
    block = Block(cosine, sine, column(item_ref[pl.ds(m, 1), :]), var_col, var_row, same_ref)

    _, centre, scaling = centre_and_scale(stats_ref[0], width)
    centre_rows = scale_rows = 0.0
    for piece in range(pieces):
        hits = series_hits(sid_col, piece)
        part = slice(piece * LANES, (piece + 1) * LANES)
        centre_rows = centre_rows + rows_of(hits, centre[:, part])
        scale_rows = scale_rows + rows_of(hits, scaling[:, part])
    hidden_ref[0] = (x - centre_rows) / scale_rows
    grad_ref[...] = cotangent_ref[0]

    def forward(layer, _):
        middle = attention_forward(
            layer, hidden_ref[layer], gain_ref[layer, 0:1, :], block, bias_ref, weights, saved
        )
        middle_ref[layer] = middle
        result = feed_forward(layer, middle, gain_ref[layer, 1:2, :], weights)
        results_ref[layer, 0] = result

        @pl.when(layer == 0)
        def _():
            hidden_ref[1] = result.astype(f32)

    def send(layer):
        packer = Packer(stage_ref, stage_sems, kept_refs, sent_refs)
        keep = sec_ref[0] == layer
        gate, up, down = (column_tiles(acc.at[layer]) for acc in feed_accs[:3])
        queries = column_tiles(attention_accs[0].at[layer])
        turned = [regroup(tile) for tile in queries[:6]]
        start = 0
        for tiles in (gate, up, down):
            packer.send(keep, 0, start, tiles)
            start += sum(tile.shape[0] for tile in tiles)
        packer.send(keep, 1, 0, turned)
        packer.send(keep, 1, width * 6, queries[6:] + column_tiles(attention_accs[1].at[layer]))
        packer.finish()

    def backward(step, _):
        layer = 1 - step
        middle_grad = feed_backward(
            layer, middle_ref[layer], gain_ref[layer, 1:2, :], grad_ref[...], weights, feed_accs
        )
        hidden_grad = attention_backward(
            layer, middle_grad, hidden_ref[layer], gain_ref[layer, 0:1, :], block, weights,
            saved, grads_ref, attention_accs,
        )
        grad_ref[...] = hidden_grad.astype(bf16)
        grad_zero_ref[0] = hidden_grad

        @pl.when(layer == 1)
        def _():
            grad_one_ref[0] = hidden_grad.astype(bf16)

        @pl.when(last)
        def _():
            send(layer)

    lax.fori_loop(0, 2, forward, None)
    lax.fori_loop(0, 2, backward, None)

    standard, hidden_grad = hidden_ref[0], grad_zero_ref[0]
    grad_rows = jnp.sum(hidden_grad, axis=1, keepdims=True)
    cross_rows = jnp.sum(hidden_grad * standard, axis=1, keepdims=True)
    standard_rows = jnp.sum(standard, axis=1, keepdims=True)
    series_ref[0] = jnp.zeros(series_ref.shape[1:], f32)
    for piece in range(pieces):
        hits = series_hits(sid_col, piece)
        part = slice(piece * LANES, (piece + 1) * LANES)
        series_ref[0, 0:1, part] = series_of(hits, grad_rows)
        series_ref[0, 1:2, part] = series_of(hits, cross_rows)
        series_ref[0, 2:3, part] = series_of(hits, standard_rows)

    @pl.when(last)
    def _():
        small_ref[...] = jnp.zeros_like(small_ref)
        for layer in range(2):
            base = 24 * layer
            for k in range(width // LANES):
                cols = slice(k * LANES, (k + 1) * LANES)
                small_ref[base + k : base + k + 1, :] = attention_accs[2][layer, :, cols]
                small_ref[base + 16 + k : base + 17 + k, :] = feed_accs[3][layer, :, cols]
            bias_sums = jnp.sum(attention_accs[3][layer], axis=1, keepdims=True)
            small_ref[base + 8 : base + 16, :] = jnp.broadcast_to(bias_sums, (8, LANES))


def final_body(
    sec_ref, x_ref, sid_ref, stats_ref, series_ref, own_first, own_second, other_grad,
    own_out, other_out, out_ref, grads_ref,
):
    i = pl.program_id(0)
    sec = sec_ref[0]
    own = (i // (pl.num_programs(0) // 2)) == sec
    grads_ref[0] = jnp.where(own, own_out[0], other_out[0])
    grad = jnp.where(
        own,
        jnp.where(sec == 0, own_first[0], own_second[0].astype(f32)),
        other_grad[0].astype(f32),
    )

    @pl.when(sec == 0)
    def _():
        x = x_ref[0].astype(f32)
        width = x.shape[1]
        entries, centre, scaling = centre_and_scale(stats_ref[0], width)
        sums = series_ref[0]
        cross = sums[1:2] * scaling
        spread_grad = -cross / (2.0 * scaling * scaling * scaling * entries)
        mean_grad = sums[0:1] / scaling + 2.0 * spread_grad * (sums[2:3] * scaling)
        tables = (centre, 1.0 / scaling, 2.0 * spread_grad, mean_grad / entries)
        sid_col = column(sid_ref[pl.ds(i, 1), :])
        looked = [0.0, 0.0, 0.0, 0.0]
        for piece in range(stats_ref.shape[-1] // LANES):
            hits = series_hits(sid_col, piece)
            part = slice(piece * LANES, (piece + 1) * LANES)
            for k in range(4):
                looked[k] = looked[k] + rows_of(hits, tables[k][:, part])
        out_ref[0] = grad * looked[1] + (x - looked[0]) * looked[2] - looked[3]

    @pl.when(sec != 0)
    def _():
        out_ref[0] = grad


class Halves:
    def __init__(self, own_ref, got_ref, bit):
        self.own_ref, self.got_ref, self.bit = own_ref, got_ref, bit
        self.half = own_ref.shape[0]
        self.at = 0

    def rows(self, start, count, low):
        own = self.own_ref[start : start + count, :]
        got = self.got_ref[start : start + count, :]
        return jnp.where((self.bit == 0) == low, own, got).astype(f32)

    def take(self, out_ref, col, count):
        done = 0
        while done < count:
            low = self.at < self.half
            room = min(count - done, (self.half if low else 2 * self.half) - self.at)
            out_ref[done : done + room, col : col + LANES] = self.rows(
                self.at - (0 if low else self.half), room, low
            )
            done += room
            self.at += room


def unpack_body(bit_ref, *refs):
    parts = [Halves(refs[2 * k], refs[2 * k + 1], bit_ref[k]) for k in range(2)]
    refs = refs[4:]
    count = len(refs) // 2
    outs, scratch, sems = refs[:count], refs[count : 2 * count], refs[2 * count]
    copies = []
    for out_ref, scratch_ref in zip(outs, scratch):
        for col in range(0, scratch_ref.shape[1], LANES):
            while parts[0].at == 2 * parts[0].half:
                parts.pop(0)
            parts[0].take(scratch_ref, col, scratch_ref.shape[0])
        copies.append(pltpu.make_async_copy(scratch_ref, out_ref, sems.at[len(copies)]))
        copies[-1].start()
    for copy in copies:
        copy.wait()


def unpack_small_body(sec_ref, small_ref, attention_gain_ref, feed_gain_ref, bias_ref):
    base = 24 * sec_ref[0]
    for k in range(attention_gain_ref.shape[1] // LANES):
        cols = slice(k * LANES, (k + 1) * LANES)
        attention_gain_ref[:, cols] = small_ref[pl.ds(base + k, 1), :]
        feed_gain_ref[:, cols] = small_ref[pl.ds(base + 16 + k, 1), :]
    same = small_ref[pl.ds(base + 8, 8), :].T[0:1, : bias_ref.shape[1]]
    bias_ref[0:1, :] = same
    bias_ref[1:2, :] = -same


def swapped(x):
    return lax.ppermute(x, "section", [(0, 1), (1, 0)])


def to_section(x, section):
    return lax.ppermute(x, "section", [(1 - section, section)])


def exchange_steps(count):
    bits = []
    step = 1
    while step < count:
        bits.append(step)
        step *= 2
    other = list(bits)
    for k in range(0, len(bits) - 1, 2):
        other[k], other[k + 1] = bits[k + 1], bits[k]
    return bits, other


def partner(x, by_first, by_second, count):
    pairs = [(i, i ^ by_first) for i in range(count)]
    pairs += [(count + i, count + (i ^ by_second)) for i in range(count)]
    return lax.ppermute(x, ("section", "dp"), pairs)


def place(steps, section, index):
    step = jnp.where(section == 0, *steps)
    return (index // step) % 2


def halve(parts, orders, k, section, index, count, *more):
    keeps, sends = [], []
    for current, order in zip(parts, orders):
        bit = place(order[k], section, index)
        half = current.shape[0] // 2
        keeps.append(lax.dynamic_slice_in_dim(current, bit * half, half, 0))
        sends.append(lax.dynamic_slice_in_dim(current, (1 - bit) * half, half, 0))
    sends, keeps, more = lax.optimization_barrier((sends, keeps, more))
    got = [partner(send, *order[k], count) for send, order in zip(sends, orders)]
    parts = [(a.astype(f32) + b.astype(f32)).astype(bf16) for a, b in zip(keeps, got)]
    return (parts, *more)


def double(parts, orders, k, section, index, count):
    parts = lax.optimization_barrier(parts)
    result = []
    for current, order in zip(parts, orders):
        bit = place(order[k], section, index)
        got = partner(current, *order[k], count)
        low = jnp.where(bit == 0, current, got)
        high = jnp.where(bit == 0, got, current)
        result.append(jnp.concatenate([low, high], axis=0))
    return result


HBM = pl.BlockSpec(memory_space=pl.ANY)
SCALARS = pl.BlockSpec(memory_space=pltpu.SMEM)


def whole_block(shape):
    return pl.BlockSpec(shape, lambda i, *_: (0,) * len(shape))


def by_step(shape):
    return pl.BlockSpec((1,) + shape, lambda i, *_: (i,) + (0,) * len(shape))


def by_batch(shape, own):
    return pl.BlockSpec((1,) + shape, lambda i, s: (own * s[0] + i,) + (0,) * len(shape))


def call(body, grid, in_specs, out_specs, out_shapes, scratch, flops, name):
    return pl.pallas_call(
        body,
        grid_spec=pltpu.PrefetchScalarGridSpec(
            num_scalar_prefetch=1,
            grid=(grid,),
            in_specs=in_specs,
            out_specs=out_specs,
            scratch_shapes=scratch,
        ),
        out_shape=out_shapes,
        compiler_params=pltpu.CompilerParams(vmem_limit_bytes=57 * 2**20),
        cost_estimate=pl.CostEstimate(flops=flops, bytes_accessed=2**22, transcendentals=0),
        name=name,
    )


def shape(*dims, dtype=f32):
    return jax.ShapeDtypeStruct(dims, dtype)


class Sizes:
    def __init__(self, inputs, heads, hidden, count):
        self.micro, self.rows, self.width = inputs.shape
        self.own = self.micro // 2
        self.heads, self.hidden, self.count = heads, hidden, count
        rows, width, own = self.rows, self.width, self.own
        self.stats = (8, -(-SER_DEV * count // LANES) * LANES)
        self.all_rows = whole_block((self.micro, rows))
        self.row = by_step((rows, width))
        self.row_batch = by_batch((rows, width), own)
        self.gain = whole_block((8, width))
        self.row_shape = shape(own, rows, width)
        self.low_shape = shape(own, rows, width, dtype=bf16)
        self.flops = 2 * rows * (4 * width * width + 3 * width * hidden) * own


def rotary_table(rows):
    lane = np.arange(LANES)
    frequency = np.float32(10000.0) ** (
        -(lane % (HD // 2)).astype(np.float32) * np.float32(2.0 / HD)
    )
    angle = np.arange(rows, dtype=np.float32)[:, None] * frequency[None, :].astype(np.float32)
    cosine = np.cos(angle.astype(np.float64))
    sine = np.sin(angle.astype(np.float64)) * np.where(lane < HD, -1.0, 1.0)
    parts = []
    for values in (cosine, sine):
        high = values.astype(jnp.bfloat16)
        parts += [high, (values - high.astype(np.float64)).astype(jnp.bfloat16)]
    return np.concatenate(parts, axis=1)


def series_stats(z, sec, inputs, series_id):
    return call(
        stats_body, z.own, [z.row_batch, z.all_rows], by_step(z.stats), shape(z.own, *z.stats),
        [], 10**7, "series_stats",
    )(sec, inputs, series_id)


def layers(z, sec, bias, inputs, cotangent, series_id, item, variate, stats, gains, own, other):
    table = rotary_table(z.rows)
    rows, width, hidden = z.rows, z.width, z.hidden
    parts = [
        shape(3 * width * hidden // LANES, LANES, dtype=bf16),
        shape(4 * width * width // LANES, LANES, dtype=bf16),
    ]

    def both(*dims, dtype=f32):
        return pltpu.VMEM((2,) + dims, dtype)

    return call(
        layers_body, z.own,
        [SCALARS, z.row_batch, z.row_batch, z.all_rows, z.all_rows, z.all_rows, by_step(z.stats),
         whole_block(table.shape), whole_block((2, 8, width))] + [HBM] * 14,
        [pl.BlockSpec((2, 1, rows, width), lambda i, *_: (0, i, 0, 0)), z.row, z.row,
         by_step(z.stats), whole_block((48, LANES))] + [HBM] * 4,
        [shape(2, z.own, rows, width, dtype=bf16), z.low_shape, z.row_shape,
         shape(z.own, *z.stats), shape(48, LANES)] + parts * 2,
        [both(width, 4 * width + 2 * hidden, dtype=bf16), both(hidden, width, dtype=bf16),
         both(width, hidden), both(width, hidden), both(hidden, width), both(1, width),
         both(width, 3 * width), both(width, width), both(1, width), both(8, rows),
         both(rows, 3 * width, dtype=bf16), both(z.heads, rows, rows, dtype=bf16),
         both(rows, width), both(rows, width),
         pltpu.VMEM((rows, rows), f32), pltpu.VMEM((rows, 3 * width), bf16),
         both(rows, width), both(rows, width), pltpu.VMEM((rows, width), bf16),
         both(8 * width, LANES, dtype=bf16),
         pltpu.SemaphoreType.DMA((2, 7)), pltpu.SemaphoreType.DMA((2,))],
        12 * z.flops, "layers",
    )(sec, bias, inputs, cotangent, series_id, item, variate, stats, jnp.asarray(table),
      gains, *own, *other)


def final(z, sec, inputs, series_id, stats, series, own_first, own_second, other_grad,
          own_out, other_out):
    own_count = z.own

    def own_step(i, s):
        return (jnp.clip(i - own_count * s[0], 0, own_count - 1), 0, 0)

    def other_step(i, s):
        return (jnp.clip(i - own_count * (1 - s[0]), 0, own_count - 1), 0, 0)

    own_spec = pl.BlockSpec((1, z.rows, z.width), own_step)
    other_spec = pl.BlockSpec((1, z.rows, z.width), other_step)
    return call(
        final_body, z.micro,
        [z.row, z.all_rows, by_step(z.stats), by_step(z.stats), own_spec, own_spec,
         other_spec, own_spec, other_spec],
        [z.row, z.row],
        [shape(z.micro, z.rows, z.width), shape(z.micro, z.rows, z.width, dtype=bf16)],
        [], 10**10, "final",
    )(sec, inputs, series_id, stats, series, own_first, own_second, other_grad, own_out, other_out)


def per_device(
    inputs,
    series_id,
    item_offset,
    variate_offset,
    cotangent,
    attention_gain,
    query_weight,
    key_weight,
    value_weight,
    out_weight,
    variate_bias,
    feed_gain,
    gate_weight,
    up_weight,
    down_weight,
):
    section = lax.axis_index("section")
    index = lax.axis_index("dp")
    count = lax.axis_size("dp")
    on_first = section == 0
    sec = section.astype(jnp.int32).reshape(1)
    heads = variate_bias.shape[1]
    z = Sizes(inputs, heads, down_weight.shape[1], count)
    width = z.width

    stats = series_stats(z, sec, inputs, series_id)
    for step in exchange_steps(count)[0]:
        stats = merge_stats(stats, partner(stats, step, step, count), width)

    own_small = jnp.concatenate(
        [
            attention_gain,
            feed_gain,
            jnp.pad(variate_bias.reshape(1, 2 * heads), ((0, 0), (0, width - 2 * heads))),
        ],
        axis=0,
    ).astype(f32)
    own_small = jnp.pad(own_small, ((0, 5), (0, 0)))
    other_small = swapped(own_small)
    own = tuple(
        w[0]
        for w in (
            query_weight, key_weight, value_weight, out_weight, gate_weight, up_weight, down_weight
        )
    )
    other = tuple(swapped(w) for w in own)
    gains = (
        jnp.where(on_first, own_small, other_small),
        jnp.where(on_first, other_small, own_small),
    )
    gains = jnp.stack(gains)
    bias = gains[:, 2, : 2 * heads].reshape(-1)

    results, grad_one, standard_grad, series_sums, small_sums, *packs = layers(
        z, sec, bias, inputs, cotangent, series_id, item_offset, variate_offset, stats, gains,
        own, other,
    )
    result_one, result_two = results[0], results[1]

    parts = [
        (k.astype(f32) + swapped(t).astype(f32)).astype(bf16)
        for k, t in zip(packs[:2], packs[2:])
    ]
    bits, turned = exchange_steps(count)
    near = list(zip(bits, turned))
    orders = (near, near[2:] + near[:2])
    rounds = len(bits)

    series_rows = z.own * z.stats[0] * z.stats[1] // LANES
    small = jnp.concatenate(
        [series_sums.reshape(-1, LANES), small_sums], axis=0
    )
    for k in range(rounds):
        parts, small = halve(parts, orders, k, section, index, count, small)
        small = small + partner(small, bits[rounds - 1 - k], bits[rounds - 1 - k], count)
    other_sums = swapped(small)
    mine = small[:series_rows].reshape((z.own,) + z.stats)
    theirs = other_sums[:series_rows].reshape((z.own,) + z.stats)
    series_all = jnp.where(
        on_first, jnp.concatenate([mine, theirs]), jnp.concatenate([theirs, mine])
    )
    small = small[series_rows:] + other_sums[series_rows:]
    other_stats = swapped(stats)
    stats_all = jnp.where(
        on_first, jnp.concatenate([stats, other_stats]), jnp.concatenate([other_stats, stats])
    )

    own_out = jnp.where(on_first, result_one, result_two)
    other_out = swapped(jnp.where(on_first, result_two, result_one))
    other_grad = swapped(jnp.where(on_first, grad_one, standard_grad.astype(bf16)))

    for k in reversed(range(1, rounds)):
        parts = double(parts, orders, k, section, index, count)
    sec_late, parts = lax.optimization_barrier((sec, parts))
    input_grads, section_output = final(
        z, sec_late, inputs, series_id, stats_all, series_all, standard_grad, grad_one, other_grad,
        own_out, other_out,
    )
    others = [partner(p, *o[0], count) for p, o in zip(parts, orders)]
    parts, input_grads, section_output = lax.optimization_barrier(
        (parts, input_grads, section_output)
    )
    last_bits = jnp.stack([place(o[0], section, index) for o in orders]).astype(jnp.int32)

    vmem = pl.BlockSpec(memory_space=pltpu.VMEM)

    large = [shape(width, z.hidden)] * 2 + [shape(z.hidden, width)] + [shape(width, width)] * 4
    grad_gate, grad_up, grad_down, grad_query, grad_key, grad_value, grad_out = pl.pallas_call(
        unpack_body,
        in_specs=[SCALARS] + [vmem] * 4,
        out_specs=[HBM] * 7,
        out_shape=large,
        scratch_shapes=[pltpu.VMEM(s.shape, f32) for s in large] + [pltpu.SemaphoreType.DMA((7,))],
        compiler_params=pltpu.CompilerParams(vmem_limit_bytes=57 * 2**20),
        name="unpack",
    )(last_bits, *(array for pair in zip(parts, others) for array in pair))
    grad_attention_gain, grad_feed_gain, grad_bias = pl.pallas_call(
        unpack_small_body,
        in_specs=[SCALARS, vmem],
        out_shape=[shape(1, width)] * 2 + [shape(2, heads)],
        name="unpack_small",
    )(sec, small)
    return (
        section_output[None],
        input_grads[None],
        grad_attention_gain,
        grad_query[None],
        grad_key[None],
        grad_value[None],
        grad_out[None],
        grad_bias.T[None],
        grad_feed_gain,
        grad_gate[None],
        grad_up[None],
        grad_down[None],
    )


def solution(mesh):
    placed = (
        P(None, "dp", None),
        P(None, "dp"),
        P(None, "dp"),
        P(None, "dp"),
        P(None, "dp", None),
        P("section", None),
        P("section", None, None),
        P("section", None, None),
        P("section", None, None),
        P("section", None, None),
        P("section", None, None),
        P("section", None),
        P("section", None, None),
        P("section", None, None),
        P("section", None, None),
    )
    return jax.shard_map(
        per_device,
        mesh=mesh,
        in_specs=placed,
        out_specs=(
            P("section", None, "dp", None),
            P("section", None, "dp", None),
            P("section", None),
            P("section", None, None),
            P("section", None, None),
            P("section", None, None),
            P("section", None, None),
            P("section", None, None),
            P("section", None),
            P("section", None, None),
            P("section", None, None),
            P("section", None, None),
        ),
        check_vma=False,
    )
```

profile of v0, /device:TPU:0, one launch (start us, length us, event | category | flops | bytes accessed | tf_op | source)
XLA Modules:
  0.0 268.4 jit_solution(16404419218856835255)
XLA Ops:
  0.7 3.9 %series_stats.1 = f32[3,8,128]{2,1,0:T(8,128)} custom-call(s32[1]{0:T(128)} %bitcast.sec_ref, bf16[6,512,384]{2,1,0:T(8,128)(2,1)} %x_ref.5, s32[6,512]{1,0:T(8,128)} %sid_ref.5), custom_call_target="tpu_custom_call" | custom-call | flops 10000000 | bytes 4194304 | tf_op jit(solution)/shard_map/series_stats/pallas_call | solution.py:796
  4.6 2.9 %collective-permute-start.1 = (f32[3,8,128]{2,1,0:T(8,128)}, f32[3,8,128]{2,1,0:T(8,128)S(1)}, u32[]{:S(2)}, u32[]{:S(2)}) collective-permute-start(f32[3,8,128]{2,1,0:T(8,128)} %series_stats.1), channel_id=1, source_target_pairs={{0,1},{1,0},{2,3},{3,2},{4,5},{5,4},{6,7},{7,6},{8,9},{9,8},{10,11... | collective-permute-start | bytes 36872 | tf_op jit(solution)/shard_map/ppermute | solution.py:694
  10.3 2.1 collective-permute-start.2
  14.1 2.1 collective-permute-start.3
  18.0 3.1 %collective-permute-start.4 = (f32[3,8,128]{2,1,0:T(8,128)S(1)}, f32[3,8,128]{2,1,0:T(8,128)S(1)}, u32[]{:S(2)}, u32[]{:S(2)}) collective-permute-start(f32[3,8,128]{2,1,0:T(8,128)S(1)} %pad_maximum_fusion.9), channel_id=1, source_target_pairs={{0,8},{1,9},{2,10},{3,11},{4,12},{5,13},{6,14},{7,15},{8,0},{9,1},... | collective-permute-start | bytes 36872 | tf_op jit(solution)/shard_map/ppermute | solution.py:694
  27.5 116.4 %layers.1 = (bf16[2,3,512,384]{3,2,1,0:T(8,128)(2,1)}, bf16[3,512,384]{2,1,0:T(8,128)(2,1)}, f32[3,512,384]{2,1,0:T(8,128)}, f32[3,8,128]{2,1,0:T(8,128)}, f32[4...) custom-call(s32[1]{0:T(128)} %bitcast.sec_ref, ...), custom_call_target="tpu_custom_call" | custom-call | flops 65229815808 | bytes 4194304 | tf_op jit(solution)/shard_map/layers/pallas_call | solution.py:813
  151.5 2.0 collective-permute-start.15
  155.0 2.6 collective-permute-start.16
  157.6 10.4 %collective-permute-done.16 = f32[72,128]{1,0:T(8,128)} collective-permute-done((f32[72,128]{1,0:T(8,128)}, f32[72,128]{1,0:T(8,128)}, u32[]{:S(2)}, u32[]{:S(2)}) %collective-permute-start.16) | collective-permute-done | bytes 36896 | tf_op jit(solution)/shard_map/ppermute | solution.py:694
  171.5 3.4 %collective-permute-start.18 = (bf16[1152,128]{1,0:T(8,128)(2,1)S(1)}, bf16[1152,128]{1,0:T(8,128)(2,1)S(1)}, u32[]{:S(2)}, u32[]{:S(2)}) collective-permute-start(bf16[1152,128]{1,0:T(8,128)(2,1)S(1)} %get-tuple-element.80), channel_id=1, source_target_pairs={{0,8},{1,9},{2,10},{3,11},{4,12},{5,13},{6,14},{7,15},{8,0},{9,1},... | collective-permute-start | bytes 884744 | tf_op jit(solution)/shard_map/ppermute | solution.py:694
  176.4 5.5 %collective-permute-done.19 = f32[72,128]{1,0:T(8,128)S(1)} collective-permute-done((f32[72,128]{1,0:T(8,128)}, f32[72,128]{1,0:T(8,128)S(1)}, u32[]{:S(2)}, u32[]{:S(2)}) %collective-permute-start.19) | collective-permute-done | bytes 36896 | tf_op jit(solution)/shard_map/ppermute | solution.py:694
  182.8 2.0 collective-permute-done.17
  188.6 2.1 collective-permute-start.20
  190.8 7.7 %collective-permute-done.20 = bf16[1152,128]{1,0:T(8,128)(2,1)S(1)} collective-permute-done((bf16[1152,128]{1,0:T(8,128)(2,1)S(1)}, bf16[1152,128]{1,0:T(8,128)(2,1)S(1)}, u32[]{:S(2)}, u32[]{:S(2)}) %collective-permute-start.20) | collective-permute-done | bytes 294944 | tf_op jit(solution)/shard_map/ppermute | solution.py:694
  199.9 2.4 collective-permute-start.23
  203.1 2.9 %collective-permute-done.23 = bf16[576,128]{1,0:T(8,128)(2,1)S(1)} collective-permute-done((bf16[576,128]{1,0:T(8,128)(2,1)S(1)}, bf16[576,128]{1,0:T(8,128)(2,1)S(1)}, u32[]{:S(2)}, u32[]{:S(2)}) %collective-permute-start.23) | collective-permute-done | bytes 147488 | tf_op jit(solution)/shard_map/ppermute | solution.py:694
  206.1 3.1 %collective-permute-start.26 = (bf16[288,128]{1,0:T(8,128)(2,1)S(1)}, bf16[288,128]{1,0:T(8,128)(2,1)S(1)}, u32[]{:S(2)}, u32[]{:S(2)}) collective-permute-start(bf16[288,128]{1,0:T(8,128)(2,1)S(1)} %add_convert_fusion.9), channel_id=1, source_target_pairs={{0,2},{1,3},{2,0},{3,1},{4,6},{5,7},{6,4},{7,5},{8,10},{9,11},{10,... | collective-permute-start | bytes 221192 | tf_op jit(solution)/shard_map/ppermute | solution.py:694
  212.3 6.2 %collective-permute-done.25 = bf16[576,128]{1,0:T(8,128)(2,1)S(1)} collective-permute-done((bf16[576,128]{1,0:T(8,128)(2,1)S(1)}, bf16[576,128]{1,0:T(8,128)(2,1)S(1)}, u32[]{:S(2)}, u32[]{:S(2)}) %collective-permute-start.25) | collective-permute-done | bytes 147488 | tf_op jit(solution)/shard_map/ppermute | solution.py:694
  218.6 2.0 collective-permute-start.28
  223.9 8.5 %collective-permute-done.27 = bf16[1152,128]{1,0:T(8,128)(2,1)S(1)} collective-permute-done((bf16[1152,128]{1,0:T(8,128)(2,1)S(1)}, bf16[1152,128]{1,0:T(8,128)(2,1)S(1)}, u32[]{:S(2)}, u32[]{:S(2)}) %collective-permute-start.27) | collective-permute-done | bytes 294944 | tf_op jit(solution)/shard_map/ppermute | solution.py:694
  235.1 7.8 %collective-permute-done.30 = bf16[1152,128]{1,0:T(8,128)(2,1)S(1)} collective-permute-done((bf16[1152,128]{1,0:T(8,128)(2,1)S(1)}, bf16[1152,128]{1,0:T(8,128)(2,1)S(1)}, u32[]{:S(2)}, u32[]{:S(2)}) %collective-permute-start.30) | collective-permute-done | bytes 294944 | tf_op jit(solution)/shard_map/ppermute | solution.py:694
  245.8 2.5 collective-permute-start.37
  249.3 10.2 %final.1 = (f32[6,512,384]{2,1,0:T(8,128)}, bf16[6,512,384]{2,1,0:T(8,128)(2,1)}) custom-call(s32[1]{0:T(128)} %bitcast.sec_ref, bf16[6,512,384]{2,1,0:T(8,128)(2,1)} %x_ref.5, s32[6,512]{1,0:T(8,128)} %sid_ref.5, f32[6,8,128]{2,1,0:T(8,128)} %maximum_select_fusion.stats_ref, f32[6,8,128]{2,1,0:T(8,128)} %maximum_select_fusion.1.series_ref, ...), custom_call_target="tpu_custom_call" | custom-call | flops 10000000000 | bytes 4194304 | tf_op jit(solution)/shard_map/final/pallas_call | solution.py:847
  263.1 5.1 %unpack.1 = (f32[384,1024]{1,0:T(8,128)}, f32[384,1024]{1,0:T(8,128)}, f32[1024,384]{1,0:T(8,128)}, f32[384,384]{1,0:T(8,128)}, f32[384,384]{1,0:T(8,128)}, /*index=5*/f32[384,384]{1,0:T(8,128)}, f32[384,384]{1,0:T(8,128)}) custom-call(s32[2]{0:T(128)} %pad_add_fusion.bit_ref, bf16[4608,128]{1,0:T(8,128)(2,1)} %copy-done, bf16[4608,128]{1,0:T(8,128)(2,1)} %copy-done.6, ...), custom_call_target="tpu_custom_call" | custom-call | tf_op jit(solution)/shard_map/unpack/pallas_call | solution.py:965
  (165 shorter events, 50.2 us)
Async XLA Ops:
  16.3 10.2 %collective-permute-start.9 = (bf16[384,1024]{1,0:T(8,128)(2,1)S(1)}, bf16[384,1024]{1,0:T(8,128)(2,1)S(1)}, u32[]{:S(2)}, u32[]{:S(2)}) collective-permute-start(bf16[384,1024]{1,0:T(8,128)(2,1)S(1)} %bitcast.40), channel_id=1, source_target_pairs={{0,16},{16,0},{1,17},{17,1},{2,18},{18,2},{3,19},{19,3},{4,20},{20... | collective-permute-start | bytes 2359304 | tf_op jit(solution)/shard_map/ppermute | solution.py:672
  16.8 9.7 %collective-permute-start.10 = (bf16[384,1024]{1,0:T(8,128)(2,1)S(1)}, bf16[384,1024]{1,0:T(8,128)(2,1)}, u32[]{:S(2)}, u32[]{:S(2)}) collective-permute-start(bf16[384,1024]{1,0:T(8,128)(2,1)S(1)} %bitcast.42), channel_id=1, source_target_pairs={{0,16},{16,0},{1,17},{17,1},{2,18},{18,2},{3,19},{19,3},{4,20},{20... | collective-permute-start | bytes 2359304 | tf_op jit(solution)/shard_map/ppermute | solution.py:672
  16.9 9.6 %collective-permute-start.11 = (bf16[1024,384]{1,0:T(8,128)(2,1)S(1)}, bf16[1024,384]{1,0:T(8,128)(2,1)}, u32[]{:S(2)}, u32[]{:S(2)}) collective-permute-start(bf16[1024,384]{1,0:T(8,128)(2,1)S(1)} %bitcast.44), channel_id=1, source_target_pairs={{0,16},{16,0},{1,17},{17,1},{2,18},{18,2},{3,19},{19,3},{4,20},{20... | collective-permute-start | bytes 2359304 | tf_op jit(solution)/shard_map/ppermute | solution.py:672
  144.6 6.1 %collective-permute-start.12 = (bf16[9216,128]{1,0:T(8,128)(2,1)}, bf16[9216,128]{1,0:T(8,128)(2,1)S(1)}, u32[]{:S(2)}, u32[]{:S(2)}) collective-permute-start(bf16[9216,128]{1,0:T(8,128)(2,1)} %get-tuple-element.67), channel_id=1, source_target_pairs={{0,16},{16,0},{1,17},{17,1},{2,18},{18,2},{3,19},{19,3},{4,20},{20... | collective-permute-start | bytes 7077896 | tf_op jit(solution)/shard_map/ppermute | solution.py:672
  151.5 17.9 %collective-permute-start.15 = (bf16[2304,128]{1,0:T(8,128)(2,1)}, bf16[2304,128]{1,0:T(8,128)(2,1)S(1)}, u32[]{:S(2)}, u32[]{:S(2)}) collective-permute-start(bf16[2304,128]{1,0:T(8,128)(2,1)} %get-tuple-element.75), channel_id=1, source_target_pairs={{0,4},{1,5},{2,6},{3,7},{4,0},{5,1},{6,2},{7,3},{8,12},{9,13},{10,... | collective-permute-start | bytes 1769480 | tf_op jit(solution)/shard_map/ppermute | solution.py:694
  153.5 16.3 %collective-permute-start.14 = (bf16[4608,128]{1,0:T(8,128)(2,1)S(1)}, bf16[4608,128]{1,0:T(8,128)(2,1)}, u32[]{:S(2)}, u32[]{:S(2)}) collective-permute-start(bf16[4608,128]{1,0:T(8,128)(2,1)S(1)} %get-tuple-element.73), channel_id=1, source_target_pairs={{0,1},{1,0},{2,3},{3,2},{4,5},{5,4},{6,7},{7,6},{8,9},{9,8},{10,11... | collective-permute-start | bytes 3538952 | tf_op jit(solution)/shard_map/ppermute | solution.py:694
  155.0 13.0 %collective-permute-start.16 = (f32[72,128]{1,0:T(8,128)}, f32[72,128]{1,0:T(8,128)}, u32[]{:S(2)}, u32[]{:S(2)}) collective-permute-start(f32[72,128]{1,0:T(8,128)} %pad_maximum_fusion.6), channel_id=1, source_target_pairs={{0,8},{1,9},{2,10},{3,11},{4,12},{5,13},{6,14},{7,15},{8,0},{9,1},... | collective-permute-start | bytes 110600 | tf_op jit(solution)/shard_map/ppermute | solution.py:694
  171.5 11.1 %collective-permute-start.18 = (bf16[1152,128]{1,0:T(8,128)(2,1)S(1)}, bf16[1152,128]{1,0:T(8,128)(2,1)S(1)}, u32[]{:S(2)}, u32[]{:S(2)}) collective-permute-start(bf16[1152,128]{1,0:T(8,128)(2,1)S(1)} %get-tuple-element.80), channel_id=1, source_target_pairs={{0,8},{1,9},{2,10},{3,11},{4,12},{5,13},{6,14},{7,15},{8,0},{9,1},... | collective-permute-start | bytes 884744 | tf_op jit(solution)/shard_map/ppermute | solution.py:694
  174.9 7.0 %collective-permute-start.19 = (f32[72,128]{1,0:T(8,128)}, f32[72,128]{1,0:T(8,128)S(1)}, u32[]{:S(2)}, u32[]{:S(2)}) collective-permute-start(f32[72,128]{1,0:T(8,128)} %add.262), channel_id=1, source_target_pairs={{0,4},{1,5},{2,6},{3,7},{4,0},{5,1},{6,2},{7,3},{8,12},{9,13},{10,... | collective-permute-start | bytes 110600 | tf_op jit(solution)/shard_map/ppermute | solution.py:694
  174.9 9.9 %collective-permute-start.17 = (bf16[2304,128]{1,0:T(8,128)(2,1)S(1)}, bf16[2304,128]{1,0:T(8,128)(2,1)S(1)}, u32[]{:S(2)}, u32[]{:S(2)}) collective-permute-start(bf16[2304,128]{1,0:T(8,128)(2,1)S(1)} %get-tuple-element.78), channel_id=1, source_target_pairs={{0,2},{1,3},{2,0},{3,1},{4,6},{5,7},{6,4},{7,5},{8,10},{9,11},{10,... | collective-permute-start | bytes 1769480 | tf_op jit(solution)/shard_map/ppermute | solution.py:694
  188.6 10.7 %collective-permute-start.31 = (f32[3,8,128]{2,1,0:T(8,128)S(1)}, f32[3,8,128]{2,1,0:T(8,128)S(1)}, u32[]{:S(2)}, u32[]{:S(2)}) collective-permute-start(f32[3,8,128]{2,1,0:T(8,128)S(1)} %copy-done.12), channel_id=1, source_target_pairs={{0,16},{16,0},{1,17},{17,1},{2,18},{18,2},{3,19},{19,3},{4,20},{20... | collective-permute-start | bytes 36872 | tf_op jit(solution)/shard_map/ppermute | solution.py:672
  188.6 10.0 %collective-permute-start.20 = (bf16[1152,128]{1,0:T(8,128)(2,1)S(1)}, bf16[1152,128]{1,0:T(8,128)(2,1)S(1)}, u32[]{:S(2)}, u32[]{:S(2)}) collective-permute-start(bf16[1152,128]{1,0:T(8,128)(2,1)S(1)} %get-tuple-element.83), channel_id=1, source_target_pairs={{0,4},{1,5},{2,6},{3,7},{4,0},{5,1},{6,2},{7,3},{8,12},{9,13},{10,... | collective-permute-start | bytes 884744 | tf_op jit(solution)/shard_map/ppermute | solution.py:694
  199.9 6.1 %collective-permute-start.23 = (bf16[576,128]{1,0:T(8,128)(2,1)S(1)}, bf16[576,128]{1,0:T(8,128)(2,1)S(1)}, u32[]{:S(2)}, u32[]{:S(2)}) collective-permute-start(bf16[576,128]{1,0:T(8,128)(2,1)S(1)} %get-tuple-element.88), channel_id=1, source_target_pairs={{0,8},{1,9},{2,10},{3,11},{4,12},{5,13},{6,14},{7,15},{8,0},{9,1},... | collective-permute-start | bytes 442376 | tf_op jit(solution)/shard_map/ppermute | solution.py:694
  206.1 6.2 %collective-permute-start.26 = (bf16[288,128]{1,0:T(8,128)(2,1)S(1)}, bf16[288,128]{1,0:T(8,128)(2,1)S(1)}, u32[]{:S(2)}, u32[]{:S(2)}) collective-permute-start(bf16[288,128]{1,0:T(8,128)(2,1)S(1)} %add_convert_fusion.9), channel_id=1, source_target_pairs={{0,2},{1,3},{2,0},{3,1},{4,6},{5,7},{6,4},{7,5},{8,10},{9,11},{10,... | collective-permute-start | bytes 221192 | tf_op jit(solution)/shard_map/ppermute | solution.py:694
  210.8 37.5 %collective-permute-start.35 = (bf16[3,512,384]{2,1,0:T(8,128)(2,1)}, bf16[3,512,384]{2,1,0:T(8,128)(2,1)}, u32[]{:S(2)}, u32[]{:S(2)}) collective-permute-start(bf16[3,512,384]{2,1,0:T(8,128)(2,1)} %get-tuple-element.126), channel_id=1, source_target_pairs={{0,16},{16,0},{1,17},{17,1},{2,18},{18,2},{3,19},{19,3},{4,20},{20... | collective-permute-start | bytes 3538952 | tf_op jit(solution)/shard_map/ppermute | solution.py:672
  210.8 11.1 %collective-permute-start.32 = (f32[72,128]{1,0:T(8,128)S(1)}, f32[72,128]{1,0:T(8,128)S(1)}, u32[]{:S(2)}, u32[]{:S(2)}) collective-permute-start(f32[72,128]{1,0:T(8,128)S(1)} %add.276), channel_id=1, source_target_pairs={{0,1},{1,0},{2,3},{3,2},{4,5},{5,4},{6,7},{7,6},{8,9},{9,8},{10,11... | collective-permute-start | bytes 110600 | tf_op jit(solution)/shard_map/ppermute | solution.py:694
  210.9 7.7 %collective-permute-start.25 = (bf16[576,128]{1,0:T(8,128)(2,1)S(1)}, bf16[576,128]{1,0:T(8,128)(2,1)S(1)}, u32[]{:S(2)}, u32[]{:S(2)}) collective-permute-start(bf16[576,128]{1,0:T(8,128)(2,1)S(1)} %add_convert_fusion.7), channel_id=1, source_target_pairs={{0,8},{1,9},{2,10},{3,11},{4,12},{5,13},{6,14},{7,15},{8,0},{9,1},... | collective-permute-start | bytes 442376 | tf_op jit(solution)/shard_map/ppermute | solution.py:694
  221.9 26.4 %collective-permute-start.34 = (bf16[3,512,384]{2,1,0:T(8,128)(2,1)}, bf16[3,512,384]{2,1,0:T(8,128)(2,1)S(1)}, u32[]{:S(2)}, u32[]{:S(2)}) collective-permute-start(bf16[3,512,384]{2,1,0:T(8,128)(2,1)} %convert_select_fusion), channel_id=1, source_target_pairs={{0,16},{16,0},{1,17},{17,1},{2,18},{18,2},{3,19},{19,3},{4,20},{20... | collective-permute-start | bytes 3538952 | tf_op jit(solution)/shard_map/ppermute | solution.py:672
  221.9 10.7 %collective-permute-start.33 = (f32[72,128]{1,0:T(8,128)S(1)}, f32[72,128]{1,0:T(8,128)S(1)}, u32[]{:S(2)}, u32[]{:S(2)}) collective-permute-start(f32[72,128]{1,0:T(8,128)S(1)} %add.279), channel_id=1, source_target_pairs={{0,16},{16,0},{1,17},{17,1},{2,18},{18,2},{3,19},{19,3},{4,20},{20... | collective-permute-start | bytes 110600 | tf_op jit(solution)/shard_map/ppermute | solution.py:672
  222.5 9.9 %collective-permute-start.27 = (bf16[1152,128]{1,0:T(8,128)(2,1)S(1)}, bf16[1152,128]{1,0:T(8,128)(2,1)S(1)}, u32[]{:S(2)}, u32[]{:S(2)}) collective-permute-start(bf16[1152,128]{1,0:T(8,128)(2,1)S(1)} %pad_maximum_fusion.3), channel_id=1, source_target_pairs={{0,4},{1,5},{2,6},{3,7},{4,0},{5,1},{6,2},{7,3},{8,12},{9,13},{10,... | collective-permute-start | bytes 884744 | tf_op jit(solution)/shard_map/ppermute | solution.py:694
  232.5 10.4 %collective-permute-start.30 = (bf16[1152,128]{1,0:T(8,128)(2,1)S(1)}, bf16[1152,128]{1,0:T(8,128)(2,1)S(1)}, u32[]{:S(2)}, u32[]{:S(2)}) collective-permute-start(bf16[1152,128]{1,0:T(8,128)(2,1)S(1)} %pad_maximum_fusion.4), channel_id=1, source_target_pairs={{0,8},{1,9},{2,10},{3,11},{4,12},{5,13},{6,14},{7,15},{8,0},{9,1},... | collective-permute-start | bytes 884744 | tf_op jit(solution)/shard_map/ppermute | solution.py:694
  234.6 9.9 %collective-permute-start.29 = (bf16[2304,128]{1,0:T(8,128)(2,1)S(1)}, bf16[2304,128]{1,0:T(8,128)(2,1)S(1)}, u32[]{:S(2)}, u32[]{:S(2)}) collective-permute-start(bf16[2304,128]{1,0:T(8,128)(2,1)S(1)} %pad_maximum_fusion.1), channel_id=1, source_target_pairs={{0,2},{1,3},{2,0},{3,1},{4,6},{5,7},{6,4},{7,5},{8,10},{9,11},{10,... | collective-permute-start | bytes 1769480 | tf_op jit(solution)/shard_map/ppermute | solution.py:694
  244.6 16.6 %collective-permute-start.36 = (bf16[4608,128]{1,0:T(8,128)(2,1)S(1)}, bf16[4608,128]{1,0:T(8,128)(2,1)S(1)}, u32[]{:S(2)}, u32[]{:S(2)}) collective-permute-start(bf16[4608,128]{1,0:T(8,128)(2,1)S(1)} %pad_maximum_fusion.refs_0_), channel_id=1, source_target_pairs={{0,1},{1,0},{2,3},{3,2},{4,5},{5,4},{6,7},{7,6},{8,9},{9,8},{10,11... | collective-permute-start | bytes 3538952 | tf_op jit(solution)/shard_map/ppermute | solution.py:694
  245.8 15.4 %collective-permute-start.37 = (bf16[2304,128]{1,0:T(8,128)(2,1)S(1)}, bf16[2304,128]{1,0:T(8,128)(2,1)S(1)}, u32[]{:S(2)}, u32[]{:S(2)}) collective-permute-start(bf16[2304,128]{1,0:T(8,128)(2,1)S(1)} %pad_maximum_fusion.2.refs_2_), channel_id=1, source_target_pairs={{0,4},{1,5},{2,6},{3,7},{4,0},{5,1},{6,2},{7,3},{8,12},{9,13},{10,... | collective-permute-start | bytes 1769480 | tf_op jit(solution)/shard_map/ppermute | solution.py:694
  (38 other events, 484.8 us)
where the time goes:
time: 269 us; the launch traced here: 268 us
  Pallas kernels  137 us (51%)
  waiting for transfers between devices  65.5 us (24%)
  starting transfers between devices  42.5 us (16%)
  other arithmetic  16 us (6%)
  local copies, waits for them, and re-layouts  6.15 us (2%)
    pallas_call x1, Pallas kernels, layers(): call(layers_body, z.own, [SCALARS, z.row_batch, z.row_batch, z.all_rows,...  116 us
    ppermute x24, waiting for transfers between devices, partner(): return lax.ppermute(x, ('section', 'dp'), pairs)  62.1 us
    ppermute x24, starting transfers between devices, partner(): return lax.ppermute(x, ('section', 'dp'), pairs)  39.6 us
    pallas_call x1, Pallas kernels, final(): call(final_body, z.micro, [z.row, z.all_rows, by_step(z.stats), by_step(z...  10.2 us
  transfers between devices with their start and end apart: 38, of which 22 were waited for; matrix products, arithmetic and copies ran while one was open for 5% of the time, Pallas kernels for 4%

commit v1 on v0

--- a/solution.py
+++ b/solution.py
@@ -10,7 +10,7 @@
 BLOCK = 512
 SER_DEV = 4
 LANES = 128
-CHUNK = 256
+CHUNK = 512
 TILE = 256
 
 norm_epsilon = 1e-05
@@ -71,40 +71,41 @@
 
 
 def stats_body(sec_ref, x_ref, sid_ref, out_ref):
-    m = pl.num_programs(0) * sec_ref[0] + pl.program_id(0)
-    x = x_ref[0].astype(f32)
-    width = x.shape[1]
-    sid_col = column(sid_ref[pl.ds(m, 1), :])
+    own, _, width = x_ref.shape
     pieces = out_ref.shape[-1] // LANES
-    totals = jnp.sum(x, axis=1, keepdims=True)
-    centre = jnp.zeros_like(totals)
-    out_ref[0] = jnp.zeros(out_ref.shape[1:], f32)
-    for piece in range(pieces):
-        hits = series_hits(sid_col, piece)
-        count = series_of(hits, 1.0)
-        total = series_of(hits, totals)
-        centre = centre + rows_of(hits, total / (jnp.maximum(count, 1.0) * width))
-        out_ref[0, 0:1, piece * LANES : (piece + 1) * LANES] = count
-        out_ref[0, 1:2, piece * LANES : (piece + 1) * LANES] = total
-    centred = x - centre
-    squares = jnp.sum(centred * centred, axis=1, keepdims=True)
-    for piece in range(pieces):
-        hits = series_hits(sid_col, piece)
-        out_ref[0, 2:3, piece * LANES : (piece + 1) * LANES] = series_of(hits, squares)
+    out_ref[...] = jnp.zeros_like(out_ref)
+    for i in range(own):
+        x = x_ref[i].astype(f32)
+        sid_col = column(sid_ref[pl.ds(own * sec_ref[0] + i, 1), :])
+        totals = jnp.sum(x, axis=1, keepdims=True)
+        centre = jnp.zeros_like(totals)
+        for piece in range(pieces):
+            hits = series_hits(sid_col, piece)
+            count = series_of(hits, 1.0)
+            total = series_of(hits, totals)
+            centre = centre + rows_of(hits, total / (jnp.maximum(count, 1.0) * width))
+            out_ref[i, 0:1, piece * LANES : (piece + 1) * LANES] = count
+            out_ref[i, 1:2, piece * LANES : (piece + 1) * LANES] = total
+        centred = x - centre
+        squares = jnp.sum(centred * centred, axis=1, keepdims=True)
+        for piece in range(pieces):
+            hits = series_hits(sid_col, piece)
+            out_ref[i, 2:3, piece * LANES : (piece + 1) * LANES] = series_of(hits, squares)
 
 
 def merge_stats(here, there, width):
-    count_a, total_a, spread_a = here[:, 0], here[:, 1], here[:, 2]
-    count_b, total_b, spread_b = there[:, 0], there[:, 1], there[:, 2]
+    count_a, total_a, spread_a = here[:, 0:1], here[:, 1:2], here[:, 2:3]
+    count_b, total_b, spread_b = there[:, 0:1], there[:, 1:2], there[:, 2:3]
     count = count_a + count_b
     gap = total_a / (jnp.maximum(count_a, 1.0) * width) - total_b / (
         jnp.maximum(count_b, 1.0) * width
     )
     weight = count_a * count_b * width / jnp.maximum(count, 1.0)
-    spread = spread_a + spread_b + gap * gap * weight
-    rest = jnp.zeros_like(here[:, 3:])
-    return jnp.concatenate(
-        [jnp.stack([count, total_a + total_b, spread], axis=1), rest], axis=1
+    row = lax.broadcasted_iota(jnp.int32, here.shape, 1)
+    return jnp.where(
+        row == 0,
+        count,
+        jnp.where(row == 1, total_a + total_b, spread_a + spread_b + gap * gap * weight),
     )
 
 
@@ -188,9 +189,8 @@
         ).astype(bf16)
 
 
-def attention_forward(layer, hidden, gains, block, bias_ref, weights, saved):
+def attention_forward(layer, hidden, gains, block, bias, weights, saved):
     qkv_ref, prob_ref, inv_ref, mixed_ref = (ref.at[layer] for ref in saved)
-    bias_at = layer * (bias_ref.shape[0] // 2)
     rows, width = hidden.shape
     pairs = width // LANES
     tiles = rows // TILE
@@ -250,7 +250,7 @@
         following = scores_of(*order[n + 1]) if n + 1 < len(order) else None
         head = 2 * p + half
         cols = slice(t * TILE, (t + 1) * TILE)
-        gap = bias_ref[bias_at + 2 * head] - bias_ref[bias_at + 2 * head + 1]
+        gap = bias[0:1, 2 * head : 2 * head + 1] - bias[0:1, 2 * head + 1 : 2 * head + 2]
         biased = scores + block.same_ref[:, cols] * gap
         peak = jnp.max(biased, axis=0, keepdims=True)
         prob = jnp.exp(biased - peak).astype(bf16)
@@ -271,7 +271,6 @@
 
 def feed_forward(layer, middle, gains, weights):
     big_ref, down_ref = weights.big_ref.at[layer], weights.down_ref.at[layer]
-    weights.wait_feed(layer)
     width = middle.shape[1]
     hidden = down_ref.shape[0]
     feed = (middle * inverse_rms(middle) * gains).astype(bf16)
@@ -284,7 +283,7 @@
     return total.astype(bf16)
 
 
-def feed_backward(layer, middle, gains, grad_low, weights, accs):
+def feed_backward(layer, middle, gains, grad_low, weights, accs, active_ref):
     gate_acc, up_acc, down_acc, gain_acc = (acc.at[layer] for acc in accs)
     big_ref, down_ref = weights.big_ref.at[layer], weights.down_ref.at[layer]
     width = middle.shape[1]
@@ -303,6 +302,7 @@
         gated = sigmoid(gate)
         swish = gate * gated
         active = (swish * up).astype(bf16)
+        active_ref[:, at : at + CHUNK] = active
         gate_grad = (act_grad * up * (gated + swish * (1.0 - gated))).astype(bf16)
         up_grad = (act_grad * swish).astype(bf16)
         feed_grad = feed_grad + dot(gate_grad, gate_w, RIGHT_T) + dot(up_grad, up_w, RIGHT_T)
@@ -354,7 +354,10 @@
             grad_low = jnp.where(in_head(half, lane, False), grad_pair, 0.0).astype(bf16)
             tail_low = jnp.where(lane // 2 == half, tail, 0.0).astype(bf16)
             q_mine = jnp.where(in_head(half, lane, True), q_pair, 0.0).astype(bf16)
-            k_mine = jnp.where(in_head(half, row_index(rows), True), k_turned, 0.0).astype(bf16)
+            low = half * (HD // 2)
+            k_mine = jnp.concatenate(
+                [k_turned[low : low + HD // 2], k_turned[HD + low : HD + low + HD // 2]], axis=0
+            )
             heads.append(
                 (jnp.concatenate([grad_low, tail_low], axis=1), grad_low, q_mine, k_mine)
             )
@@ -389,9 +392,11 @@
         part_q = dot(k_mine, score_low)
         value_grad = part_v if value_grad is None else value_grad + part_v
         key_grad = part_k if key_grad is None else key_grad + part_k
-        query_grad[t] = part_q if half == 0 else query_grad[t] + part_q
+        query_grad[t, half] = part_q
         if half == 1:
-            back = query_grad[t].T * HD**-0.5
+            one, two = query_grad.pop((t, 0)), query_grad.pop((t, 1))
+            mid = HD // 2
+            back = jnp.concatenate([one[:mid], two[:mid], one[mid:], two[mid:]], axis=0).T * HD**-0.5
             grads_ref[cols, at : at + LANES] = turn_back(
                 back, block.cosine[cols, :], block.sine[cols, :]
             ).astype(bf16)
@@ -459,15 +464,16 @@
 
 
 def layers_body(
-    sec_ref, bias_ref, x_ref, cotangent_ref, sid_ref, item_ref, var_ref, stats_ref, table_ref,
-    gain_ref, *refs
+    sec_ref, x_ref, cotangent_ref, sid_ref, item_ref, var_ref, stats_ref, table_ref,
+    own_small_ref, other_small_ref, *refs
 ):
     own_refs, other_refs, refs = refs[:7], refs[7:14], refs[14:]
     results_ref, grad_one_ref, grad_zero_ref, series_ref, small_ref = refs[:5]
     kept_refs, sent_refs, refs = refs[5:7], refs[7:9], refs[9:]
     big_ref, down_ref, refs = refs[0], refs[1], refs[2:]
     feed_accs, attention_accs, saved, refs = refs[:4], refs[4:8], refs[8:12], refs[12:]
-    same_ref, grads_ref, hidden_ref, middle_ref, grad_ref, stage_ref, sems, stage_sems = refs
+    same_ref, grads_ref, hidden_ref, middle_ref, grad_ref, active_ref, stage_ref, *refs = refs
+    sems, stage_sems = refs
 
     i = pl.program_id(0)
     last = i == pl.num_programs(0) - 1
@@ -505,16 +511,23 @@
     hidden_ref[0] = (x - centre_rows) / scale_rows
     grad_ref[...] = cotangent_ref[0]
 
+    def small_row(layer, k):
+        return jnp.where(
+            sec_ref[0] == layer, own_small_ref[k : k + 1, :], other_small_ref[k : k + 1, :]
+        )
+
     def forward(layer, _):
         middle = attention_forward(
-            layer, hidden_ref[layer], gain_ref[layer, 0:1, :], block, bias_ref, weights, saved
+            layer, hidden_ref[layer], small_row(layer, 0), block, small_row(layer, 2), weights,
+            saved,
         )
         middle_ref[layer] = middle
-        result = feed_forward(layer, middle, gain_ref[layer, 1:2, :], weights)
-        results_ref[layer, 0] = result
+        weights.wait_feed(layer)
 
         @pl.when(layer == 0)
         def _():
+            result = feed_forward(layer, middle_ref[0], small_row(layer, 1), weights)
+            results_ref[0, 0] = result
             hidden_ref[1] = result.astype(f32)
 
     def send(layer):
@@ -534,10 +547,17 @@
     def backward(step, _):
         layer = 1 - step
         middle_grad = feed_backward(
-            layer, middle_ref[layer], gain_ref[layer, 1:2, :], grad_ref[...], weights, feed_accs
+            layer, middle_ref[layer], small_row(layer, 1), grad_ref[...], weights, feed_accs,
+            active_ref,
         )
+
+        @pl.when(layer == 1)
+        def _():
+            total = middle_ref[1] + dot(active_ref[...], weights.down_ref[1])
+            results_ref[1, 0] = total.astype(bf16)
+
         hidden_grad = attention_backward(
-            layer, middle_grad, hidden_ref[layer], gain_ref[layer, 0:1, :], block, weights,
+            layer, middle_grad, hidden_ref[layer], small_row(layer, 0), block, weights,
             saved, grads_ref, attention_accs,
         )
         grad_ref[...] = hidden_grad.astype(bf16)
@@ -712,6 +732,13 @@
     return (parts, *more)
 
 
+def add_whole(parts, orders, k, count, *more):
+    parts, more = lax.optimization_barrier((parts, more))
+    got = [partner(part, *order[k], count) for part, order in zip(parts, orders)]
+    parts = [(a.astype(f32) + b.astype(f32)).astype(bf16) for a, b in zip(parts, got)]
+    return (parts, *more)
+
+
 def double(parts, orders, k, section, index, count):
     parts = lax.optimization_barrier(parts)
     result = []
@@ -794,12 +821,14 @@
 
 def series_stats(z, sec, inputs, series_id):
     return call(
-        stats_body, z.own, [z.row_batch, z.all_rows], by_step(z.stats), shape(z.own, *z.stats),
+        stats_body, 1,
+        [pl.BlockSpec((z.own, z.rows, z.width), lambda i, s: (s[0], 0, 0)), z.all_rows],
+        whole_block((z.own,) + z.stats), shape(z.own, *z.stats),
         [], 10**7, "series_stats",
     )(sec, inputs, series_id)
 
 
-def layers(z, sec, bias, inputs, cotangent, series_id, item, variate, stats, gains, own, other):
+def layers(z, sec, inputs, cotangent, series_id, item, variate, stats, small, own, other):
     table = rotary_table(z.rows)
     rows, width, hidden = z.rows, z.width, z.hidden
     parts = [
@@ -812,8 +841,8 @@
 
     return call(
         layers_body, z.own,
-        [SCALARS, z.row_batch, z.row_batch, z.all_rows, z.all_rows, z.all_rows, by_step(z.stats),
-         whole_block(table.shape), whole_block((2, 8, width))] + [HBM] * 14,
+        [z.row_batch, z.row_batch, z.all_rows, z.all_rows, z.all_rows, by_step(z.stats),
+         whole_block(table.shape), whole_block((8, width)), whole_block((8, width))] + [HBM] * 14,
         [pl.BlockSpec((2, 1, rows, width), lambda i, *_: (0, i, 0, 0)), z.row, z.row,
          by_step(z.stats), whole_block((48, LANES))] + [HBM] * 4,
         [shape(2, z.own, rows, width, dtype=bf16), z.low_shape, z.row_shape,
@@ -825,11 +854,12 @@
          both(rows, width), both(rows, width),
          pltpu.VMEM((rows, rows), f32), pltpu.VMEM((rows, 3 * width), bf16),
          both(rows, width), both(rows, width), pltpu.VMEM((rows, width), bf16),
+         pltpu.VMEM((rows, hidden), bf16),
          both(8 * width, LANES, dtype=bf16),
          pltpu.SemaphoreType.DMA((2, 7)), pltpu.SemaphoreType.DMA((2,))],
         12 * z.flops, "layers",
-    )(sec, bias, inputs, cotangent, series_id, item, variate, stats, jnp.asarray(table),
-      gains, *own, *other)
+    )(sec, inputs, cotangent, series_id, item, variate, stats, jnp.asarray(table),
+      *small, *own, *other)
 
 
 def final(z, sec, inputs, series_id, stats, series, own_first, own_second, other_grad,
@@ -880,10 +910,6 @@
     z = Sizes(inputs, heads, down_weight.shape[1], count)
     width = z.width
 
-    stats = series_stats(z, sec, inputs, series_id)
-    for step in exchange_steps(count)[0]:
-        stats = merge_stats(stats, partner(stats, step, step, count), width)
-
     own_small = jnp.concatenate(
         [
             attention_gain,
@@ -901,18 +927,17 @@
         )
     )
     other = tuple(swapped(w) for w in own)
-    gains = (
-        jnp.where(on_first, own_small, other_small),
-        jnp.where(on_first, other_small, own_small),
-    )
-    gains = jnp.stack(gains)
-    bias = gains[:, 2, : 2 * heads].reshape(-1)
+    stats = series_stats(z, sec, inputs, series_id)
+    steps = exchange_steps(count)[0]
+    for k, step in enumerate(steps):
+        if k == len(steps) - 1:
+            stats, other, other_small = lax.optimization_barrier((stats, other, other_small))
+        stats = merge_stats(stats, partner(stats, step, step, count), width)
 
     results, grad_one, standard_grad, series_sums, small_sums, *packs = layers(
-        z, sec, bias, inputs, cotangent, series_id, item_offset, variate_offset, stats, gains,
-        own, other,
-    )
-    result_one, result_two = results[0], results[1]
+        z, sec, inputs, cotangent, series_id, item_offset, variate_offset, stats,
+        (own_small, other_small), own, other,
+    )
 
     parts = [
         (k.astype(f32) + swapped(t).astype(f32)).astype(bf16)
@@ -927,36 +952,43 @@
     small = jnp.concatenate(
         [series_sums.reshape(-1, LANES), small_sums], axis=0
     )
-    for k in range(rounds):
-        parts, small = halve(parts, orders, k, section, index, count, small)
-        small = small + partner(small, bits[rounds - 1 - k], bits[rounds - 1 - k], count)
-    other_sums = swapped(small)
+    parts = halve(parts, orders, 0, section, index, count)[0]
+    for k in range(1, rounds):
+        if k < rounds - 1:
+            parts, small = halve(parts, orders, k, section, index, count, small)
+        else:
+            parts, small = add_whole(parts, orders, k, count, small)
+        small = small + partner(small, bits[rounds - k], bits[rounds - k], count)
+    for k in reversed(range(1, rounds - 1)):
+        if k == rounds - 2:
+            parts, small = lax.optimization_barrier((parts, small))
+            small = small + partner(small, bits[0], bits[0], count)
+        if k == 1:
+            parts, small, results, grad_one, standard_grad, stats = lax.optimization_barrier(
+                (parts, small, results, grad_one, standard_grad, stats)
+            )
+            result_one, result_two = results[0], results[1]
+            own_out = jnp.where(on_first, result_one, result_two)
+            other_out = swapped(jnp.where(on_first, result_two, result_one))
+            other_grad = swapped(jnp.where(on_first, grad_one, standard_grad.astype(bf16)))
+            other_sums = swapped(small)
+            other_stats = swapped(stats)
+        parts = double(parts, orders, k, section, index, count)
     mine = small[:series_rows].reshape((z.own,) + z.stats)
     theirs = other_sums[:series_rows].reshape((z.own,) + z.stats)
     series_all = jnp.where(
         on_first, jnp.concatenate([mine, theirs]), jnp.concatenate([theirs, mine])
     )
     small = small[series_rows:] + other_sums[series_rows:]
-    other_stats = swapped(stats)
     stats_all = jnp.where(
         on_first, jnp.concatenate([stats, other_stats]), jnp.concatenate([other_stats, stats])
     )
-
-    own_out = jnp.where(on_first, result_one, result_two)
-    other_out = swapped(jnp.where(on_first, result_two, result_one))
-    other_grad = swapped(jnp.where(on_first, grad_one, standard_grad.astype(bf16)))
-
-    for k in reversed(range(1, rounds)):
-        parts = double(parts, orders, k, section, index, count)
     sec_late, parts = lax.optimization_barrier((sec, parts))
     input_grads, section_output = final(
         z, sec_late, inputs, series_id, stats_all, series_all, standard_grad, grad_one, other_grad,
         own_out, other_out,
     )
     others = [partner(p, *o[0], count) for p, o in zip(parts, orders)]
-    parts, input_grads, section_output = lax.optimization_barrier(
-        (parts, input_grads, section_output)
-    )
     last_bits = jnp.stack([place(o[0], section, index) for o in orders]).astype(jnp.int32)
 
     vmem = pl.BlockSpec(memory_space=pltpu.VMEM)

time: 269 us -> 258 us (0.959)
  starting transfers between devices: 42.5 us -> 32.6 us
  Pallas kernels: 137 us -> 134 us
    ppermute x24 -> x22, starting transfers between devices: 39.6 us -> 29.9 us  [partner(): return lax.ppermute(x, ('section', 'dp'), pairs)]
    pallas_call x2, Pallas kernels: 120 us -> 117 us  [the longest x1 113 us: layers(): call(layers_body, z.own, [z.row_batch, z.row_batch, z.all_rows, z.all_row...]
    ppermute x14, waiting for transfers between devices: 3.33 us -> 6.37 us  [swapped(): return lax.ppermute(x, 'section', [(0, 1), (1, 0)])]
    ppermute x24 -> x22, waiting for transfers between devices: 62.1 us -> 60.8 us  [partner(): return lax.ppermute(x, ('section', 'dp'), pairs)]
  transfers between devices with their start and end apart: 38 -> 36, of which waited for: 22 -> 21; matrix products, arithmetic and copies ran while one was open for 5% -> 5% of each run, Pallas kernels for 4% -> 5%
where the time goes in v1:
time: 258 us; the launch traced here: 257 us
  Pallas kernels  134 us (52%)
  waiting for transfers between devices  67.2 us (26%)
  starting transfers between devices  32.6 us (13%)
  other arithmetic  15.2 us (6%)
  local copies, waits for them, and re-layouts  6.76 us (3%)
    pallas_call x1, Pallas kernels, layers(): call(layers_body, z.own, [z.row_batch, z.row_batch, z.all_rows, z.all_row...  113 us
    ppermute x22, waiting for transfers between devices, partner(): return lax.ppermute(x, ('section', 'dp'), pairs)  60.8 us
    ppermute x22, starting transfers between devices, partner(): return lax.ppermute(x, ('section', 'dp'), pairs)  29.9 us
    pallas_call x1, Pallas kernels, final(): call(final_body, z.micro, [z.row, z.all_rows, by_step(z.stats), by_step(z...  10.2 us
    ppermute x14, waiting for transfers between devices, swapped(): return lax.ppermute(x, 'section', [(0, 1), (1, 0)])  6.37 us
  transfers between devices with their start and end apart: 36, of which 21 were waited for; matrix products, arithmetic and copies ran while one was open for 5% of the time, Pallas kernels for 5%

profile of v1, /device:TPU:0, one launch (start us, length us, event | category | flops | bytes accessed | tf_op | source)
XLA Modules:
  0.0 256.7 jit_solution(17037750107129339237)
XLA Ops:
  0.7 3.4 %series_stats.1 = f32[3,8,128]{2,1,0:T(8,128)} custom-call(s32[1]{0:T(128)} %bitcast.sec_ref, bf16[6,512,384]{2,1,0:T(8,128)(2,1)} %x_ref.5, s32[6,512]{1,0:T(8,128)} %sid_ref.5), custom_call_target="tpu_custom_call" | custom-call | flops 10000000 | bytes 4194304 | tf_op jit(solution)/shard_map/series_stats/pallas_call | solution.py:823
  4.1 2.9 %collective-permute-start = (f32[3,8,128]{2,1,0:T(8,128)}, f32[3,8,128]{2,1,0:T(8,128)S(1)}, u32[]{:S(2)}, u32[]{:S(2)}) collective-permute-start(f32[3,8,128]{2,1,0:T(8,128)} %series_stats.1), channel_id=1, source_target_pairs={{0,1},{1,0},{2,3},{3,2},{4,5},{5,4},{6,7},{7,6},{8,9},{9,8},{10,11... | collective-permute-start | bytes 36872 | tf_op jit(solution)/shard_map/ppermute | solution.py:714
  9.9 2.1 collective-permute-start.1
  13.7 2.1 collective-permute-start.2
  21.1 3.1 %collective-permute-start.11 = (f32[3,8,128]{2,1,0:T(8,128)S(1)}, f32[3,8,128]{2,1,0:T(8,128)S(1)}, u32[]{:S(2)}, u32[]{:S(2)}) collective-permute-start(f32[3,8,128]{2,1,0:T(8,128)S(1)} %select_select_fusion.1), channel_id=1, source_target_pairs={{0,8},{1,9},{2,10},{3,11},{4,12},{5,13},{6,14},{7,15},{8,0},{9,1},... | collective-permute-start | bytes 36872 | tf_op jit(solution)/shard_map/ppermute | solution.py:714
  26.7 113.5 %layers.1 = (bf16[2,3,512,384]{3,2,1,0:T(8,128)(2,1)}, bf16[3,512,384]{2,1,0:T(8,128)(2,1)}, f32[3,512,384]{2,1,0:T(8,128)}, f32[3,8,128]{2,1,0:T(8,128)}, f32[4...) custom-call(s32[1]{0:T(128)} %bitcast.sec_ref, ...), custom_call_target="tpu_custom_call" | custom-call | flops 65229815808 | bytes 4194304 | tf_op jit(solution)/shard_map/layers/pallas_call | solution.py:842
  140.8 2.5 collective-permute-done.13
  147.6 2.0 collective-permute-start.15
  152.4 11.4 %collective-permute-done.15 = bf16[2304,128]{1,0:T(8,128)(2,1)S(1)} collective-permute-done((bf16[2304,128]{1,0:T(8,128)(2,1)}, bf16[2304,128]{1,0:T(8,128)(2,1)S(1)}, u32[]{:S(2)}, u32[]{:S(2)}) %collective-permute-start.15) | collective-permute-done | bytes 589856 | tf_op jit(solution)/shard_map/ppermute | solution.py:714
  164.0 1.9 collective-permute-done.14
  167.5 2.7 %collective-permute-start.17 = (bf16[1152,128]{1,0:T(8,128)(2,1)S(1)}, bf16[1152,128]{1,0:T(8,128)(2,1)S(1)}, u32[]{:S(2)}, u32[]{:S(2)}) collective-permute-start(bf16[1152,128]{1,0:T(8,128)(2,1)S(1)} %get-tuple-element.98), channel_id=1, source_target_pairs={{0,8},{1,9},{2,10},{3,11},{4,12},{5,13},{6,14},{7,15},{8,0},{9,1},... | collective-permute-start | bytes 884744 | tf_op jit(solution)/shard_map/ppermute | solution.py:714
  172.1 7.7 %collective-permute-done.18 = f32[72,128]{1,0:T(8,128)S(1)} collective-permute-done((f32[72,128]{1,0:T(8,128)}, f32[72,128]{1,0:T(8,128)S(1)}, u32[]{:S(2)}, u32[]{:S(2)}) %collective-permute-start.18) | collective-permute-done | bytes 36896 | tf_op jit(solution)/shard_map/ppermute | solution.py:714
  182.6 2.0 collective-permute-start.21
  184.6 8.2 %collective-permute-done.21 = f32[72,128]{1,0:T(8,128)S(1)} collective-permute-done((f32[72,128]{1,0:T(8,128)S(1)}, f32[72,128]{1,0:T(8,128)S(1)}, u32[]{:S(2)}, u32[]{:S(2)}) %collective-permute-start.21) | collective-permute-done | bytes 36896 | tf_op jit(solution)/shard_map/ppermute | solution.py:714
  195.0 3.5 %collective-permute-done.24 = f32[72,128]{1,0:T(8,128)S(1)} collective-permute-done((f32[72,128]{1,0:T(8,128)S(1)}, f32[72,128]{1,0:T(8,128)S(1)}, u32[]{:S(2)}, u32[]{:S(2)}) %collective-permute-start.24) | collective-permute-done | bytes 36896 | tf_op jit(solution)/shard_map/ppermute | solution.py:714
  198.6 10.9 %collective-permute-done.22 = bf16[1152,128]{1,0:T(8,128)(2,1)S(1)} collective-permute-done((bf16[1152,128]{1,0:T(8,128)(2,1)S(1)}, bf16[1152,128]{1,0:T(8,128)(2,1)S(1)}, u32[]{:S(2)}, u32[]{:S(2)}) %collective-permute-start.22) | collective-permute-done | bytes 294944 | tf_op jit(solution)/shard_map/ppermute | solution.py:714
  209.7 2.0 collective-permute-start.27
  212.4 2.8 %collective-permute-done.27 = f32[72,128]{1,0:T(8,128)S(1)} collective-permute-done((f32[72,128]{1,0:T(8,128)S(1)}, f32[72,128]{1,0:T(8,128)S(1)}, u32[]{:S(2)}, u32[]{:S(2)}) %collective-permute-start.27) | collective-permute-done | bytes 36896 | tf_op jit(solution)/shard_map/ppermute | solution.py:714
  215.3 3.7 %collective-permute-done.25 = bf16[1152,128]{1,0:T(8,128)(2,1)S(1)} collective-permute-done((bf16[1152,128]{1,0:T(8,128)(2,1)S(1)}, bf16[1152,128]{1,0:T(8,128)(2,1)S(1)}, u32[]{:S(2)}, u32[]{:S(2)}) %collective-permute-start.25) | collective-permute-done | bytes 294944 | tf_op jit(solution)/shard_map/ppermute | solution.py:714
  228.2 2.3 collective-permute-done.29
  233.9 2.0 collective-permute-start.35
  237.0 10.2 %final.1 = (f32[6,512,384]{2,1,0:T(8,128)}, bf16[6,512,384]{2,1,0:T(8,128)(2,1)}) custom-call(s32[1]{0:T(128)} %bitcast.sec_ref, bf16[6,512,384]{2,1,0:T(8,128)(2,1)} %x_ref.5, s32[6,512]{1,0:T(8,128)} %sid_ref.5, f32[6,8,128]{2,1,0:T(8,128)} %maximum_select_fusion.stats_ref, f32[6,8,128]{2,1,0:T(8,128)} %maximum_select_fusion.1.series_ref, ...), custom_call_target="tpu_custom_call" | custom-call | flops 10000000000 | bytes 4194304 | tf_op jit(solution)/shard_map/final/pallas_call | solution.py:877
  247.2 2.4 collective-permute-done.35.refs_3_
  251.4 5.1 %unpack.1 = (f32[384,1024]{1,0:T(8,128)}, f32[384,1024]{1,0:T(8,128)}, f32[1024,384]{1,0:T(8,128)}, f32[384,384]{1,0:T(8,128)}, f32[384,384]{1,0:T(8,128)}, /*index=5*/f32[384,384]{1,0:T(8,128)}, f32[384,384]{1,0:T(8,128)}) custom-call(s32[2]{0:T(128)} %pad_add_fusion.bit_ref, bf16[4608,128]{1,0:T(8,128)(2,1)} %copy-done, bf16[4608,128]{1,0:T(8,128)(2,1)} %copy-done.6, ...), custom_call_target="tpu_custom_call" | custom-call | tf_op jit(solution)/shard_map/unpack/pallas_call | solution.py:997
  (168 shorter events, 45.1 us)
Async XLA Ops:
  11.9 9.1 %collective-permute-start.7 = (bf16[384,1024]{1,0:T(8,128)(2,1)S(1)}, bf16[384,1024]{1,0:T(8,128)(2,1)S(1)}, u32[]{:S(2)}, u32[]{:S(2)}) collective-permute-start(bf16[384,1024]{1,0:T(8,128)(2,1)S(1)} %bitcast.80), channel_id=1, source_target_pairs={{0,16},{16,0},{1,17},{17,1},{2,18},{18,2},{3,19},{19,3},{4,20},{20... | collective-permute-start | bytes 2359304 | tf_op jit(solution)/shard_map/ppermute | solution.py:692
  12.4 8.6 %collective-permute-start.8 = (bf16[384,1024]{1,0:T(8,128)(2,1)S(1)}, bf16[384,1024]{1,0:T(8,128)(2,1)S(1)}, u32[]{:S(2)}, u32[]{:S(2)}) collective-permute-start(bf16[384,1024]{1,0:T(8,128)(2,1)S(1)} %bitcast.82), channel_id=1, source_target_pairs={{0,16},{16,0},{1,17},{17,1},{2,18},{18,2},{3,19},{19,3},{4,20},{20... | collective-permute-start | bytes 2359304 | tf_op jit(solution)/shard_map/ppermute | solution.py:692
  12.5 8.6 %collective-permute-start.9 = (bf16[1024,384]{1,0:T(8,128)(2,1)S(1)}, bf16[1024,384]{1,0:T(8,128)(2,1)S(1)}, u32[]{:S(2)}, u32[]{:S(2)}) collective-permute-start(bf16[1024,384]{1,0:T(8,128)(2,1)S(1)} %bitcast.84), channel_id=1, source_target_pairs={{0,16},{16,0},{1,17},{17,1},{2,18},{18,2},{3,19},{19,3},{4,20},{20... | collective-permute-start | bytes 2359304 | tf_op jit(solution)/shard_map/ppermute | solution.py:692
  140.3 6.4 %collective-permute-start.12 = (bf16[9216,128]{1,0:T(8,128)(2,1)}, bf16[9216,128]{1,0:T(8,128)(2,1)S(1)}, u32[]{:S(2)}, u32[]{:S(2)}) collective-permute-start(bf16[9216,128]{1,0:T(8,128)(2,1)} %get-tuple-element.86), channel_id=1, source_target_pairs={{0,16},{16,0},{1,17},{17,1},{2,18},{18,2},{3,19},{19,3},{4,20},{20... | collective-permute-start | bytes 7077896 | tf_op jit(solution)/shard_map/ppermute | solution.py:692
  147.6 16.2 %collective-permute-start.15 = (bf16[2304,128]{1,0:T(8,128)(2,1)}, bf16[2304,128]{1,0:T(8,128)(2,1)S(1)}, u32[]{:S(2)}, u32[]{:S(2)}) collective-permute-start(bf16[2304,128]{1,0:T(8,128)(2,1)} %get-tuple-element.92), channel_id=1, source_target_pairs={{0,4},{1,5},{2,6},{3,7},{4,0},{5,1},{6,2},{7,3},{8,12},{9,13},{10,... | collective-permute-start | bytes 1769480 | tf_op jit(solution)/shard_map/ppermute | solution.py:714
  149.6 16.3 %collective-permute-start.14 = (bf16[4608,128]{1,0:T(8,128)(2,1)S(1)}, bf16[4608,128]{1,0:T(8,128)(2,1)}, u32[]{:S(2)}, u32[]{:S(2)}) collective-permute-start(bf16[4608,128]{1,0:T(8,128)(2,1)S(1)} %get-tuple-element.90), channel_id=1, source_target_pairs={{0,1},{1,0},{2,3},{3,2},{4,5},{5,4},{6,7},{7,6},{8,9},{9,8},{10,11... | collective-permute-start | bytes 3538952 | tf_op jit(solution)/shard_map/ppermute | solution.py:714
  167.5 13.0 %collective-permute-start.17 = (bf16[1152,128]{1,0:T(8,128)(2,1)S(1)}, bf16[1152,128]{1,0:T(8,128)(2,1)S(1)}, u32[]{:S(2)}, u32[]{:S(2)}) collective-permute-start(bf16[1152,128]{1,0:T(8,128)(2,1)S(1)} %get-tuple-element.98), channel_id=1, source_target_pairs={{0,8},{1,9},{2,10},{3,11},{4,12},{5,13},{6,14},{7,15},{8,0},{9,1},... | collective-permute-start | bytes 884744 | tf_op jit(solution)/shard_map/ppermute | solution.py:714
  170.2 9.5 %collective-permute-start.18 = (f32[72,128]{1,0:T(8,128)}, f32[72,128]{1,0:T(8,128)S(1)}, u32[]{:S(2)}, u32[]{:S(2)}) collective-permute-start(f32[72,128]{1,0:T(8,128)} %pad_maximum_fusion.4), channel_id=1, source_target_pairs={{0,8},{1,9},{2,10},{3,11},{4,12},{5,13},{6,14},{7,15},{8,0},{9,1},... | collective-permute-start | bytes 110600 | tf_op jit(solution)/shard_map/ppermute | solution.py:714
  170.5 10.1 %collective-permute-start.16 = (bf16[2304,128]{1,0:T(8,128)(2,1)S(1)}, bf16[2304,128]{1,0:T(8,128)(2,1)S(1)}, u32[]{:S(2)}, u32[]{:S(2)}) collective-permute-start(bf16[2304,128]{1,0:T(8,128)(2,1)S(1)} %get-tuple-element.96), channel_id=1, source_target_pairs={{0,2},{1,3},{2,0},{3,1},{4,6},{5,7},{6,4},{7,5},{8,10},{9,11},{10,... | collective-permute-start | bytes 1769480 | tf_op jit(solution)/shard_map/ppermute | solution.py:714
  180.9 11.9 %collective-permute-start.20 = (bf16[576,128]{1,0:T(8,128)(2,1)S(1)}, bf16[576,128]{1,0:T(8,128)(2,1)S(1)}, u32[]{:S(2)}, u32[]{:S(2)}) collective-permute-start(bf16[576,128]{1,0:T(8,128)(2,1)S(1)} %get-tuple-element.103), channel_id=1, source_target_pairs={{0,1},{1,0},{2,3},{3,2},{4,5},{5,4},{6,7},{7,6},{8,9},{9,8},{10,11... | collective-permute-start | bytes 442376 | tf_op jit(solution)/shard_map/ppermute | solution.py:714
  182.6 10.2 %collective-permute-start.19 = (bf16[1152,128]{1,0:T(8,128)(2,1)S(1)}, bf16[1152,128]{1,0:T(8,128)(2,1)S(1)}, u32[]{:S(2)}, u32[]{:S(2)}) collective-permute-start(bf16[1152,128]{1,0:T(8,128)(2,1)S(1)} %get-tuple-element.101), channel_id=1, source_target_pairs={{0,4},{1,5},{2,6},{3,7},{4,0},{5,1},{6,2},{7,3},{8,12},{9,13},{10,... | collective-permute-start | bytes 884744 | tf_op jit(solution)/shard_map/ppermute | solution.py:714
  182.6 10.2 %collective-permute-start.21 = (f32[72,128]{1,0:T(8,128)S(1)}, f32[72,128]{1,0:T(8,128)S(1)}, u32[]{:S(2)}, u32[]{:S(2)}) collective-permute-start(f32[72,128]{1,0:T(8,128)S(1)} %add.196), channel_id=1, source_target_pairs={{0,4},{1,5},{2,6},{3,7},{4,0},{5,1},{6,2},{7,3},{8,12},{9,13},{10,... | collective-permute-start | bytes 110600 | tf_op jit(solution)/shard_map/ppermute | solution.py:714
  193.0 5.6 %collective-permute-start.23 = (bf16[576,128]{1,0:T(8,128)(2,1)S(1)}, bf16[576,128]{1,0:T(8,128)(2,1)S(1)}, u32[]{:S(2)}, u32[]{:S(2)}) collective-permute-start(bf16[576,128]{1,0:T(8,128)(2,1)S(1)} %add_convert_fusion.9), channel_id=1, source_target_pairs={{0,2},{1,3},{2,0},{3,1},{4,6},{5,7},{6,4},{7,5},{8,10},{9,11},{10,... | collective-permute-start | bytes 442376 | tf_op jit(solution)/shard_map/ppermute | solution.py:714
  194.3 15.2 %collective-permute-start.22 = (bf16[1152,128]{1,0:T(8,128)(2,1)S(1)}, bf16[1152,128]{1,0:T(8,128)(2,1)S(1)}, u32[]{:S(2)}, u32[]{:S(2)}) collective-permute-start(bf16[1152,128]{1,0:T(8,128)(2,1)S(1)} %add_convert_fusion.6), channel_id=1, source_target_pairs={{0,8},{1,9},{2,10},{3,11},{4,12},{5,13},{6,14},{7,15},{8,0},{9,1},... | collective-permute-start | bytes 884744 | tf_op jit(solution)/shard_map/ppermute | solution.py:714
  209.6 5.6 %collective-permute-start.26 = (bf16[576,128]{1,0:T(8,128)(2,1)S(1)}, bf16[576,128]{1,0:T(8,128)(2,1)S(1)}, u32[]{:S(2)}, u32[]{:S(2)}) collective-permute-start(bf16[576,128]{1,0:T(8,128)(2,1)S(1)} %add_convert_fusion.8), channel_id=1, source_target_pairs={{0,1},{1,0},{2,3},{3,2},{4,5},{5,4},{6,7},{7,6},{8,9},{9,8},{10,11... | collective-permute-start | bytes 442376 | tf_op jit(solution)/shard_map/ppermute | solution.py:714
  212.3 6.7 %collective-permute-start.25 = (bf16[1152,128]{1,0:T(8,128)(2,1)S(1)}, bf16[1152,128]{1,0:T(8,128)(2,1)S(1)}, u32[]{:S(2)}, u32[]{:S(2)}) collective-permute-start(bf16[1152,128]{1,0:T(8,128)(2,1)S(1)} %add_convert_fusion.5), channel_id=1, source_target_pairs={{0,4},{1,5},{2,6},{3,7},{4,0},{5,1},{6,2},{7,3},{8,12},{9,13},{10,... | collective-permute-start | bytes 884744 | tf_op jit(solution)/shard_map/ppermute | solution.py:714
  219.1 6.5 %collective-permute-start.31 = (f32[72,128]{1,0:T(8,128)S(1)}, f32[72,128]{1,0:T(8,128)S(1)}, u32[]{:S(2)}, u32[]{:S(2)}) collective-permute-start(f32[72,128]{1,0:T(8,128)S(1)} %add.203), channel_id=1, source_target_pairs={{0,16},{16,0},{1,17},{17,1},{2,18},{18,2},{3,19},{19,3},{4,20},{20... | collective-permute-start | bytes 110600 | tf_op jit(solution)/shard_map/ppermute | solution.py:692
  219.2 5.8 %collective-permute-start.30 = (f32[3,8,128]{2,1,0:T(8,128)S(1)}, f32[3,8,128]{2,1,0:T(8,128)S(1)}, u32[]{:S(2)}, u32[]{:S(2)}) collective-permute-start(f32[3,8,128]{2,1,0:T(8,128)S(1)} %copy-done.8), channel_id=1, source_target_pairs={{0,16},{16,0},{1,17},{17,1},{2,18},{18,2},{3,19},{19,3},{4,20},{20... | collective-permute-start | bytes 36872 | tf_op jit(solution)/shard_map/ppermute | solution.py:692
  219.7 10.8 %collective-permute-start.29 = (bf16[1152,128]{1,0:T(8,128)(2,1)S(1)}, bf16[1152,128]{1,0:T(8,128)(2,1)S(1)}, u32[]{:S(2)}, u32[]{:S(2)}) collective-permute-start(bf16[1152,128]{1,0:T(8,128)(2,1)S(1)} %pad_maximum_fusion.3), channel_id=1, source_target_pairs={{0,8},{1,9},{2,10},{3,11},{4,12},{5,13},{6,14},{7,15},{8,0},{9,1},... | collective-permute-start | bytes 884744 | tf_op jit(solution)/shard_map/ppermute | solution.py:714
  221.2 10.0 %collective-permute-start.28 = (bf16[2304,128]{1,0:T(8,128)(2,1)S(1)}, bf16[2304,128]{1,0:T(8,128)(2,1)}, u32[]{:S(2)}, u32[]{:S(2)}) collective-permute-start(bf16[2304,128]{1,0:T(8,128)(2,1)S(1)} %pad_maximum_fusion.1), channel_id=1, source_target_pairs={{0,2},{1,3},{2,0},{3,1},{4,6},{5,7},{6,4},{7,5},{8,10},{9,11},{10,... | collective-permute-start | bytes 1769480 | tf_op jit(solution)/shard_map/ppermute | solution.py:714
  222.9 13.1 %collective-permute-start.33 = (bf16[3,512,384]{2,1,0:T(8,128)(2,1)}, bf16[3,512,384]{2,1,0:T(8,128)(2,1)}, u32[]{:S(2)}, u32[]{:S(2)}) collective-permute-start(bf16[3,512,384]{2,1,0:T(8,128)(2,1)} %get-tuple-element.148), channel_id=1, source_target_pairs={{0,16},{16,0},{1,17},{17,1},{2,18},{18,2},{3,19},{19,3},{4,20},{20... | collective-permute-start | bytes 3538952 | tf_op jit(solution)/shard_map/ppermute | solution.py:692
  225.0 11.0 %collective-permute-start.32 = (bf16[3,512,384]{2,1,0:T(8,128)(2,1)}, bf16[3,512,384]{2,1,0:T(8,128)(2,1)S(1)}, u32[]{:S(2)}, u32[]{:S(2)}) collective-permute-start(bf16[3,512,384]{2,1,0:T(8,128)(2,1)} %convert_select_fusion), channel_id=1, source_target_pairs={{0,16},{16,0},{1,17},{17,1},{2,18},{18,2},{3,19},{19,3},{4,20},{20... | collective-permute-start | bytes 3538952 | tf_op jit(solution)/shard_map/ppermute | solution.py:692
  232.4 17.2 %collective-permute-start.34 = (bf16[4608,128]{1,0:T(8,128)(2,1)S(1)}, bf16[4608,128]{1,0:T(8,128)(2,1)S(1)}, u32[]{:S(2)}, u32[]{:S(2)}) collective-permute-start(bf16[4608,128]{1,0:T(8,128)(2,1)S(1)} %pad_maximum_fusion.refs_0_), channel_id=1, source_target_pairs={{0,1},{1,0},{2,3},{3,2},{4,5},{5,4},{6,7},{7,6},{8,9},{9,8},{10,11... | collective-permute-start | bytes 3538952 | tf_op jit(solution)/shard_map/ppermute | solution.py:714
  233.9 15.6 %collective-permute-start.35 = (bf16[2304,128]{1,0:T(8,128)(2,1)S(1)}, bf16[2304,128]{1,0:T(8,128)(2,1)S(1)}, u32[]{:S(2)}, u32[]{:S(2)}) collective-permute-start(bf16[2304,128]{1,0:T(8,128)(2,1)S(1)} %pad_maximum_fusion.2.refs_2_), channel_id=1, source_target_pairs={{0,4},{1,5},{2,6},{3,7},{4,0},{5,1},{6,2},{7,3},{8,12},{9,13},{10,... | collective-permute-start | bytes 1769480 | tf_op jit(solution)/shard_map/ppermute | solution.py:714
  (39 other events, 210.1 us)

commit v2 on v1

--- a/solution.py
+++ b/solution.py
@@ -1,3 +1,5 @@
+import functools
+
 import jax
 import jax.numpy as jnp
 import numpy as np
@@ -637,44 +639,53 @@
         out_ref[0] = grad
 
 
-class Halves:
-    def __init__(self, own_ref, got_ref, bit):
-        self.own_ref, self.got_ref, self.bit = own_ref, got_ref, bit
-        self.half = own_ref.shape[0]
-        self.at = 0
-
-    def rows(self, start, count, low):
-        own = self.own_ref[start : start + count, :]
-        got = self.got_ref[start : start + count, :]
-        return jnp.where((self.bit == 0) == low, own, got).astype(f32)
-
-    def take(self, out_ref, col, count):
-        done = 0
-        while done < count:
-            low = self.at < self.half
-            room = min(count - done, (self.half if low else 2 * self.half) - self.at)
-            out_ref[done : done + room, col : col + LANES] = self.rows(
-                self.at - (0 if low else self.half), room, low
+def unpack_body(held, count, bit_ref, feed_ref, attention_ref, *refs):
+    refs = refs[count:]
+    gate, up, down, query, key, value, out = refs[:7]
+    gate_at, up_at, down_at, one_at, two_at, sems = refs[7:]
+    half_up = up_at.shape[1]
+
+    def leave(k, source_ref, at, scratch_ref, target_ref):
+        rows = scratch_ref.shape[0]
+        for col in range(0, scratch_ref.shape[1], LANES):
+            scratch_ref[:, col : col + LANES] = source_ref[at : at + rows, :].astype(f32)
+            at += rows
+        copy = pltpu.make_async_copy(scratch_ref, target_ref, sems.at[k])
+        copy.start()
+        return copy
+
+    gate_rows = gate_at.shape[0] * gate_at.shape[1] // LANES
+    up_rows = up_at.shape[0] * half_up // LANES
+    one_rows = one_at.shape[0] * one_at.shape[1] // LANES
+
+    def feed(low):
+        if low:
+            return [
+                leave(0, feed_ref, 0, gate_at, gate),
+                leave(1, feed_ref, gate_rows, up_at, up.at[:, pl.ds(0, half_up)]),
+            ]
+        return [
+            leave(0, feed_ref, up_rows, down_at, down),
+            leave(1, feed_ref, 0, up_at, up.at[:, pl.ds(half_up, half_up)]),
+        ]
+
+    def attention(low):
+        first, second = (query, key) if low else (value, out)
+        return [
+            leave(2, attention_ref, 0, one_at, first),
+            leave(3, attention_ref, one_rows, two_at, second),
+        ]
+
+    for feed_low in range(2):
+        for attention_low in range(2):
+            here = (bit_ref[0] == (1 - feed_low if held else feed_low)) & (
+                bit_ref[1] == (1 - attention_low if held else attention_low)
             )
-            done += room
-            self.at += room
-
-
-def unpack_body(bit_ref, *refs):
-    parts = [Halves(refs[2 * k], refs[2 * k + 1], bit_ref[k]) for k in range(2)]
-    refs = refs[4:]
-    count = len(refs) // 2
-    outs, scratch, sems = refs[:count], refs[count : 2 * count], refs[2 * count]
-    copies = []
-    for out_ref, scratch_ref in zip(outs, scratch):
-        for col in range(0, scratch_ref.shape[1], LANES):
-            while parts[0].at == 2 * parts[0].half:
-                parts.pop(0)
-            parts[0].take(scratch_ref, col, scratch_ref.shape[0])
-        copies.append(pltpu.make_async_copy(scratch_ref, out_ref, sems.at[len(copies)]))
-        copies[-1].start()
-    for copy in copies:
-        copy.wait()
+
+            @pl.when(here)
+            def _(feed_low=feed_low, attention_low=attention_low):
+                for copy in feed(feed_low) + attention(attention_low):
+                    copy.wait()
 
 
 def unpack_small_body(sec_ref, small_ref, attention_gain_ref, feed_gain_ref, bias_ref):
@@ -988,21 +999,31 @@
         z, sec_late, inputs, series_id, stats_all, series_all, standard_grad, grad_one, other_grad,
         own_out, other_out,
     )
+    last_bits = jnp.stack([place(o[0], section, index) for o in orders]).astype(jnp.int32)
     others = [partner(p, *o[0], count) for p, o in zip(parts, orders)]
-    last_bits = jnp.stack([place(o[0], section, index) for o in orders]).astype(jnp.int32)
-
     vmem = pl.BlockSpec(memory_space=pltpu.VMEM)
-
     large = [shape(width, z.hidden)] * 2 + [shape(z.hidden, width)] + [shape(width, width)] * 4
-    grad_gate, grad_up, grad_down, grad_query, grad_key, grad_value, grad_out = pl.pallas_call(
-        unpack_body,
-        in_specs=[SCALARS] + [vmem] * 4,
-        out_specs=[HBM] * 7,
-        out_shape=large,
-        scratch_shapes=[pltpu.VMEM(s.shape, f32) for s in large] + [pltpu.SemaphoreType.DMA((7,))],
-        compiler_params=pltpu.CompilerParams(vmem_limit_bytes=57 * 2**20),
-        name="unpack",
-    )(last_bits, *(array for pair in zip(parts, others) for array in pair))
+
+    def unpack(held, halves, before):
+        return pl.pallas_call(
+            functools.partial(unpack_body, held, len(before)),
+            in_specs=[SCALARS] + [vmem] * 2 + [HBM] * len(before),
+            out_specs=[HBM] * 7,
+            out_shape=large,
+            input_output_aliases={3 + k: k for k in range(len(before))},
+            scratch_shapes=[
+                pltpu.VMEM((width, z.hidden), f32), pltpu.VMEM((width, z.hidden // 2), f32),
+                pltpu.VMEM((z.hidden, width), f32), pltpu.VMEM((width, width), f32),
+                pltpu.VMEM((width, width), f32), pltpu.SemaphoreType.DMA((4,)),
+            ],
+            compiler_params=pltpu.CompilerParams(vmem_limit_bytes=57 * 2**20),
+            cost_estimate=pl.CostEstimate(flops=5 * 10**9, bytes_accessed=2**22, transcendentals=0),
+            name="unpack",
+        )(last_bits, *halves, *before)
+
+    grad_gate, grad_up, grad_down, grad_query, grad_key, grad_value, grad_out = unpack(
+        False, others, unpack(True, parts, ())
+    )
     grad_attention_gain, grad_feed_gain, grad_bias = pl.pallas_call(
         unpack_small_body,
         in_specs=[SCALARS, vmem],

time: 258 us -> 254 us (0.984)
  waiting for transfers between devices: 67.2 us -> 64.3 us
  local copies, waits for them, and re-layouts: 6.76 us -> 3.91 us
    ppermute x22, waiting for transfers between devices: 60.8 us -> 57.5 us  [partner(): return lax.ppermute(x, ('section', 'dp'), pairs)]
    unnamed x66 -> x58, local copies, waits for them, and re-layouts: 4.64 us -> 1.83 us
    pallas_call x1 -> x2, Pallas kernels: 5.14 us -> 6.83 us  [unpack(): pl.pallas_call(functools.partial(unpack_body, held, len(before)), in_spec...]
  transfers between devices with their start and end apart: 36 -> 36, of which waited for: 21 -> 22; matrix products, arithmetic and copies ran while one was open for 5% -> 6% of each run, Pallas kernels for 5% -> 6%
where the time goes in v2:
time: 254 us; the launch traced here: 253 us
  Pallas kernels  135 us (53%)
  waiting for transfers between devices  64.3 us (25%)
  starting transfers between devices  32.6 us (13%)
  other arithmetic  15.6 us (6%)
  local copies, waits for them, and re-layouts  3.91 us (2%)
    pallas_call x1, Pallas kernels, layers(): call(layers_body, z.own, [z.row_batch, z.row_batch, z.all_rows, z.all_row...  114 us
    ppermute x22, waiting for transfers between devices, partner(): return lax.ppermute(x, ('section', 'dp'), pairs)  57.5 us
    ppermute x22, starting transfers between devices, partner(): return lax.ppermute(x, ('section', 'dp'), pairs)  30 us
    pallas_call x1, Pallas kernels, final(): call(final_body, z.micro, [z.row, z.all_rows, by_step(z.stats), by_step(z...  10.1 us
    pallas_call x2, Pallas kernels, unpack(): pl.pallas_call(functools.partial(unpack_body, held, len(before)), in_spec...  6.83 us
    ppermute x14, waiting for transfers between devices, swapped(): return lax.ppermute(x, 'section', [(0, 1), (1, 0)])  6.78 us
  transfers between devices with their start and end apart: 36, of which 22 were waited for; matrix products, arithmetic and copies ran while one was open for 6% of the time, Pallas kernels for 6%

profile of v2, /device:TPU:0, one launch (start us, length us, event | category | flops | bytes accessed | tf_op | source)
XLA Modules:
  0.0 253.1 jit_solution(2523615372576763789)
XLA Ops:
  0.7 3.4 %series_stats.1 = f32[3,8,128]{2,1,0:T(8,128)} custom-call(s32[1]{0:T(128)} %bitcast.sec_ref, bf16[6,512,384]{2,1,0:T(8,128)(2,1)} %x_ref.5, s32[6,512]{1,0:T(8,128)} %sid_ref.5), custom_call_target="tpu_custom_call" | custom-call | flops 10000000 | bytes 4194304 | tf_op jit(solution)/shard_map/series_stats/pallas_call | solution.py:834
  4.1 2.9 %collective-permute-start = (f32[3,8,128]{2,1,0:T(8,128)}, f32[3,8,128]{2,1,0:T(8,128)S(1)}, u32[]{:S(2)}, u32[]{:S(2)}) collective-permute-start(f32[3,8,128]{2,1,0:T(8,128)} %series_stats.1), channel_id=1, source_target_pairs={{0,1},{1,0},{2,3},{3,2},{4,5},{5,4},{6,7},{7,6},{8,9},{9,8},{10,11... | collective-permute-start | bytes 36872 | tf_op jit(solution)/shard_map/ppermute | solution.py:725
  9.9 2.1 collective-permute-start.1
  13.7 2.1 collective-permute-start.2
  21.1 3.1 %collective-permute-start.11 = (f32[3,8,128]{2,1,0:T(8,128)S(1)}, f32[3,8,128]{2,1,0:T(8,128)S(1)}, u32[]{:S(2)}, u32[]{:S(2)}) collective-permute-start(f32[3,8,128]{2,1,0:T(8,128)S(1)} %select_select_fusion.1), channel_id=1, source_target_pairs={{0,8},{1,9},{2,10},{3,11},{4,12},{5,13},{6,14},{7,15},{8,0},{9,1},... | collective-permute-start | bytes 36872 | tf_op jit(solution)/shard_map/ppermute | solution.py:725
  26.6 113.5 %layers.1 = (bf16[2,3,512,384]{3,2,1,0:T(8,128)(2,1)}, bf16[3,512,384]{2,1,0:T(8,128)(2,1)}, f32[3,512,384]{2,1,0:T(8,128)}, f32[3,8,128]{2,1,0:T(8,128)}, f32[4...) custom-call(s32[1]{0:T(128)} %bitcast.sec_ref, ...), custom_call_target="tpu_custom_call" | custom-call | flops 65229815808 | bytes 4194304 | tf_op jit(solution)/shard_map/layers/pallas_call | solution.py:853
  140.7 2.5 %collective-permute-done.13 = bf16[4608,128]{1,0:T(8,128)(2,1)S(1)} collective-permute-done((bf16[4608,128]{1,0:T(8,128)(2,1)}, bf16[4608,128]{1,0:T(8,128)(2,1)S(1)}, u32[]{:S(2)}, u32[]{:S(2)}) %collective-permute-start.13) | collective-permute-done | bytes 1179680 | tf_op jit(solution)/shard_map/ppermute | solution.py:703
  147.6 2.0 collective-permute-start.15
  152.4 11.4 %collective-permute-done.15 = bf16[2304,128]{1,0:T(8,128)(2,1)S(1)} collective-permute-done((bf16[2304,128]{1,0:T(8,128)(2,1)}, bf16[2304,128]{1,0:T(8,128)(2,1)S(1)}, u32[]{:S(2)}, u32[]{:S(2)}) %collective-permute-start.15) | collective-permute-done | bytes 589856 | tf_op jit(solution)/shard_map/ppermute | solution.py:725
  164.0 1.9 collective-permute-done.14
  167.5 2.7 %collective-permute-start.17 = (bf16[1152,128]{1,0:T(8,128)(2,1)S(1)}, bf16[1152,128]{1,0:T(8,128)(2,1)S(1)}, u32[]{:S(2)}, u32[]{:S(2)}) collective-permute-start(bf16[1152,128]{1,0:T(8,128)(2,1)S(1)} %get-tuple-element.105), channel_id=1, source_target_pairs={{0,8},{1,9},{2,10},{3,11},{4,12},{5,13},{6,14},{7,15},{8,0},{9,1},... | collective-permute-start | bytes 884744 | tf_op jit(solution)/shard_map/ppermute | solution.py:725
  172.0 7.7 %collective-permute-done.18 = f32[72,128]{1,0:T(8,128)S(1)} collective-permute-done((f32[72,128]{1,0:T(8,128)}, f32[72,128]{1,0:T(8,128)S(1)}, u32[]{:S(2)}, u32[]{:S(2)}) %collective-permute-start.18) | collective-permute-done | bytes 36896 | tf_op jit(solution)/shard_map/ppermute | solution.py:725
  180.9 1.7 collective-permute-start.20
  182.6 2.0 collective-permute-start.21
  184.6 8.2 %collective-permute-done.21 = f32[72,128]{1,0:T(8,128)S(1)} collective-permute-done((f32[72,128]{1,0:T(8,128)S(1)}, f32[72,128]{1,0:T(8,128)S(1)}, u32[]{:S(2)}, u32[]{:S(2)}) %collective-permute-start.21) | collective-permute-done | bytes 36896 | tf_op jit(solution)/shard_map/ppermute | solution.py:725
  195.0 3.5 %collective-permute-done.24 = f32[72,128]{1,0:T(8,128)S(1)} collective-permute-done((f32[72,128]{1,0:T(8,128)S(1)}, f32[72,128]{1,0:T(8,128)S(1)}, u32[]{:S(2)}, u32[]{:S(2)}) %collective-permute-start.24) | collective-permute-done | bytes 36896 | tf_op jit(solution)/shard_map/ppermute | solution.py:725
  198.6 10.8 %collective-permute-done.22 = bf16[1152,128]{1,0:T(8,128)(2,1)S(1)} collective-permute-done((bf16[1152,128]{1,0:T(8,128)(2,1)S(1)}, bf16[1152,128]{1,0:T(8,128)(2,1)S(1)}, u32[]{:S(2)}, u32[]{:S(2)}) %collective-permute-start.22) | collective-permute-done | bytes 294944 | tf_op jit(solution)/shard_map/ppermute | solution.py:725
  209.6 2.0 collective-permute-start.27
  212.4 2.8 %collective-permute-done.27 = f32[72,128]{1,0:T(8,128)S(1)} collective-permute-done((f32[72,128]{1,0:T(8,128)S(1)}, f32[72,128]{1,0:T(8,128)S(1)}, u32[]{:S(2)}, u32[]{:S(2)}) %collective-permute-start.27) | collective-permute-done | bytes 36896 | tf_op jit(solution)/shard_map/ppermute | solution.py:725
  215.2 3.8 %collective-permute-done.25 = bf16[1152,128]{1,0:T(8,128)(2,1)S(1)} collective-permute-done((bf16[1152,128]{1,0:T(8,128)(2,1)S(1)}, bf16[1152,128]{1,0:T(8,128)(2,1)S(1)}, u32[]{:S(2)}, u32[]{:S(2)}) %collective-permute-start.25) | collective-permute-done | bytes 294944 | tf_op jit(solution)/shard_map/ppermute | solution.py:725
  232.1 2.0 collective-permute-start.35
  234.1 3.5 %unpack.2 = (f32[384,1024]{1,0:T(8,128)}, f32[384,1024]{1,0:T(8,128)}, f32[1024,384]{1,0:T(8,128)}, f32[384,384]{1,0:T(8,128)}, f32[384,384]{1,0:T(8,128)}, /*index=5*/f32[384,384]{1,0:T(8,128)}, f32[384,384]{1,0:T(8,128)}) custom-call(s32[2]{0:T(128)} %pad_add_fusion.bit_ref, bf16[4608,128]{1,0:T(8,128)(2,1)} %copy-done.4, bf16[2304,128]{1,0:T(8,128)(2,1)} %copy-done.5), custom_call_target="tpu_custom_call" | custom-call | flops 5000000000 | bytes 4194304 | tf_op jit(solution)/shard_map/unpack/pallas_call | solution.py:1008
  237.7 10.1 %final.1 = (f32[6,512,384]{2,1,0:T(8,128)}, bf16[6,512,384]{2,1,0:T(8,128)(2,1)}) custom-call(s32[1]{0:T(128)} %bitcast.sec_ref, bf16[6,512,384]{2,1,0:T(8,128)(2,1)} %x_ref.5, s32[6,512]{1,0:T(8,128)} %sid_ref.5, f32[6,8,128]{2,1,0:T(8,128)} %maximum_select_fusion.stats_ref, f32[6,8,128]{2,1,0:T(8,128)} %maximum_select_fusion.1.series_ref, ...), custom_call_target="tpu_custom_call" | custom-call | flops 10000000000 | bytes 4194304 | tf_op jit(solution)/shard_map/final/pallas_call | solution.py:888
  249.6 3.4 %unpack.3 = (f32[384,1024]{1,0:T(8,128)}, f32[384,1024]{1,0:T(8,128)}, f32[1024,384]{1,0:T(8,128)}, f32[384,384]{1,0:T(8,128)}, f32[384,384]{1,0:T(8,128)}, /*index=5*/f32[384,384]{1,0:T(8,128)}, f32[384,384]{1,0:T(8,128)}) custom-call(s32[2]{0:T(128)} %pad_add_fusion.bit_ref, ...), custom_call_target="tpu_custom_call", output_to_operand_aliasing={{0}: (3, {}), {1}: (4, {}), {2}: (5, {}), {3}: (6, {}), {4}... | custom-call | flops 5000000000 | bytes 4194304 | tf_op jit(solution)/shard_map/unpack/pallas_call | solution.py:1008
  (161 shorter events, 42.8 us)
Async XLA Ops:
  7.0 14.0 %collective-permute-start.7 = (bf16[384,1024]{1,0:T(8,128)(2,1)S(1)}, bf16[384,1024]{1,0:T(8,128)(2,1)S(1)}, u32[]{:S(2)}, u32[]{:S(2)}) collective-permute-start(bf16[384,1024]{1,0:T(8,128)(2,1)S(1)} %bitcast.77), channel_id=1, source_target_pairs={{0,16},{16,0},{1,17},{17,1},{2,18},{18,2},{3,19},{19,3},{4,20},{20... | collective-permute-start | bytes 2359304 | tf_op jit(solution)/shard_map/ppermute | solution.py:703
  7.0 14.0 %collective-permute-start.8 = (bf16[384,1024]{1,0:T(8,128)(2,1)S(1)}, bf16[384,1024]{1,0:T(8,128)(2,1)}, u32[]{:S(2)}, u32[]{:S(2)}) collective-permute-start(bf16[384,1024]{1,0:T(8,128)(2,1)S(1)} %bitcast.79), channel_id=1, source_target_pairs={{0,16},{16,0},{1,17},{17,1},{2,18},{18,2},{3,19},{19,3},{4,20},{20... | collective-permute-start | bytes 2359304 | tf_op jit(solution)/shard_map/ppermute | solution.py:703
  7.6 13.5 %collective-permute-start.9 = (bf16[1024,384]{1,0:T(8,128)(2,1)S(1)}, bf16[1024,384]{1,0:T(8,128)(2,1)}, u32[]{:S(2)}, u32[]{:S(2)}) collective-permute-start(bf16[1024,384]{1,0:T(8,128)(2,1)S(1)} %bitcast.81), channel_id=1, source_target_pairs={{0,16},{16,0},{1,17},{17,1},{2,18},{18,2},{3,19},{19,3},{4,20},{20... | collective-permute-start | bytes 2359304 | tf_op jit(solution)/shard_map/ppermute | solution.py:703
  140.2 6.4 %collective-permute-start.12 = (bf16[9216,128]{1,0:T(8,128)(2,1)}, bf16[9216,128]{1,0:T(8,128)(2,1)S(1)}, u32[]{:S(2)}, u32[]{:S(2)}) collective-permute-start(bf16[9216,128]{1,0:T(8,128)(2,1)} %get-tuple-element.93), channel_id=1, source_target_pairs={{0,16},{16,0},{1,17},{17,1},{2,18},{18,2},{3,19},{19,3},{4,20},{20... | collective-permute-start | bytes 7077896 | tf_op jit(solution)/shard_map/ppermute | solution.py:703
  147.6 16.2 %collective-permute-start.15 = (bf16[2304,128]{1,0:T(8,128)(2,1)}, bf16[2304,128]{1,0:T(8,128)(2,1)S(1)}, u32[]{:S(2)}, u32[]{:S(2)}) collective-permute-start(bf16[2304,128]{1,0:T(8,128)(2,1)} %get-tuple-element.99), channel_id=1, source_target_pairs={{0,4},{1,5},{2,6},{3,7},{4,0},{5,1},{6,2},{7,3},{8,12},{9,13},{10,... | collective-permute-start | bytes 1769480 | tf_op jit(solution)/shard_map/ppermute | solution.py:725
  149.5 16.3 %collective-permute-start.14 = (bf16[4608,128]{1,0:T(8,128)(2,1)S(1)}, bf16[4608,128]{1,0:T(8,128)(2,1)}, u32[]{:S(2)}, u32[]{:S(2)}) collective-permute-start(bf16[4608,128]{1,0:T(8,128)(2,1)S(1)} %get-tuple-element.97), channel_id=1, source_target_pairs={{0,1},{1,0},{2,3},{3,2},{4,5},{5,4},{6,7},{7,6},{8,9},{9,8},{10,11... | collective-permute-start | bytes 3538952 | tf_op jit(solution)/shard_map/ppermute | solution.py:725
  167.5 13.0 %collective-permute-start.17 = (bf16[1152,128]{1,0:T(8,128)(2,1)S(1)}, bf16[1152,128]{1,0:T(8,128)(2,1)S(1)}, u32[]{:S(2)}, u32[]{:S(2)}) collective-permute-start(bf16[1152,128]{1,0:T(8,128)(2,1)S(1)} %get-tuple-element.105), channel_id=1, source_target_pairs={{0,8},{1,9},{2,10},{3,11},{4,12},{5,13},{6,14},{7,15},{8,0},{9,1},... | collective-permute-start | bytes 884744 | tf_op jit(solution)/shard_map/ppermute | solution.py:725
  170.2 9.5 %collective-permute-start.18 = (f32[72,128]{1,0:T(8,128)}, f32[72,128]{1,0:T(8,128)S(1)}, u32[]{:S(2)}, u32[]{:S(2)}) collective-permute-start(f32[72,128]{1,0:T(8,128)} %pad_maximum_fusion.4), channel_id=1, source_target_pairs={{0,8},{1,9},{2,10},{3,11},{4,12},{5,13},{6,14},{7,15},{8,0},{9,1},... | collective-permute-start | bytes 110600 | tf_op jit(solution)/shard_map/ppermute | solution.py:725
  170.5 10.1 %collective-permute-start.16 = (bf16[2304,128]{1,0:T(8,128)(2,1)S(1)}, bf16[2304,128]{1,0:T(8,128)(2,1)S(1)}, u32[]{:S(2)}, u32[]{:S(2)}) collective-permute-start(bf16[2304,128]{1,0:T(8,128)(2,1)S(1)} %get-tuple-element.103), channel_id=1, source_target_pairs={{0,2},{1,3},{2,0},{3,1},{4,6},{5,7},{6,4},{7,5},{8,10},{9,11},{10,... | collective-permute-start | bytes 1769480 | tf_op jit(solution)/shard_map/ppermute | solution.py:725
  180.9 11.9 %collective-permute-start.20 = (bf16[576,128]{1,0:T(8,128)(2,1)S(1)}, bf16[576,128]{1,0:T(8,128)(2,1)S(1)}, u32[]{:S(2)}, u32[]{:S(2)}) collective-permute-start(bf16[576,128]{1,0:T(8,128)(2,1)S(1)} %get-tuple-element.110), channel_id=1, source_target_pairs={{0,1},{1,0},{2,3},{3,2},{4,5},{5,4},{6,7},{7,6},{8,9},{9,8},{10,11... | collective-permute-start | bytes 442376 | tf_op jit(solution)/shard_map/ppermute | solution.py:725
  182.6 10.2 %collective-permute-start.19 = (bf16[1152,128]{1,0:T(8,128)(2,1)S(1)}, bf16[1152,128]{1,0:T(8,128)(2,1)S(1)}, u32[]{:S(2)}, u32[]{:S(2)}) collective-permute-start(bf16[1152,128]{1,0:T(8,128)(2,1)S(1)} %get-tuple-element.108), channel_id=1, source_target_pairs={{0,4},{1,5},{2,6},{3,7},{4,0},{5,1},{6,2},{7,3},{8,12},{9,13},{10,... | collective-permute-start | bytes 884744 | tf_op jit(solution)/shard_map/ppermute | solution.py:725
  182.6 10.2 %collective-permute-start.21 = (f32[72,128]{1,0:T(8,128)S(1)}, f32[72,128]{1,0:T(8,128)S(1)}, u32[]{:S(2)}, u32[]{:S(2)}) collective-permute-start(f32[72,128]{1,0:T(8,128)S(1)} %add.196), channel_id=1, source_target_pairs={{0,4},{1,5},{2,6},{3,7},{4,0},{5,1},{6,2},{7,3},{8,12},{9,13},{10,... | collective-permute-start | bytes 110600 | tf_op jit(solution)/shard_map/ppermute | solution.py:725
  192.9 5.6 %collective-permute-start.23 = (bf16[576,128]{1,0:T(8,128)(2,1)S(1)}, bf16[576,128]{1,0:T(8,128)(2,1)S(1)}, u32[]{:S(2)}, u32[]{:S(2)}) collective-permute-start(bf16[576,128]{1,0:T(8,128)(2,1)S(1)} %add_convert_fusion.9), channel_id=1, source_target_pairs={{0,2},{1,3},{2,0},{3,1},{4,6},{5,7},{6,4},{7,5},{8,10},{9,11},{10,... | collective-permute-start | bytes 442376 | tf_op jit(solution)/shard_map/ppermute | solution.py:725
  194.3 15.1 %collective-permute-start.22 = (bf16[1152,128]{1,0:T(8,128)(2,1)S(1)}, bf16[1152,128]{1,0:T(8,128)(2,1)S(1)}, u32[]{:S(2)}, u32[]{:S(2)}) collective-permute-start(bf16[1152,128]{1,0:T(8,128)(2,1)S(1)} %add_convert_fusion.6), channel_id=1, source_target_pairs={{0,8},{1,9},{2,10},{3,11},{4,12},{5,13},{6,14},{7,15},{8,0},{9,1},... | collective-permute-start | bytes 884744 | tf_op jit(solution)/shard_map/ppermute | solution.py:725
  209.5 5.6 %collective-permute-start.26 = (bf16[576,128]{1,0:T(8,128)(2,1)S(1)}, bf16[576,128]{1,0:T(8,128)(2,1)S(1)}, u32[]{:S(2)}, u32[]{:S(2)}) collective-permute-start(bf16[576,128]{1,0:T(8,128)(2,1)S(1)} %add_convert_fusion.8), channel_id=1, source_target_pairs={{0,1},{1,0},{2,3},{3,2},{4,5},{5,4},{6,7},{7,6},{8,9},{9,8},{10,11... | collective-permute-start | bytes 442376 | tf_op jit(solution)/shard_map/ppermute | solution.py:725
  209.6 5.5 %collective-permute-start.27 = (f32[72,128]{1,0:T(8,128)S(1)}, f32[72,128]{1,0:T(8,128)S(1)}, u32[]{:S(2)}, u32[]{:S(2)}) collective-permute-start(f32[72,128]{1,0:T(8,128)S(1)} %add.202), channel_id=1, source_target_pairs={{0,1},{1,0},{2,3},{3,2},{4,5},{5,4},{6,7},{7,6},{8,9},{9,8},{10,11... | collective-permute-start | bytes 110600 | tf_op jit(solution)/shard_map/ppermute | solution.py:725
  212.2 6.7 %collective-permute-start.25 = (bf16[1152,128]{1,0:T(8,128)(2,1)S(1)}, bf16[1152,128]{1,0:T(8,128)(2,1)S(1)}, u32[]{:S(2)}, u32[]{:S(2)}) collective-permute-start(bf16[1152,128]{1,0:T(8,128)(2,1)S(1)} %add_convert_fusion.5), channel_id=1, source_target_pairs={{0,4},{1,5},{2,6},{3,7},{4,0},{5,1},{6,2},{7,3},{8,12},{9,13},{10,... | collective-permute-start | bytes 884744 | tf_op jit(solution)/shard_map/ppermute | solution.py:725
  219.1 6.4 %collective-permute-start.31 = (f32[72,128]{1,0:T(8,128)S(1)}, f32[72,128]{1,0:T(8,128)}, u32[]{:S(2)}, u32[]{:S(2)}) collective-permute-start(f32[72,128]{1,0:T(8,128)S(1)} %add.203), channel_id=1, source_target_pairs={{0,16},{16,0},{1,17},{17,1},{2,18},{18,2},{3,19},{19,3},{4,20},{20... | collective-permute-start | bytes 110600 | tf_op jit(solution)/shard_map/ppermute | solution.py:703
  219.2 10.8 %collective-permute-start.29 = (bf16[1152,128]{1,0:T(8,128)(2,1)S(1)}, bf16[1152,128]{1,0:T(8,128)(2,1)S(1)}, u32[]{:S(2)}, u32[]{:S(2)}) collective-permute-start(bf16[1152,128]{1,0:T(8,128)(2,1)S(1)} %pad_maximum_fusion.3), channel_id=1, source_target_pairs={{0,8},{1,9},{2,10},{3,11},{4,12},{5,13},{6,14},{7,15},{8,0},{9,1},... | collective-permute-start | bytes 884744 | tf_op jit(solution)/shard_map/ppermute | solution.py:725
  220.7 10.0 %collective-permute-start.28 = (bf16[2304,128]{1,0:T(8,128)(2,1)S(1)}, bf16[2304,128]{1,0:T(8,128)(2,1)}, u32[]{:S(2)}, u32[]{:S(2)}) collective-permute-start(bf16[2304,128]{1,0:T(8,128)(2,1)S(1)} %pad_maximum_fusion.1), channel_id=1, source_target_pairs={{0,2},{1,3},{2,0},{3,1},{4,6},{5,7},{6,4},{7,5},{8,10},{9,11},{10,... | collective-permute-start | bytes 1769480 | tf_op jit(solution)/shard_map/ppermute | solution.py:725
  222.0 15.6 %collective-permute-start.32 = (bf16[3,512,384]{2,1,0:T(8,128)(2,1)}, bf16[3,512,384]{2,1,0:T(8,128)(2,1)}, u32[]{:S(2)}, u32[]{:S(2)}) collective-permute-start(bf16[3,512,384]{2,1,0:T(8,128)(2,1)} %convert_select_fusion), channel_id=1, source_target_pairs={{0,16},{16,0},{1,17},{17,1},{2,18},{18,2},{3,19},{19,3},{4,20},{20... | collective-permute-start | bytes 3538952 | tf_op jit(solution)/shard_map/ppermute | solution.py:703
  224.5 13.1 %collective-permute-start.33 = (bf16[3,512,384]{2,1,0:T(8,128)(2,1)S(1)}, bf16[3,512,384]{2,1,0:T(8,128)(2,1)}, u32[]{:S(2)}, u32[]{:S(2)}) collective-permute-start(bf16[3,512,384]{2,1,0:T(8,128)(2,1)S(1)} %get-tuple-element.162), channel_id=1, source_target_pairs={{0,16},{16,0},{1,17},{17,1},{2,18},{18,2},{3,19},{19,3},{4,20},{20... | collective-permute-start | bytes 3538952 | tf_op jit(solution)/shard_map/ppermute | solution.py:703
  232.0 16.4 %collective-permute-start.34 = (bf16[4608,128]{1,0:T(8,128)(2,1)S(1)}, bf16[4608,128]{1,0:T(8,128)(2,1)S(1)}, u32[]{:S(2)}, u32[]{:S(2)}) collective-permute-start(bf16[4608,128]{1,0:T(8,128)(2,1)S(1)} %pad_maximum_fusion.feed_ref), channel_id=1, source_target_pairs={{0,1},{1,0},{2,3},{3,2},{4,5},{5,4},{6,7},{7,6},{8,9},{9,8},{10,11... | collective-permute-start | bytes 3538952 | tf_op jit(solution)/shard_map/ppermute | solution.py:725
  232.1 16.2 %collective-permute-start.35 = (bf16[2304,128]{1,0:T(8,128)(2,1)S(1)}, bf16[2304,128]{1,0:T(8,128)(2,1)S(1)}, u32[]{:S(2)}, u32[]{:S(2)}) collective-permute-start(bf16[2304,128]{1,0:T(8,128)(2,1)S(1)} %pad_maximum_fusion.2.attention_ref), channel_id=1, source_target_pairs={{0,4},{1,5},{2,6},{3,7},{4,0},{5,1},{6,2},{7,3},{8,12},{9,13},{10,... | collective-permute-start | bytes 1769480 | tf_op jit(solution)/shard_map/ppermute | solution.py:725
  (35 other events, 166.8 us)

commit v3 on v2

--- a/solution.py
+++ b/solution.py
@@ -968,6 +968,8 @@
         if k < rounds - 1:
             parts, small = halve(parts, orders, k, section, index, count, small)
         else:
+            parts, stats = lax.optimization_barrier((parts, stats))
+            parts, other_stats = lax.optimization_barrier((parts, swapped(stats)))
             parts, small = add_whole(parts, orders, k, count, small)
         small = small + partner(small, bits[rounds - k], bits[rounds - k], count)
     for k in reversed(range(1, rounds - 1)):
@@ -975,15 +977,14 @@
             parts, small = lax.optimization_barrier((parts, small))
             small = small + partner(small, bits[0], bits[0], count)
         if k == 1:
-            parts, small, results, grad_one, standard_grad, stats = lax.optimization_barrier(
-                (parts, small, results, grad_one, standard_grad, stats)
+            parts, small, results, grad_one, standard_grad = lax.optimization_barrier(
+                (parts, small, results, grad_one, standard_grad)
             )
             result_one, result_two = results[0], results[1]
             own_out = jnp.where(on_first, result_one, result_two)
             other_out = swapped(jnp.where(on_first, result_two, result_one))
             other_grad = swapped(jnp.where(on_first, grad_one, standard_grad.astype(bf16)))
             other_sums = swapped(small)
-            other_stats = swapped(stats)
         parts = double(parts, orders, k, section, index, count)
     mine = small[:series_rows].reshape((z.own,) + z.stats)
     theirs = other_sums[:series_rows].reshape((z.own,) + z.stats)

time: 254 us -> 252 us (level)
  no operation moved by 1% of the time
where the time goes in v3:
time: 252 us; the launch traced here: 251 us
  Pallas kernels  135 us (54%)
  waiting for transfers between devices  62.8 us (25%)
  starting transfers between devices  31.6 us (13%)
  other arithmetic  15.9 us (6%)
  local copies, waits for them, and re-layouts  4.4 us (2%)
    pallas_call x1, Pallas kernels, layers(): call(layers_body, z.own, [z.row_batch, z.row_batch, z.all_rows, z.all_row...  114 us
    ppermute x22, waiting for transfers between devices, partner(): return lax.ppermute(x, ('section', 'dp'), pairs)  55.5 us
    ppermute x22, starting transfers between devices, partner(): return lax.ppermute(x, ('section', 'dp'), pairs)  29.8 us
    pallas_call x1, Pallas kernels, final(): call(final_body, z.micro, [z.row, z.all_rows, by_step(z.stats), by_step(z...  10.1 us
    ppermute x14, waiting for transfers between devices, swapped(): return lax.ppermute(x, 'section', [(0, 1), (1, 0)])  7.3 us
    pallas_call x2, Pallas kernels, unpack(): pl.pallas_call(functools.partial(unpack_body, held, len(before)), in_spec...  6.83 us
  transfers between devices with their start and end apart: 36, of which 22 were waited for; matrix products, arithmetic and copies ran while one was open for 6% of the time, Pallas kernels for 6%

profile of v3, /device:TPU:0, one launch (start us, length us, event | category | flops | bytes accessed | tf_op | source)
XLA Modules:
  0.0 251.3 jit_solution(12329275660511209393)
XLA Ops:
  0.7 3.4 %series_stats.1 = f32[3,8,128]{2,1,0:T(8,128)} custom-call(s32[1]{0:T(128)} %bitcast.sec_ref, bf16[6,512,384]{2,1,0:T(8,128)(2,1)} %x_ref.5, s32[6,512]{1,0:T(8,128)} %sid_ref.5), custom_call_target="tpu_custom_call" | custom-call | flops 10000000 | bytes 4194304 | tf_op jit(solution)/shard_map/series_stats/pallas_call | solution.py:834
  4.1 2.9 %collective-permute-start = (f32[3,8,128]{2,1,0:T(8,128)}, f32[3,8,128]{2,1,0:T(8,128)S(1)}, u32[]{:S(2)}, u32[]{:S(2)}) collective-permute-start(f32[3,8,128]{2,1,0:T(8,128)} %series_stats.1), channel_id=1, source_target_pairs={{0,1},{1,0},{2,3},{3,2},{4,5},{5,4},{6,7},{7,6},{8,9},{9,8},{10,11... | collective-permute-start | bytes 36872 | tf_op jit(solution)/shard_map/ppermute | solution.py:725
  9.9 2.1 collective-permute-start.1
  13.7 2.1 collective-permute-start.2
  21.1 3.1 %collective-permute-start.11 = (f32[3,8,128]{2,1,0:T(8,128)S(1)}, f32[3,8,128]{2,1,0:T(8,128)S(1)}, u32[]{:S(2)}, u32[]{:S(2)}) collective-permute-start(f32[3,8,128]{2,1,0:T(8,128)S(1)} %select_select_fusion.1), channel_id=1, source_target_pairs={{0,8},{1,9},{2,10},{3,11},{4,12},{5,13},{6,14},{7,15},{8,0},{9,1},... | collective-permute-start | bytes 36872 | tf_op jit(solution)/shard_map/ppermute | solution.py:725
  26.6 113.5 %layers.1 = (bf16[2,3,512,384]{3,2,1,0:T(8,128)(2,1)}, bf16[3,512,384]{2,1,0:T(8,128)(2,1)}, f32[3,512,384]{2,1,0:T(8,128)}, f32[3,8,128]{2,1,0:T(8,128)}, f32[4...) custom-call(s32[1]{0:T(128)} %bitcast.sec_ref, ...), custom_call_target="tpu_custom_call" | custom-call | flops 65229815808 | bytes 4194304 | tf_op jit(solution)/shard_map/layers/pallas_call | solution.py:853
  140.7 2.5 %collective-permute-done.13 = bf16[4608,128]{1,0:T(8,128)(2,1)S(1)} collective-permute-done((bf16[4608,128]{1,0:T(8,128)(2,1)}, bf16[4608,128]{1,0:T(8,128)(2,1)S(1)}, u32[]{:S(2)}, u32[]{:S(2)}) %collective-permute-start.13) | collective-permute-done | bytes 1179680 | tf_op jit(solution)/shard_map/ppermute | solution.py:703
  147.6 2.0 collective-permute-start.15
  152.4 11.4 %collective-permute-done.15 = bf16[2304,128]{1,0:T(8,128)(2,1)S(1)} collective-permute-done((bf16[2304,128]{1,0:T(8,128)(2,1)}, bf16[2304,128]{1,0:T(8,128)(2,1)S(1)}, u32[]{:S(2)}, u32[]{:S(2)}) %collective-permute-start.15) | collective-permute-done | bytes 589856 | tf_op jit(solution)/shard_map/ppermute | solution.py:725
  164.0 1.9 collective-permute-done.14
  167.5 2.7 %collective-permute-start.17 = (bf16[1152,128]{1,0:T(8,128)(2,1)S(1)}, bf16[1152,128]{1,0:T(8,128)(2,1)S(1)}, u32[]{:S(2)}, u32[]{:S(2)}) collective-permute-start(bf16[1152,128]{1,0:T(8,128)(2,1)S(1)} %get-tuple-element.110), channel_id=1, source_target_pairs={{0,8},{1,9},{2,10},{3,11},{4,12},{5,13},{6,14},{7,15},{8,0},{9,1},... | collective-permute-start | bytes 884744 | tf_op jit(solution)/shard_map/ppermute | solution.py:725
  172.0 7.7 %collective-permute-done.18 = f32[72,128]{1,0:T(8,128)S(1)} collective-permute-done((f32[72,128]{1,0:T(8,128)}, f32[72,128]{1,0:T(8,128)S(1)}, u32[]{:S(2)}, u32[]{:S(2)}) %collective-permute-start.18) | collective-permute-done | bytes 36896 | tf_op jit(solution)/shard_map/ppermute | solution.py:725
  180.9 1.7 collective-permute-start.20
  182.6 2.0 collective-permute-start.22
  186.2 6.2 %collective-permute-done.19 = bf16[1152,128]{1,0:T(8,128)(2,1)S(1)} collective-permute-done((bf16[1152,128]{1,0:T(8,128)(2,1)S(1)}, bf16[1152,128]{1,0:T(8,128)(2,1)S(1)}, u32[]{:S(2)}, u32[]{:S(2)}) %collective-permute-start.19) | collective-permute-done | bytes 294944 | tf_op jit(solution)/shard_map/ppermute | solution.py:725
  195.8 3.5 %collective-permute-done.25 = f32[72,128]{1,0:T(8,128)S(1)} collective-permute-done((f32[72,128]{1,0:T(8,128)S(1)}, f32[72,128]{1,0:T(8,128)S(1)}, u32[]{:S(2)}, u32[]{:S(2)}) %collective-permute-start.25) | collective-permute-done | bytes 36896 | tf_op jit(solution)/shard_map/ppermute | solution.py:725
  199.3 6.0 %collective-permute-done.23 = bf16[1152,128]{1,0:T(8,128)(2,1)S(1)} collective-permute-done((bf16[1152,128]{1,0:T(8,128)(2,1)S(1)}, bf16[1152,128]{1,0:T(8,128)(2,1)S(1)}, u32[]{:S(2)}, u32[]{:S(2)}) %collective-permute-start.23) | collective-permute-done | bytes 294944 | tf_op jit(solution)/shard_map/ppermute | solution.py:725
  208.8 2.3 collective-permute-done.28
  211.1 6.7 %collective-permute-done.26 = bf16[1152,128]{1,0:T(8,128)(2,1)S(1)} collective-permute-done((bf16[1152,128]{1,0:T(8,128)(2,1)S(1)}, bf16[1152,128]{1,0:T(8,128)(2,1)S(1)}, u32[]{:S(2)}, u32[]{:S(2)}) %collective-permute-start.26) | collective-permute-done | bytes 294944 | tf_op jit(solution)/shard_map/ppermute | solution.py:725
  226.5 2.1 collective-permute-done.30
  230.8 2.0 collective-permute-start.35
  232.9 3.5 %unpack.2 = (f32[384,1024]{1,0:T(8,128)}, f32[384,1024]{1,0:T(8,128)}, f32[1024,384]{1,0:T(8,128)}, f32[384,384]{1,0:T(8,128)}, f32[384,384]{1,0:T(8,128)}, /*index=5*/f32[384,384]{1,0:T(8,128)}, f32[384,384]{1,0:T(8,128)}) custom-call(s32[2]{0:T(128)} %pad_add_fusion.bit_ref, bf16[4608,128]{1,0:T(8,128)(2,1)} %copy-done.4, bf16[2304,128]{1,0:T(8,128)(2,1)} %copy-done.5), custom_call_target="tpu_custom_call" | custom-call | flops 5000000000 | bytes 4194304 | tf_op jit(solution)/shard_map/unpack/pallas_call | solution.py:1009
  236.4 10.1 %final.1 = (f32[6,512,384]{2,1,0:T(8,128)}, bf16[6,512,384]{2,1,0:T(8,128)(2,1)}) custom-call(s32[1]{0:T(128)} %bitcast.sec_ref, bf16[6,512,384]{2,1,0:T(8,128)(2,1)} %x_ref.5, s32[6,512]{1,0:T(8,128)} %sid_ref.5, f32[6,8,128]{2,1,0:T(8,128)} %maximum_select_fusion.stats_ref, f32[6,8,128]{2,1,0:T(8,128)} %maximum_select_fusion.1.series_ref, ...), custom_call_target="tpu_custom_call" | custom-call | flops 10000000000 | bytes 4194304 | tf_op jit(solution)/shard_map/final/pallas_call | solution.py:888
  247.8 3.4 %unpack.3 = (f32[384,1024]{1,0:T(8,128)}, f32[384,1024]{1,0:T(8,128)}, f32[1024,384]{1,0:T(8,128)}, f32[384,384]{1,0:T(8,128)}, f32[384,384]{1,0:T(8,128)}, /*index=5*/f32[384,384]{1,0:T(8,128)}, f32[384,384]{1,0:T(8,128)}) custom-call(s32[2]{0:T(128)} %pad_add_fusion.bit_ref, ...), custom_call_target="tpu_custom_call", output_to_operand_aliasing={{0}: (3, {}), {1}: (4, {}), {2}: (5, {}), {3}: (6, {}), {4}... | custom-call | flops 5000000000 | bytes 4194304 | tf_op jit(solution)/shard_map/unpack/pallas_call | solution.py:1009
  (161 shorter events, 45.2 us)
Async XLA Ops:
  4.1 4.8 %collective-permute-start = (f32[3,8,128]{2,1,0:T(8,128)}, f32[3,8,128]{2,1,0:T(8,128)S(1)}, u32[]{:S(2)}, u32[]{:S(2)}) collective-permute-start(f32[3,8,128]{2,1,0:T(8,128)} %series_stats.1), channel_id=1, source_target_pairs={{0,1},{1,0},{2,3},{3,2},{4,5},{5,4},{6,7},{7,6},{8,9},{9,8},{10,11... | collective-permute-start | bytes 36872 | tf_op jit(solution)/shard_map/ppermute | solution.py:725
  7.0 14.0 %collective-permute-start.7 = (bf16[384,1024]{1,0:T(8,128)(2,1)S(1)}, bf16[384,1024]{1,0:T(8,128)(2,1)S(1)}, u32[]{:S(2)}, u32[]{:S(2)}) collective-permute-start(bf16[384,1024]{1,0:T(8,128)(2,1)S(1)} %bitcast.77), channel_id=1, source_target_pairs={{0,16},{16,0},{1,17},{17,1},{2,18},{18,2},{3,19},{19,3},{4,20},{20... | collective-permute-start | bytes 2359304 | tf_op jit(solution)/shard_map/ppermute | solution.py:703
  7.0 14.0 %collective-permute-start.8 = (bf16[384,1024]{1,0:T(8,128)(2,1)S(1)}, bf16[384,1024]{1,0:T(8,128)(2,1)}, u32[]{:S(2)}, u32[]{:S(2)}) collective-permute-start(bf16[384,1024]{1,0:T(8,128)(2,1)S(1)} %bitcast.79), channel_id=1, source_target_pairs={{0,16},{16,0},{1,17},{17,1},{2,18},{18,2},{3,19},{19,3},{4,20},{20... | collective-permute-start | bytes 2359304 | tf_op jit(solution)/shard_map/ppermute | solution.py:703
  7.6 13.5 %collective-permute-start.9 = (bf16[1024,384]{1,0:T(8,128)(2,1)S(1)}, bf16[1024,384]{1,0:T(8,128)(2,1)}, u32[]{:S(2)}, u32[]{:S(2)}) collective-permute-start(bf16[1024,384]{1,0:T(8,128)(2,1)S(1)} %bitcast.81), channel_id=1, source_target_pairs={{0,16},{16,0},{1,17},{17,1},{2,18},{18,2},{3,19},{19,3},{4,20},{20... | collective-permute-start | bytes 2359304 | tf_op jit(solution)/shard_map/ppermute | solution.py:703
  21.1 4.8 %collective-permute-start.11 = (f32[3,8,128]{2,1,0:T(8,128)S(1)}, f32[3,8,128]{2,1,0:T(8,128)S(1)}, u32[]{:S(2)}, u32[]{:S(2)}) collective-permute-start(f32[3,8,128]{2,1,0:T(8,128)S(1)} %select_select_fusion.1), channel_id=1, source_target_pairs={{0,8},{1,9},{2,10},{3,11},{4,12},{5,13},{6,14},{7,15},{8,0},{9,1},... | collective-permute-start | bytes 36872 | tf_op jit(solution)/shard_map/ppermute | solution.py:725
  140.2 6.4 %collective-permute-start.12 = (bf16[9216,128]{1,0:T(8,128)(2,1)}, bf16[9216,128]{1,0:T(8,128)(2,1)S(1)}, u32[]{:S(2)}, u32[]{:S(2)}) collective-permute-start(bf16[9216,128]{1,0:T(8,128)(2,1)} %get-tuple-element.98), channel_id=1, source_target_pairs={{0,16},{16,0},{1,17},{17,1},{2,18},{18,2},{3,19},{19,3},{4,20},{20... | collective-permute-start | bytes 7077896 | tf_op jit(solution)/shard_map/ppermute | solution.py:703
  147.6 16.2 %collective-permute-start.15 = (bf16[2304,128]{1,0:T(8,128)(2,1)}, bf16[2304,128]{1,0:T(8,128)(2,1)S(1)}, u32[]{:S(2)}, u32[]{:S(2)}) collective-permute-start(bf16[2304,128]{1,0:T(8,128)(2,1)} %get-tuple-element.104), channel_id=1, source_target_pairs={{0,4},{1,5},{2,6},{3,7},{4,0},{5,1},{6,2},{7,3},{8,12},{9,13},{10,... | collective-permute-start | bytes 1769480 | tf_op jit(solution)/shard_map/ppermute | solution.py:725
  149.6 16.3 %collective-permute-start.14 = (bf16[4608,128]{1,0:T(8,128)(2,1)S(1)}, bf16[4608,128]{1,0:T(8,128)(2,1)}, u32[]{:S(2)}, u32[]{:S(2)}) collective-permute-start(bf16[4608,128]{1,0:T(8,128)(2,1)S(1)} %get-tuple-element.102), channel_id=1, source_target_pairs={{0,1},{1,0},{2,3},{3,2},{4,5},{5,4},{6,7},{7,6},{8,9},{9,8},{10,11... | collective-permute-start | bytes 3538952 | tf_op jit(solution)/shard_map/ppermute | solution.py:725
  167.5 13.0 %collective-permute-start.17 = (bf16[1152,128]{1,0:T(8,128)(2,1)S(1)}, bf16[1152,128]{1,0:T(8,128)(2,1)S(1)}, u32[]{:S(2)}, u32[]{:S(2)}) collective-permute-start(bf16[1152,128]{1,0:T(8,128)(2,1)S(1)} %get-tuple-element.110), channel_id=1, source_target_pairs={{0,8},{1,9},{2,10},{3,11},{4,12},{5,13},{6,14},{7,15},{8,0},{9,1},... | collective-permute-start | bytes 884744 | tf_op jit(solution)/shard_map/ppermute | solution.py:725
  170.2 9.6 %collective-permute-start.18 = (f32[72,128]{1,0:T(8,128)}, f32[72,128]{1,0:T(8,128)S(1)}, u32[]{:S(2)}, u32[]{:S(2)}) collective-permute-start(f32[72,128]{1,0:T(8,128)} %pad_maximum_fusion.4), channel_id=1, source_target_pairs={{0,8},{1,9},{2,10},{3,11},{4,12},{5,13},{6,14},{7,15},{8,0},{9,1},... | collective-permute-start | bytes 110600 | tf_op jit(solution)/shard_map/ppermute | solution.py:725
  170.5 10.1 %collective-permute-start.16 = (bf16[2304,128]{1,0:T(8,128)(2,1)S(1)}, bf16[2304,128]{1,0:T(8,128)(2,1)S(1)}, u32[]{:S(2)}, u32[]{:S(2)}) collective-permute-start(bf16[2304,128]{1,0:T(8,128)(2,1)S(1)} %get-tuple-element.108), channel_id=1, source_target_pairs={{0,2},{1,3},{2,0},{3,1},{4,6},{5,7},{6,4},{7,5},{8,10},{9,11},{10,... | collective-permute-start | bytes 1769480 | tf_op jit(solution)/shard_map/ppermute | solution.py:725
  180.9 5.2 %collective-permute-start.20 = (bf16[576,128]{1,0:T(8,128)(2,1)S(1)}, bf16[576,128]{1,0:T(8,128)(2,1)S(1)}, u32[]{:S(2)}, u32[]{:S(2)}) collective-permute-start(bf16[576,128]{1,0:T(8,128)(2,1)S(1)} %get-tuple-element.115), channel_id=1, source_target_pairs={{0,1},{1,0},{2,3},{3,2},{4,5},{5,4},{6,7},{7,6},{8,9},{9,8},{10,11... | collective-permute-start | bytes 442376 | tf_op jit(solution)/shard_map/ppermute | solution.py:725
  182.6 9.8 %collective-permute-start.19 = (bf16[1152,128]{1,0:T(8,128)(2,1)S(1)}, bf16[1152,128]{1,0:T(8,128)(2,1)S(1)}, u32[]{:S(2)}, u32[]{:S(2)}) collective-permute-start(bf16[1152,128]{1,0:T(8,128)(2,1)S(1)} %get-tuple-element.113), channel_id=1, source_target_pairs={{0,4},{1,5},{2,6},{3,7},{4,0},{5,1},{6,2},{7,3},{8,12},{9,13},{10,... | collective-permute-start | bytes 884744 | tf_op jit(solution)/shard_map/ppermute | solution.py:725
  182.6 10.2 %collective-permute-start.22 = (f32[72,128]{1,0:T(8,128)S(1)}, f32[72,128]{1,0:T(8,128)S(1)}, u32[]{:S(2)}, u32[]{:S(2)}) collective-permute-start(f32[72,128]{1,0:T(8,128)S(1)} %add.196), channel_id=1, source_target_pairs={{0,4},{1,5},{2,6},{3,7},{4,0},{5,1},{6,2},{7,3},{8,12},{9,13},{10,... | collective-permute-start | bytes 110600 | tf_op jit(solution)/shard_map/ppermute | solution.py:725
  193.7 5.5 %collective-permute-start.24 = (bf16[576,128]{1,0:T(8,128)(2,1)S(1)}, bf16[576,128]{1,0:T(8,128)(2,1)S(1)}, u32[]{:S(2)}, u32[]{:S(2)}) collective-permute-start(bf16[576,128]{1,0:T(8,128)(2,1)S(1)} %add_convert_fusion.9), channel_id=1, source_target_pairs={{0,2},{1,3},{2,0},{3,1},{4,6},{5,7},{6,4},{7,5},{8,10},{9,11},{10,... | collective-permute-start | bytes 442376 | tf_op jit(solution)/shard_map/ppermute | solution.py:725
  195.0 10.3 %collective-permute-start.23 = (bf16[1152,128]{1,0:T(8,128)(2,1)S(1)}, bf16[1152,128]{1,0:T(8,128)(2,1)S(1)}, u32[]{:S(2)}, u32[]{:S(2)}) collective-permute-start(bf16[1152,128]{1,0:T(8,128)(2,1)S(1)} %add_convert_fusion.6), channel_id=1, source_target_pairs={{0,8},{1,9},{2,10},{3,11},{4,12},{5,13},{6,14},{7,15},{8,0},{9,1},... | collective-permute-start | bytes 884744 | tf_op jit(solution)/shard_map/ppermute | solution.py:725
  205.4 5.6 %collective-permute-start.27 = (bf16[576,128]{1,0:T(8,128)(2,1)S(1)}, bf16[576,128]{1,0:T(8,128)(2,1)S(1)}, u32[]{:S(2)}, u32[]{:S(2)}) collective-permute-start(bf16[576,128]{1,0:T(8,128)(2,1)S(1)} %add_convert_fusion.8), channel_id=1, source_target_pairs={{0,1},{1,0},{2,3},{3,2},{4,5},{5,4},{6,7},{7,6},{8,9},{9,8},{10,11... | collective-permute-start | bytes 442376 | tf_op jit(solution)/shard_map/ppermute | solution.py:725
  208.8 9.1 %collective-permute-start.26 = (bf16[1152,128]{1,0:T(8,128)(2,1)S(1)}, bf16[1152,128]{1,0:T(8,128)(2,1)S(1)}, u32[]{:S(2)}, u32[]{:S(2)}) collective-permute-start(bf16[1152,128]{1,0:T(8,128)(2,1)S(1)} %add_convert_fusion.5), channel_id=1, source_target_pairs={{0,4},{1,5},{2,6},{3,7},{4,0},{5,1},{6,2},{7,3},{8,12},{9,13},{10,... | collective-permute-start | bytes 884744 | tf_op jit(solution)/shard_map/ppermute | solution.py:725
  218.0 10.6 %collective-permute-start.30 = (bf16[1152,128]{1,0:T(8,128)(2,1)S(1)}, bf16[1152,128]{1,0:T(8,128)(2,1)S(1)}, u32[]{:S(2)}, u32[]{:S(2)}) collective-permute-start(bf16[1152,128]{1,0:T(8,128)(2,1)S(1)} %pad_maximum_fusion.3), channel_id=1, source_target_pairs={{0,8},{1,9},{2,10},{3,11},{4,12},{5,13},{6,14},{7,15},{8,0},{9,1},... | collective-permute-start | bytes 884744 | tf_op jit(solution)/shard_map/ppermute | solution.py:725
  218.5 10.2 %collective-permute-start.29 = (bf16[2304,128]{1,0:T(8,128)(2,1)S(1)}, bf16[2304,128]{1,0:T(8,128)(2,1)}, u32[]{:S(2)}, u32[]{:S(2)}) collective-permute-start(bf16[2304,128]{1,0:T(8,128)(2,1)S(1)} %pad_maximum_fusion.1), channel_id=1, source_target_pairs={{0,2},{1,3},{2,0},{3,1},{4,6},{5,7},{6,4},{7,5},{8,10},{9,11},{10,... | collective-permute-start | bytes 1769480 | tf_op jit(solution)/shard_map/ppermute | solution.py:725
  220.4 16.0 %collective-permute-start.32 = (bf16[3,512,384]{2,1,0:T(8,128)(2,1)}, bf16[3,512,384]{2,1,0:T(8,128)(2,1)}, u32[]{:S(2)}, u32[]{:S(2)}) collective-permute-start(bf16[3,512,384]{2,1,0:T(8,128)(2,1)} %convert_select_fusion), channel_id=1, source_target_pairs={{0,16},{16,0},{1,17},{17,1},{2,18},{18,2},{3,19},{19,3},{4,20},{20... | collective-permute-start | bytes 3538952 | tf_op jit(solution)/shard_map/ppermute | solution.py:703
  222.5 13.9 %collective-permute-start.33 = (bf16[3,512,384]{2,1,0:T(8,128)(2,1)S(1)}, bf16[3,512,384]{2,1,0:T(8,128)(2,1)}, u32[]{:S(2)}, u32[]{:S(2)}) collective-permute-start(bf16[3,512,384]{2,1,0:T(8,128)(2,1)S(1)} %get-tuple-element.172), channel_id=1, source_target_pairs={{0,16},{16,0},{1,17},{17,1},{2,18},{18,2},{3,19},{19,3},{4,20},{20... | collective-permute-start | bytes 3538952 | tf_op jit(solution)/shard_map/ppermute | solution.py:703
  230.2 16.4 %collective-permute-start.34 = (bf16[4608,128]{1,0:T(8,128)(2,1)S(1)}, bf16[4608,128]{1,0:T(8,128)(2,1)S(1)}, u32[]{:S(2)}, u32[]{:S(2)}) collective-permute-start(bf16[4608,128]{1,0:T(8,128)(2,1)S(1)} %pad_maximum_fusion.feed_ref), channel_id=1, source_target_pairs={{0,1},{1,0},{2,3},{3,2},{4,5},{5,4},{6,7},{7,6},{8,9},{9,8},{10,11... | collective-permute-start | bytes 3538952 | tf_op jit(solution)/shard_map/ppermute | solution.py:725
  230.8 15.7 %collective-permute-start.35 = (bf16[2304,128]{1,0:T(8,128)(2,1)S(1)}, bf16[2304,128]{1,0:T(8,128)(2,1)S(1)}, u32[]{:S(2)}, u32[]{:S(2)}) collective-permute-start(bf16[2304,128]{1,0:T(8,128)(2,1)S(1)} %pad_maximum_fusion.2.attention_ref), channel_id=1, source_target_pairs={{0,4},{1,5},{2,6},{3,7},{4,0},{5,1},{6,2},{7,3},{8,12},{9,13},{10,... | collective-permute-start | bytes 1769480 | tf_op jit(solution)/shard_map/ppermute | solution.py:725
  (35 other events, 179.0 us)

commit v4 on v3

--- a/solution.py
+++ b/solution.py
@@ -778,7 +778,7 @@
     return pl.BlockSpec((1,) + shape, lambda i, s: (own * s[0] + i,) + (0,) * len(shape))
 
 
-def call(body, grid, in_specs, out_specs, out_shapes, scratch, flops, name):
+def call(body, grid, in_specs, out_specs, out_shapes, scratch, flops, name, vmem=28):
     return pl.pallas_call(
         body,
         grid_spec=pltpu.PrefetchScalarGridSpec(
@@ -789,7 +789,7 @@
             scratch_shapes=scratch,
         ),
         out_shape=out_shapes,
-        compiler_params=pltpu.CompilerParams(vmem_limit_bytes=57 * 2**20),
+        compiler_params=pltpu.CompilerParams(vmem_limit_bytes=vmem * 2**20),
         cost_estimate=pl.CostEstimate(flops=flops, bytes_accessed=2**22, transcendentals=0),
         name=name,
     )
@@ -868,7 +868,7 @@
          pltpu.VMEM((rows, hidden), bf16),
          both(8 * width, LANES, dtype=bf16),
          pltpu.SemaphoreType.DMA((2, 7)), pltpu.SemaphoreType.DMA((2,))],
-        12 * z.flops, "layers",
+        12 * z.flops, "layers", 57,
     )(sec, inputs, cotangent, series_id, item, variate, stats, jnp.asarray(table),
       *small, *own, *other)
 
@@ -1017,7 +1017,7 @@
                 pltpu.VMEM((z.hidden, width), f32), pltpu.VMEM((width, width), f32),
                 pltpu.VMEM((width, width), f32), pltpu.SemaphoreType.DMA((4,)),
             ],
-            compiler_params=pltpu.CompilerParams(vmem_limit_bytes=57 * 2**20),
+            compiler_params=pltpu.CompilerParams(vmem_limit_bytes=24 * 2**20),
             cost_estimate=pl.CostEstimate(flops=5 * 10**9, bytes_accessed=2**22, transcendentals=0),
             name="unpack",
         )(last_bits, *halves, *before)

time: 252 us -> 253 us (level)
  Pallas kernels: 135 us -> 129 us
  waiting for transfers between devices: 62.8 us -> 66.6 us
    ppermute x22, waiting for transfers between devices: 55.5 us -> 59.3 us  [partner(): return lax.ppermute(x, ('section', 'dp'), pairs)]
  transfers between devices with their start and end apart: 36 -> 36, of which waited for: 22 -> 24; matrix products, arithmetic and copies ran while one was open for 6% -> 6% of each run, Pallas kernels for 6% -> 5%
where the time goes in v4:
time: 253 us; the launch traced here: 252 us
  Pallas kernels  129 us (51%)
  waiting for transfers between devices  66.6 us (26%)
  starting transfers between devices  30.7 us (12%)
  other arithmetic  18.4 us (7%)
  local copies, waits for them, and re-layouts  5.66 us (2%)
    pallas_call x1, Pallas kernels, layers(): call(layers_body, z.own, [z.row_batch, z.row_batch, z.all_rows, z.all_row...  114 us
    ppermute x22, waiting for transfers between devices, partner(): return lax.ppermute(x, ('section', 'dp'), pairs)  59.3 us
    ppermute x22, starting transfers between devices, partner(): return lax.ppermute(x, ('section', 'dp'), pairs)  28.9 us
    pallas_call x1, Pallas kernels, final(): call(final_body, z.micro, [z.row, z.all_rows, by_step(z.stats), by_step(z...  7.78 us
    ppermute x14, waiting for transfers between devices, swapped(): return lax.ppermute(x, 'section', [(0, 1), (1, 0)])  7.3 us
  transfers between devices with their start and end apart: 36, of which 24 were waited for; matrix products, arithmetic and copies ran while one was open for 6% of the time, Pallas kernels for 5%

profile of v4, /device:TPU:0, one launch (start us, length us, event | category | flops | bytes accessed | tf_op | source)
XLA Modules:
  0.0 251.7 jit_solution(14576850230824844957)
XLA Ops:
  4.4 3.0 %collective-permute-start = (f32[3,8,128]{2,1,0:T(8,128)S(1)}, f32[3,8,128]{2,1,0:T(8,128)S(1)}, u32[]{:S(2)}, u32[]{:S(2)}) collective-permute-start(f32[3,8,128]{2,1,0:T(8,128)S(1)} %series_stats.1), channel_id=1, source_target_pairs={{0,1},{1,0},{2,3},{3,2},{4,5},{5,4},{6,7},{7,6},{8,9},{9,8},{10,11... | collective-permute-start | bytes 36872 | tf_op jit(solution)/shard_map/ppermute | solution.py:725
  9.2 2.1 collective-permute-start.1
  13.1 2.1 collective-permute-start.2
  20.5 3.1 %collective-permute-start.11 = (f32[3,8,128]{2,1,0:T(8,128)S(1)}, f32[3,8,128]{2,1,0:T(8,128)S(1)}, u32[]{:S(2)}, u32[]{:S(2)}) collective-permute-start(f32[3,8,128]{2,1,0:T(8,128)S(1)} %select_select_fusion.1), channel_id=1, source_target_pairs={{0,8},{1,9},{2,10},{3,11},{4,12},{5,13},{6,14},{7,15},{8,0},{9,1},... | collective-permute-start | bytes 36872 | tf_op jit(solution)/shard_map/ppermute | solution.py:725
  23.6 1.7 collective-permute-done.11
  26.0 113.5 %layers.1 = (bf16[2,3,512,384]{3,2,1,0:T(8,128)(2,1)}, bf16[3,512,384]{2,1,0:T(8,128)(2,1)}, f32[3,512,384]{2,1,0:T(8,128)}, f32[3,8,128]{2,1,0:T(8,128)}, f32[4...) custom-call(s32[1]{0:T(128)} %bitcast.sec_ref, ...), custom_call_target="tpu_custom_call" | custom-call | flops 65229815808 | bytes 4194304 | tf_op jit(solution)/shard_map/layers/pallas_call | solution.py:853
  140.1 2.5 %collective-permute-done.13 = bf16[4608,128]{1,0:T(8,128)(2,1)S(1)} collective-permute-done((bf16[4608,128]{1,0:T(8,128)(2,1)}, bf16[4608,128]{1,0:T(8,128)(2,1)S(1)}, u32[]{:S(2)}, u32[]{:S(2)}) %collective-permute-start.13) | collective-permute-done | bytes 1179680 | tf_op jit(solution)/shard_map/ppermute | solution.py:703
  147.0 2.0 collective-permute-start.15
  151.8 11.3 %collective-permute-done.15 = bf16[2304,128]{1,0:T(8,128)(2,1)S(1)} collective-permute-done((bf16[2304,128]{1,0:T(8,128)(2,1)}, bf16[2304,128]{1,0:T(8,128)(2,1)S(1)}, u32[]{:S(2)}, u32[]{:S(2)}) %collective-permute-start.15) | collective-permute-done | bytes 589856 | tf_op jit(solution)/shard_map/ppermute | solution.py:725
  163.3 1.9 collective-permute-done.14
  166.9 2.7 %collective-permute-start.17 = (bf16[1152,128]{1,0:T(8,128)(2,1)S(1)}, bf16[1152,128]{1,0:T(8,128)(2,1)S(1)}, u32[]{:S(2)}, u32[]{:S(2)}) collective-permute-start(bf16[1152,128]{1,0:T(8,128)(2,1)S(1)} %get-tuple-element.110), channel_id=1, source_target_pairs={{0,8},{1,9},{2,10},{3,11},{4,12},{5,13},{6,14},{7,15},{8,0},{9,1},... | collective-permute-start | bytes 884744 | tf_op jit(solution)/shard_map/ppermute | solution.py:725
  171.4 7.7 %collective-permute-done.18 = f32[72,128]{1,0:T(8,128)S(1)} collective-permute-done((f32[72,128]{1,0:T(8,128)}, f32[72,128]{1,0:T(8,128)S(1)}, u32[]{:S(2)}, u32[]{:S(2)}) %collective-permute-start.18) | collective-permute-done | bytes 36896 | tf_op jit(solution)/shard_map/ppermute | solution.py:725
  180.3 1.7 collective-permute-start.20
  182.0 2.0 collective-permute-start.22
  185.5 6.3 %collective-permute-done.19 = bf16[1152,128]{1,0:T(8,128)(2,1)S(1)} collective-permute-done((bf16[1152,128]{1,0:T(8,128)(2,1)S(1)}, bf16[1152,128]{1,0:T(8,128)(2,1)S(1)}, u32[]{:S(2)}, u32[]{:S(2)}) %collective-permute-start.19) | collective-permute-done | bytes 294944 | tf_op jit(solution)/shard_map/ppermute | solution.py:725
  195.2 3.5 %collective-permute-done.25 = f32[72,128]{1,0:T(8,128)S(1)} collective-permute-done((f32[72,128]{1,0:T(8,128)S(1)}, f32[72,128]{1,0:T(8,128)S(1)}, u32[]{:S(2)}, u32[]{:S(2)}) %collective-permute-start.25) | collective-permute-done | bytes 36896 | tf_op jit(solution)/shard_map/ppermute | solution.py:725
  198.7 6.0 %collective-permute-done.23 = bf16[1152,128]{1,0:T(8,128)(2,1)S(1)} collective-permute-done((bf16[1152,128]{1,0:T(8,128)(2,1)S(1)}, bf16[1152,128]{1,0:T(8,128)(2,1)S(1)}, u32[]{:S(2)}, u32[]{:S(2)}) %collective-permute-start.23) | collective-permute-done | bytes 294944 | tf_op jit(solution)/shard_map/ppermute | solution.py:725
  208.2 2.8 %collective-permute-done.28 = f32[72,128]{1,0:T(8,128)S(1)} collective-permute-done((f32[72,128]{1,0:T(8,128)S(1)}, f32[72,128]{1,0:T(8,128)S(1)}, u32[]{:S(2)}, u32[]{:S(2)}) %collective-permute-start.28) | collective-permute-done | bytes 36896 | tf_op jit(solution)/shard_map/ppermute | solution.py:725
  211.8 5.7 %collective-permute-done.26 = bf16[1152,128]{1,0:T(8,128)(2,1)S(1)} collective-permute-done((bf16[1152,128]{1,0:T(8,128)(2,1)}, bf16[1152,128]{1,0:T(8,128)(2,1)S(1)}, u32[]{:S(2)}, u32[]{:S(2)}) %collective-permute-start.26) | collective-permute-done | bytes 294944 | tf_op jit(solution)/shard_map/ppermute | solution.py:725
  227.7 2.5 collective-permute-done.30
  234.6 2.6 %unpack.2 = (f32[384,1024]{1,0:T(8,128)}, f32[384,1024]{1,0:T(8,128)}, f32[1024,384]{1,0:T(8,128)}, f32[384,384]{1,0:T(8,128)}, f32[384,384]{1,0:T(8,128)}, /*index=5*/f32[384,384]{1,0:T(8,128)}, f32[384,384]{1,0:T(8,128)}) custom-call(s32[2]{0:T(128)S(1)} %pad_add_fusion.bit_ref, bf16[4608,128]{1,0:T(8,128)(2,1)S(1)} %pad_maximum_fusion.feed_ref, ...), custom_call_target="tpu_custom_call" | custom-call | flops 5000000000 | bytes 4194304 | tf_op jit(solution)/shard_map/unpack/pallas_call | solution.py:1009
  237.3 7.8 %final.1 = (f32[6,512,384]{2,1,0:T(8,128)}, bf16[6,512,384]{2,1,0:T(8,128)(2,1)}) custom-call(s32[1]{0:T(128)} %bitcast.sec_ref, bf16[6,512,384]{2,1,0:T(8,128)(2,1)S(1)} %copy-done.1, s32[6,512]{1,0:T(8,128)S(1)} %copy-done.7, f32[6,8,128]{2,1,0:T(8,128)S(1)} %copy-done.5, f32[6,8,128]{2,1,0:T(8,128)S(1)} %maximum_select_fusion.1.series_ref, ...), custom_call_target="tpu_custom_call" | custom-call | flops 10000000000 | bytes 4194304 | tf_op jit(solution)/shard_map/final/pallas_call | solution.py:888
  245.0 3.2 %collective-permute-done.35.attention_ref = bf16[2304,128]{1,0:T(8,128)(2,1)S(1)} collective-permute-done((bf16[2304,128]{1,0:T(8,128)(2,1)S(1)}, bf16[2304,128]{1,0:T(8,128)(2,1)S(1)}, u32[]{:S(2)}, u32[]{:S(2)}) %collective-permute-start.35) | collective-permute-done | bytes 589856 | tf_op jit(solution)/shard_map/ppermute | solution.py:725
  249.1 2.5 unpack.3
  (165 shorter events, 50.3 us)
Async XLA Ops:
  7.4 13.0 %collective-permute-start.7 = (bf16[384,1024]{1,0:T(8,128)(2,1)S(1)}, bf16[384,1024]{1,0:T(8,128)(2,1)S(1)}, u32[]{:S(2)}, u32[]{:S(2)}) collective-permute-start(bf16[384,1024]{1,0:T(8,128)(2,1)S(1)} %bitcast.77), channel_id=1, source_target_pairs={{0,16},{16,0},{1,17},{17,1},{2,18},{18,2},{3,19},{19,3},{4,20},{20... | collective-permute-start | bytes 2359304 | tf_op jit(solution)/shard_map/ppermute | solution.py:703
  7.4 13.0 %collective-permute-start.8 = (bf16[384,1024]{1,0:T(8,128)(2,1)S(1)}, bf16[384,1024]{1,0:T(8,128)(2,1)}, u32[]{:S(2)}, u32[]{:S(2)}) collective-permute-start(bf16[384,1024]{1,0:T(8,128)(2,1)S(1)} %bitcast.79), channel_id=1, source_target_pairs={{0,16},{16,0},{1,17},{17,1},{2,18},{18,2},{3,19},{19,3},{4,20},{20... | collective-permute-start | bytes 2359304 | tf_op jit(solution)/shard_map/ppermute | solution.py:703
  8.0 12.5 %collective-permute-start.9 = (bf16[1024,384]{1,0:T(8,128)(2,1)S(1)}, bf16[1024,384]{1,0:T(8,128)(2,1)}, u32[]{:S(2)}, u32[]{:S(2)}) collective-permute-start(bf16[1024,384]{1,0:T(8,128)(2,1)S(1)} %bitcast.81), channel_id=1, source_target_pairs={{0,16},{16,0},{1,17},{17,1},{2,18},{18,2},{3,19},{19,3},{4,20},{20... | collective-permute-start | bytes 2359304 | tf_op jit(solution)/shard_map/ppermute | solution.py:703
  20.5 4.8 %collective-permute-start.11 = (f32[3,8,128]{2,1,0:T(8,128)S(1)}, f32[3,8,128]{2,1,0:T(8,128)S(1)}, u32[]{:S(2)}, u32[]{:S(2)}) collective-permute-start(f32[3,8,128]{2,1,0:T(8,128)S(1)} %select_select_fusion.1), channel_id=1, source_target_pairs={{0,8},{1,9},{2,10},{3,11},{4,12},{5,13},{6,14},{7,15},{8,0},{9,1},... | collective-permute-start | bytes 36872 | tf_op jit(solution)/shard_map/ppermute | solution.py:725
  139.6 6.4 %collective-permute-start.12 = (bf16[9216,128]{1,0:T(8,128)(2,1)}, bf16[9216,128]{1,0:T(8,128)(2,1)S(1)}, u32[]{:S(2)}, u32[]{:S(2)}) collective-permute-start(bf16[9216,128]{1,0:T(8,128)(2,1)} %get-tuple-element.98), channel_id=1, source_target_pairs={{0,16},{16,0},{1,17},{17,1},{2,18},{18,2},{3,19},{19,3},{4,20},{20... | collective-permute-start | bytes 7077896 | tf_op jit(solution)/shard_map/ppermute | solution.py:703
  147.0 16.2 %collective-permute-start.15 = (bf16[2304,128]{1,0:T(8,128)(2,1)}, bf16[2304,128]{1,0:T(8,128)(2,1)S(1)}, u32[]{:S(2)}, u32[]{:S(2)}) collective-permute-start(bf16[2304,128]{1,0:T(8,128)(2,1)} %get-tuple-element.104), channel_id=1, source_target_pairs={{0,4},{1,5},{2,6},{3,7},{4,0},{5,1},{6,2},{7,3},{8,12},{9,13},{10,... | collective-permute-start | bytes 1769480 | tf_op jit(solution)/shard_map/ppermute | solution.py:725
  148.9 16.3 %collective-permute-start.14 = (bf16[4608,128]{1,0:T(8,128)(2,1)S(1)}, bf16[4608,128]{1,0:T(8,128)(2,1)}, u32[]{:S(2)}, u32[]{:S(2)}) collective-permute-start(bf16[4608,128]{1,0:T(8,128)(2,1)S(1)} %get-tuple-element.102), channel_id=1, source_target_pairs={{0,1},{1,0},{2,3},{3,2},{4,5},{5,4},{6,7},{7,6},{8,9},{9,8},{10,11... | collective-permute-start | bytes 3538952 | tf_op jit(solution)/shard_map/ppermute | solution.py:725
  166.9 13.0 %collective-permute-start.17 = (bf16[1152,128]{1,0:T(8,128)(2,1)S(1)}, bf16[1152,128]{1,0:T(8,128)(2,1)S(1)}, u32[]{:S(2)}, u32[]{:S(2)}) collective-permute-start(bf16[1152,128]{1,0:T(8,128)(2,1)S(1)} %get-tuple-element.110), channel_id=1, source_target_pairs={{0,8},{1,9},{2,10},{3,11},{4,12},{5,13},{6,14},{7,15},{8,0},{9,1},... | collective-permute-start | bytes 884744 | tf_op jit(solution)/shard_map/ppermute | solution.py:725
  169.6 9.5 %collective-permute-start.18 = (f32[72,128]{1,0:T(8,128)}, f32[72,128]{1,0:T(8,128)S(1)}, u32[]{:S(2)}, u32[]{:S(2)}) collective-permute-start(f32[72,128]{1,0:T(8,128)} %pad_maximum_fusion.4), channel_id=1, source_target_pairs={{0,8},{1,9},{2,10},{3,11},{4,12},{5,13},{6,14},{7,15},{8,0},{9,1},... | collective-permute-start | bytes 110600 | tf_op jit(solution)/shard_map/ppermute | solution.py:725
  169.9 10.1 %collective-permute-start.16 = (bf16[2304,128]{1,0:T(8,128)(2,1)S(1)}, bf16[2304,128]{1,0:T(8,128)(2,1)S(1)}, u32[]{:S(2)}, u32[]{:S(2)}) collective-permute-start(bf16[2304,128]{1,0:T(8,128)(2,1)S(1)} %get-tuple-element.108), channel_id=1, source_target_pairs={{0,2},{1,3},{2,0},{3,1},{4,6},{5,7},{6,4},{7,5},{8,10},{9,11},{10,... | collective-permute-start | bytes 1769480 | tf_op jit(solution)/shard_map/ppermute | solution.py:725
  180.3 5.2 %collective-permute-start.20 = (bf16[576,128]{1,0:T(8,128)(2,1)S(1)}, bf16[576,128]{1,0:T(8,128)(2,1)S(1)}, u32[]{:S(2)}, u32[]{:S(2)}) collective-permute-start(bf16[576,128]{1,0:T(8,128)(2,1)S(1)} %get-tuple-element.115), channel_id=1, source_target_pairs={{0,1},{1,0},{2,3},{3,2},{4,5},{5,4},{6,7},{7,6},{8,9},{9,8},{10,11... | collective-permute-start | bytes 442376 | tf_op jit(solution)/shard_map/ppermute | solution.py:725
  182.0 9.8 %collective-permute-start.19 = (bf16[1152,128]{1,0:T(8,128)(2,1)S(1)}, bf16[1152,128]{1,0:T(8,128)(2,1)S(1)}, u32[]{:S(2)}, u32[]{:S(2)}) collective-permute-start(bf16[1152,128]{1,0:T(8,128)(2,1)S(1)} %get-tuple-element.113), channel_id=1, source_target_pairs={{0,4},{1,5},{2,6},{3,7},{4,0},{5,1},{6,2},{7,3},{8,12},{9,13},{10,... | collective-permute-start | bytes 884744 | tf_op jit(solution)/shard_map/ppermute | solution.py:725
  182.0 10.2 %collective-permute-start.22 = (f32[72,128]{1,0:T(8,128)S(1)}, f32[72,128]{1,0:T(8,128)S(1)}, u32[]{:S(2)}, u32[]{:S(2)}) collective-permute-start(f32[72,128]{1,0:T(8,128)S(1)} %add.196), channel_id=1, source_target_pairs={{0,4},{1,5},{2,6},{3,7},{4,0},{5,1},{6,2},{7,3},{8,12},{9,13},{10,... | collective-permute-start | bytes 110600 | tf_op jit(solution)/shard_map/ppermute | solution.py:725
  193.1 5.5 %collective-permute-start.24 = (bf16[576,128]{1,0:T(8,128)(2,1)S(1)}, bf16[576,128]{1,0:T(8,128)(2,1)S(1)}, u32[]{:S(2)}, u32[]{:S(2)}) collective-permute-start(bf16[576,128]{1,0:T(8,128)(2,1)S(1)} %add_convert_fusion.9), channel_id=1, source_target_pairs={{0,2},{1,3},{2,0},{3,1},{4,6},{5,7},{6,4},{7,5},{8,10},{9,11},{10,... | collective-permute-start | bytes 442376 | tf_op jit(solution)/shard_map/ppermute | solution.py:725
  194.4 10.3 %collective-permute-start.23 = (bf16[1152,128]{1,0:T(8,128)(2,1)S(1)}, bf16[1152,128]{1,0:T(8,128)(2,1)S(1)}, u32[]{:S(2)}, u32[]{:S(2)}) collective-permute-start(bf16[1152,128]{1,0:T(8,128)(2,1)S(1)} %add_convert_fusion.6), channel_id=1, source_target_pairs={{0,8},{1,9},{2,10},{3,11},{4,12},{5,13},{6,14},{7,15},{8,0},{9,1},... | collective-permute-start | bytes 884744 | tf_op jit(solution)/shard_map/ppermute | solution.py:725
  205.5 5.5 %collective-permute-start.27 = (bf16[576,128]{1,0:T(8,128)(2,1)S(1)}, bf16[576,128]{1,0:T(8,128)(2,1)S(1)}, u32[]{:S(2)}, u32[]{:S(2)}) collective-permute-start(bf16[576,128]{1,0:T(8,128)(2,1)S(1)} %add_convert_fusion.8), channel_id=1, source_target_pairs={{0,1},{1,0},{2,3},{3,2},{4,5},{5,4},{6,7},{7,6},{8,9},{9,8},{10,11... | collective-permute-start | bytes 442376 | tf_op jit(solution)/shard_map/ppermute | solution.py:725
  208.2 9.3 %collective-permute-start.26 = (bf16[1152,128]{1,0:T(8,128)(2,1)}, bf16[1152,128]{1,0:T(8,128)(2,1)S(1)}, u32[]{:S(2)}, u32[]{:S(2)}) collective-permute-start(bf16[1152,128]{1,0:T(8,128)(2,1)} %add_convert_fusion.5), channel_id=1, source_target_pairs={{0,4},{1,5},{2,6},{3,7},{4,0},{5,1},{6,2},{7,3},{8,12},{9,13},{10,... | collective-permute-start | bytes 884744 | tf_op jit(solution)/shard_map/ppermute | solution.py:725
  219.4 4.9 %collective-permute-start.31 = (f32[72,128]{1,0:T(8,128)S(1)}, f32[72,128]{1,0:T(8,128)}, u32[]{:S(2)}, u32[]{:S(2)}) collective-permute-start(f32[72,128]{1,0:T(8,128)S(1)} %add.203), channel_id=1, source_target_pairs={{0,16},{16,0},{1,17},{17,1},{2,18},{18,2},{3,19},{19,3},{4,20},{20... | collective-permute-start | bytes 110600 | tf_op jit(solution)/shard_map/ppermute | solution.py:703
  219.4 10.8 %collective-permute-start.30 = (bf16[1152,128]{1,0:T(8,128)(2,1)}, bf16[1152,128]{1,0:T(8,128)(2,1)}, u32[]{:S(2)}, u32[]{:S(2)}) collective-permute-start(bf16[1152,128]{1,0:T(8,128)(2,1)} %pad_maximum_fusion.3), channel_id=1, source_target_pairs={{0,8},{1,9},{2,10},{3,11},{4,12},{5,13},{6,14},{7,15},{8,0},{9,1},... | collective-permute-start | bytes 884744 | tf_op jit(solution)/shard_map/ppermute | solution.py:725
  219.9 11.4 %collective-permute-start.29 = (bf16[2304,128]{1,0:T(8,128)(2,1)}, bf16[2304,128]{1,0:T(8,128)(2,1)}, u32[]{:S(2)}, u32[]{:S(2)}) collective-permute-start(bf16[2304,128]{1,0:T(8,128)(2,1)} %pad_maximum_fusion.1), channel_id=1, source_target_pairs={{0,2},{1,3},{2,0},{3,1},{4,6},{5,7},{6,4},{7,5},{8,10},{9,11},{10,... | collective-permute-start | bytes 1769480 | tf_op jit(solution)/shard_map/ppermute | solution.py:725
  221.7 15.5 %collective-permute-start.32 = (bf16[3,512,384]{2,1,0:T(8,128)(2,1)}, bf16[3,512,384]{2,1,0:T(8,128)(2,1)}, u32[]{:S(2)}, u32[]{:S(2)}) collective-permute-start(bf16[3,512,384]{2,1,0:T(8,128)(2,1)} %convert_select_fusion), channel_id=1, source_target_pairs={{0,16},{16,0},{1,17},{17,1},{2,18},{18,2},{3,19},{19,3},{4,20},{20... | collective-permute-start | bytes 3538952 | tf_op jit(solution)/shard_map/ppermute | solution.py:703
  224.3 13.0 %collective-permute-start.33 = (bf16[3,512,384]{2,1,0:T(8,128)(2,1)}, bf16[3,512,384]{2,1,0:T(8,128)(2,1)}, u32[]{:S(2)}, u32[]{:S(2)}) collective-permute-start(bf16[3,512,384]{2,1,0:T(8,128)(2,1)} %get-tuple-element.172), channel_id=1, source_target_pairs={{0,16},{16,0},{1,17},{17,1},{2,18},{18,2},{3,19},{19,3},{4,20},{20... | collective-permute-start | bytes 3538952 | tf_op jit(solution)/shard_map/ppermute | solution.py:703
  232.8 16.3 %collective-permute-start.34 = (bf16[4608,128]{1,0:T(8,128)(2,1)S(1)}, bf16[4608,128]{1,0:T(8,128)(2,1)S(1)}, u32[]{:S(2)}, u32[]{:S(2)}) collective-permute-start(bf16[4608,128]{1,0:T(8,128)(2,1)S(1)} %pad_maximum_fusion.feed_ref), channel_id=1, source_target_pairs={{0,1},{1,0},{2,3},{3,2},{4,5},{5,4},{6,7},{7,6},{8,9},{9,8},{10,11... | collective-permute-start | bytes 3538952 | tf_op jit(solution)/shard_map/ppermute | solution.py:725
  233.5 14.7 %collective-permute-start.35 = (bf16[2304,128]{1,0:T(8,128)(2,1)S(1)}, bf16[2304,128]{1,0:T(8,128)(2,1)S(1)}, u32[]{:S(2)}, u32[]{:S(2)}) collective-permute-start(bf16[2304,128]{1,0:T(8,128)(2,1)S(1)} %pad_maximum_fusion.2.attention_ref), channel_id=1, source_target_pairs={{0,4},{1,5},{2,6},{3,7},{4,0},{5,1},{6,2},{7,3},{8,12},{9,13},{10,... | collective-permute-start | bytes 1769480 | tf_op jit(solution)/shard_map/ppermute | solution.py:725
  (37 other events, 183.3 us)
